TPU v7x, 32 devices: a whole 2x2x4 slice. The times are simulated.
32 devices in a mesh: row: 4 (over z), col: 8 (over y, x, core).
Axes of the slice: x: 2, y: 2, z: 4, core: 2. Of those that a mesh axis runs over, the one named last changes fastest.
Arguments:
- right_side: bfloat16 [16384, 16384], P('row', 'col'), may hold values from -180 to 180
- theta_left: bfloat16 [512, 16384], P(None, 'row'), may hold values from -0.125 to 0.125
- theta_right: bfloat16 [512, 16384], P(None, 'col'), may hold values from -0.125 to 0.125
- query_rows: int32 [1024, 2], replicated, may hold values from 0 to 16384, as said below
- query_cols: int32 [1024, 2], replicated, may hold values from 0 to 16384, as said below
Outputs:
- residual: float32 [16384, 16384], P('row', 'col')
- step_ratio: float32 [1], replicated
- answers: float32 [1024], replicated
Inputs may be any that keep to these rules, and one draw needn't show every extreme that they name: `query_rows`: each row is a start and an end with 0 <= start < end <= 16384. `query_cols`: each row is a start and an end with 0 <= start < end <= 16384.
All inputs are finite; a program needn't handle non-finite values.
Results may differ from a plain program's by a relative error of at most 0.0003.
Values sent between devices are 32-bit elements; how exact they have to be, the bound alone decides.
No kernel may reach another device: no remote copies, remote signals or barrier semaphores. Data moves between devices by JAX's collectives and lax.ppermute only.
A program may use at most 256 MiB of HBM per device.

v0:
```python
import jax
import jax.numpy as jnp
from jax import lax
from jax.sharding import PartitionSpec as P


def prefix_2(part, axis, combine, identity):
    place = lax.axis_index(axis)
    gathered = lax.all_gather(part, axis)
    state = jnp.zeros_like(part) + jnp.asarray(identity, part.dtype)

    def one(hop, state):
        return combine(state, lax.dynamic_index_in_dim(gathered, hop, 0, False))

    return lax.fori_loop(0, place, one, state)


def add_pair(earlier, later):
    return earlier + later


def cum_last(values):
    length = values.shape[1]
    block_len = 128
    index_line = jnp.arange(block_len)
    upper_tri = (index_line[:, None] <= index_line[None, :]).astype(jnp.float32)
    pieces = values.reshape(values.shape[0], length // block_len, block_len)
    within = jnp.einsum("rbk,kj->rbj", pieces, upper_tri, precision=lax.Precision.HIGHEST)
    totals = within[:, :, -1]
    carried = jnp.cumsum(totals, axis=1) - totals
    return (within + carried[:, :, None]).reshape(values.shape)


def cum_first(values):
    length = values.shape[0]
    block_len = 128
    index_line = jnp.arange(block_len)
    lower_tri = (index_line[:, None] >= index_line[None, :]).astype(jnp.float32)
    pieces = values.reshape(length // block_len, block_len, values.shape[1])
    within = jnp.einsum("ik,bkc->bic", lower_tri, pieces, precision=lax.Precision.HIGHEST)
    totals = within[:, -1, :]
    carried = jnp.cumsum(totals, axis=0) - totals
    return (within + carried[:, None, :]).reshape(values.shape)


def down_scan(column_totals):
    return prefix_2(column_totals, "row", add_pair, jnp.zeros_like(column_totals))


def shards(right_side, theta_left, theta_right, query_rows, query_cols):
    highest = lax.Precision.HIGHEST
    block_rows, block_cols = right_side.shape
    start_field = right_side.astype(jnp.float32)
    left_wide = theta_left.astype(jnp.float32)
    right_wide = theta_right.astype(jnp.float32)
    start_norm = lax.psum(jnp.sum(start_field * start_field), ("row", "col"))
    partial_right = lax.dot_general(
        right_side, theta_right, (((1,), (1,)), ((), ())), preferred_element_type=jnp.float32
    )
    summed_right = lax.psum(partial_right, "col")
    middle = start_field + jnp.dot(
        summed_right, right_wide, precision=highest, preferred_element_type=jnp.float32
    )
    partial_left = jnp.dot(left_wide, middle, precision=highest, preferred_element_type=jnp.float32)
    summed_left = lax.psum(partial_left, "row")
    image_field = middle + lax.dot_general(
        left_wide,
        summed_left,
        (((0,), (0,)), ((), ())),
        precision=highest,
        preferred_element_type=jnp.float32,
    )
    curvature = lax.psum(jnp.sum(start_field * image_field), ("row", "col"))
    alpha_step = start_norm / curvature
    residual = start_field - alpha_step * image_field
    fresh = lax.psum(jnp.sum(residual * residual), ("row", "col"))
    step_ratio = (fresh / start_norm).reshape(1)
    solution = alpha_step * start_field
    across = cum_last(solution)
    row_totals = across[:, -1]
    left_carry = prefix_2(row_totals, "col", add_pair, jnp.zeros_like(row_totals))
    vertical = cum_first(across + left_carry[:, None])
    upper_carry = down_scan(vertical[-1, :])
    prefix = vertical + upper_carry[None, :]
    row_start = lax.axis_index("row") * block_rows
    col_start = lax.axis_index("col") * block_cols
    flat_prefix = prefix.reshape(-1)

    def corner_value(row_bound, col_bound):
        local_row = row_bound - 1 - row_start
        local_col = col_bound - 1 - col_start
        inside = (
            (local_row >= 0)
            & (local_row < block_rows)
            & (local_col >= 0)
            & (local_col < block_cols)
        )
        position_flat = jnp.clip(local_row, 0, block_rows - 1) * block_cols + jnp.clip(
            local_col, 0, block_cols - 1
        )
        return jnp.where(inside, jnp.take(flat_prefix, position_flat), 0.0)

    low_row = query_rows[:, 0]
    high_row = query_rows[:, 1]
    low_col = query_cols[:, 0]
    high_col = query_cols[:, 1]
    partial_answers = (
        corner_value(high_row, high_col)
        - corner_value(low_row, high_col)
        - corner_value(high_row, low_col)
        + corner_value(low_row, low_col)
    )
    combined = lax.psum(partial_answers, ("row", "col"))
    area = (high_row - low_row).astype(jnp.float32) * (high_col - low_col).astype(jnp.float32)
    answers = combined / jnp.sqrt(area)
    return (residual, step_ratio, answers)


def solution(mesh):
    return jax.shard_map(
        shards,
        mesh=mesh,
        in_specs=(P("row", "col"), P(None, "row"), P(None, "col"), P(), P()),
        out_specs=(P("row", "col"), P(), P()),
        check_vma=False,
    )
```

profile of v0, /device:TPU:0, one launch (start us, length us, event | category | flops | bytes accessed | tf_op | source)
XLA Modules:
  0.0 1040.4 jit_solution(10291765985156420507)
XLA Ops:
  7.2 0.0 copy-start
  7.2 0.0 all-reduce.5.cloned.1.call-start
  7.2 1.5 copy-done
  8.8 14.5 %fusion.27 = f32[4096,512]{1,0:T(8,128)} fusion(bf16[4096,2048]{1,0:T(8,128)(2,1)} %param.11, bf16[512,2048]{1,0:T(8,128)(2,1)S(1)} %copy-done), kind=kOutput, calls=%fused_computation.72 | convolution fusion | flops 8589934592 | bytes 27262976 | tf_op jit(solution)/shard_map/dot_general | solution.py:57
  23.3 0.0 all-reduce.5.cloned.1.call-update
  23.3 0.0 all-reduce.7.cloned.1.call-start
  23.4 129.4 %all-reduce.5.cloned.1.call-done = f32[4096,512]{1,0:T(8,128)} async-done(((f32[4096,512]{1,0:T(8,128)}), f32[4096,512]{1,0:T(8,128)}) %all-reduce.5.cloned.1.call-update) | async-done | bytes 8388624 | tf_op jit(solution)/shard_map/psum | solution.py:60
  152.7 32.0 %fusion.28 = f32[4096,2048]{1,0:T(8,128)} fusion(f32[4096,512]{1,0:T(8,128)} %all-reduce.5.cloned.1.call-done, bf16[512,2048]{1,0:T(8,128)(2,1)S(1)} %copy-done), kind=kOutput, calls=%fused_computation.73 | convolution fusion | flops 51539607552 | bytes 44040192 | tf_op jit(solution)/shard_map/dot_general | solution.py:61
  184.7 59.3 %fusion.13 = f32[512,2048]{0,1:T(8,128)} fusion(bf16[512,4096]{1,0:T(8,128)(2,1)S(1)} %copy-done.4, f32[4096,2048]{1,0:T(8,128)} %fusion.28, bf16[4096,2048]{1,0:T(8,128)(2,1)} %param.11), kind=kOutput, calls=%fused_computation.27 | convolution fusion | flops 51556384768 | bytes 58720256 | tf_op jit(solution)/shard_map/dot_general | solution.py:64
  244.1 0.0 all-reduce.7.cloned.1.call-update
  244.1 0.7 and_reduce_fusion.3
  244.8 0.0 copy-start.7
  244.8 0.0 copy-start.9
  244.9 0.0 copy-start.11
  244.9 0.0 copy-start.13
  244.9 0.6 fusion.23
  245.5 0.6 fusion.24
  246.1 0.6 fusion.25
  246.7 0.6 fusion.26
  247.3 0.6 multiply_rsqrt_fusion
  247.9 151.5 %all-reduce.7.cloned.1.call-done = f32[512,2048]{0,1:T(8,128)} async-done(((f32[512,2048]{0,1:T(8,128)}), f32[512,2048]{0,1:T(8,128)}) %all-reduce.7.cloned.1.call-update) | async-done | bytes 4194320 | tf_op jit(solution)/shard_map/psum | solution.py:65
  399.4 48.5 %fusion.1 = (f32[]{:T(128)}, f32[]{:T(128)}, f32[2048,4096]{0,1:T(8,128)}) fusion(bf16[4096,2048]{1,0:T(8,128)(2,1)} %param.11, f32[4096,2048]{1,0:T(8,128)} %fusion.28, f32[512,2048]{0,1:T(8,128)} %all-reduce.7.cloned.1.call-done, bf16[512,4096]{1,0:T(8,128)(2,1)} %param.12), kind=kOutput, calls=%fused_computation.12 | convolution fusion | flops 51598327808 | bytes 92274696 | tf_op jit(solution)/shard_map/dot_general | solution.py:66
  447.9 0.0 copy-done.11
  447.9 40.0 %all-reduce.1 = (f32[]{:T(128)}, f32[]{:T(128)}) all-reduce(f32[]{:T(128)} %get-tuple-element.53, f32[]{:T(128)} %get-tuple-element.52), channel_id=1, replica_groups=mesh['row'=4,'col'=8] {'row','col'}, use_global_device_ids=true, to_apply=%region_1.0 | all-reduce | flops 2 | bytes 16 | tf_op jit(solution)/shard_map/psum | solution.py:56
  489.2 48.9 %multiply_reduce_fusion = (f32[]{:T(128)}, f32[4096,2048]{1,0:T(8,128)}, f32[512,16,8,128]{3,2,1,0:T(8,128)}) fusion(f32[2048,4096]{0,1:T(8,128)} %get-tuple-element.85, f32[4096,2048]{1,0:T(8,128)} %fusion.28, f32[]{:T(128)S(6)} %div.9, bf16[4096,2048]{1,0:T(8,128)(2,1)} %param.11), kind=kLoop, calls=%fused_computation.20 | loop fusion | flops 67108864 | bytes 150994944 | tf_op jit(solution)/shard_map/reduce_sum | solution.py:76
  538.1 29.4 %fusion.3 = f32[4096,16,128]{0,2,1:T(8,128)} fusion(f32[512,16,8,128]{3,2,1,0:T(8,128)} %get-tuple-element.80), kind=kOutput, calls=%fused_computation.14 | convolution fusion | flops 12884918272 | bytes 67108864 | tf_op jit(solution)/shard_map/rbk,kj->rbj/dot_general | solution.py:28
  567.5 1.9 slice.40
  569.4 0.2 copy.20
  569.6 0.2 reduce_window_sum.22
  569.8 2.0 copy_subtract_fusion
  571.8 0.2 copy.40
  571.9 14.2 %broadcast_add_fusion.1 = f32[4096,16,128]{0,2,1:T(8,128)S(1)} fusion(f32[4096,16,128]{0,2,1:T(8,128)} %fusion.3, f32[4096,16]{0,1:T(8,128)S(1)} %bitcast.76), kind=kLoop, calls=%fused_computation.26 | loop fusion | flops 8388608 | bytes 67371008 | tf_op jit(solution)/shard_map/add | solution.py:31
  586.1 0.0 copy-start.2
  586.1 11.1 %copy-done.2 = f32[4096,16,128]{0,2,1:T(8,128)} copy-done((f32[4096,16,128]{0,2,1:T(8,128)}, f32[4096,16,128]{0,2,1:T(8,128)S(1)}, u32[]{:S(2)}) %copy-start.2) | copy-done | bytes 33554456
  597.2 10.2 all-gather
  607.4 0.6 broadcast.172
  608.0 0.9 reduce.11
  609.0 27.7 %copy.28 = f32[256,8,32,128]{3,2,1,0:T(8,128)} copy(f32[256,8,32,128]{3,1,2,0:T(8,128)} %bitcast.67) | data formatting | bytes 67108864
  636.7 35.6 %copy.22 = f32[32,128,2048]{2,1,0:T(8,128)} copy(f32[32,128,2048]{1,0,2:T(8,128)} %bitcast.74) | data formatting | bytes 67108864 | tf_op jit(solution)/shard_map/reshape | solution.py:31
  672.3 33.1 %fusion.9 = f32[32,128,2048]{2,1,0:T(8,128)} fusion(f32[32,128,2048]{2,1,0:T(8,128)} %copy.22, f32[32,128]{1,0:T(8,128)S(1)} %bitcast.78), kind=kOutput, calls=%fused_computation.22 | convolution fusion | flops 12893306880 | bytes 67125248 | tf_op jit(solution)/shard_map/ik,bkc->bic/dot_general | solution.py:40
  705.4 2.7 slice_subtract_fusion
  708.1 0.1 copy.39
  708.2 12.7 %broadcast_add_fusion = f32[32,128,2048]{2,1,0:T(8,128)S(1)} fusion(f32[32,128,2048]{2,1,0:T(8,128)} %fusion.9, f32[32,2048]{1,0:T(8,128)S(1)} %bitcast.77), kind=kLoop, calls=%fused_computation.24 | loop fusion | flops 8388608 | bytes 67371008 | tf_op jit(solution)/shard_map/add | solution.py:43
  720.8 11.1 %copy-done.3 = f32[32,128,2048]{2,1,0:T(8,128)} copy-done((f32[32,128,2048]{2,1,0:T(8,128)}, f32[32,128,2048]{2,1,0:T(8,128)S(1)}, u32[]{:S(2)}) %copy-start.3) | copy-done | bytes 33554456
  731.9 13.1 %all-gather.1 = f32[4,1,2048]{2,1,0:T(1,128)S(1)} all-gather(f32[1,1,2048]{2,1,0:T(1,128)S(1)} %slice_bitcast_fusion), channel_id=1, replica_groups=mesh['row'=4,'col'=8] {'row'}, dimensions={0}, use_global_device_ids=true | all-gather | bytes 40960 | tf_op jit(solution)/shard_map/all_gather | solution.py:9
  745.1 0.0 slice-start
  745.1 0.0 slice-start.1
  745.1 0.0 slice-start.2
  745.1 14.5 %broadcast_bitcast_fusion = f32[512,16,8,128]{3,2,1,0:T(8,128)} fusion(f32[2048]{0:T(1024)S(1)} %get-tuple-element.51), kind=kLoop, calls=%fused_computation.23 | loop fusion | bytes 33562624
  759.6 0.0 slice-start.7
  759.6 29.5 %copy.30 = f32[512,16,8,128]{3,1,2,0:T(8,128)} copy(f32[512,16,8,128]{3,2,1,0:T(8,128)} %broadcast_bitcast_fusion) | data formatting | bytes 67108864
  789.1 0.0 slice-done.3
  789.1 0.0 slice-done.4
  789.1 0.0 slice-done.5
  789.2 0.0 slice-done.6
  789.2 13.7 %copy.29 = f32[512,16,8,128]{3,1,2,0:T(8,128)} copy(f32[512,16,8,128]{3,2,1,0:T(8,128)S(1)} %bitcast.71) | data formatting | bytes 67108864
  803.0 0.0 copy-start.1
  803.0 33.4 %add.122 = f32[8388608]{0:T(1024)} add(f32[8388608]{0:T(1024)} %bitcast.73, f32[8388608]{0:T(1024)} %bitcast.72) | non-fusion elementwise | flops 8388608 | bytes 100663296 | tf_op jit(solution)/shard_map/add | solution.py:84
  836.5 43.7 %gather_fusion = f32[1024]{0:T(1024)S(1)} fusion(f32[8388608]{0:T(1024)} %add.122, s32[1024]{0:T(1024)S(1)} %copy-done.19), kind=kCustom, calls=%fused_computation.clone | custom fusion | bytes 12288 | tf_op jit(solution)/shard_map/jit(_take)/gather | solution.py:101
  880.2 36.3 %gather_fusion.1 = f32[1024]{0:T(1024)S(1)} fusion(f32[8388608]{0:T(1024)} %add.122, s32[1024]{0:T(1024)S(1)} %copy-done.18), kind=kCustom, calls=%fused_computation.1.clone | custom fusion | bytes 12288 | tf_op jit(solution)/shard_map/jit(_take)/gather | solution.py:101
  916.5 41.7 %gather_fusion.2 = f32[1024]{0:T(1024)S(1)} fusion(f32[8388608]{0:T(1024)} %add.122, s32[1024]{0:T(1024)S(1)} %copy-done.16), kind=kCustom, calls=%fused_computation.2.clone | custom fusion | bytes 12288 | tf_op jit(solution)/shard_map/jit(_take)/gather | solution.py:101
  958.2 34.7 %gather_fusion.3 = f32[1024]{0:T(1024)S(1)} fusion(f32[8388608]{0:T(1024)} %add.122, s32[1024]{0:T(1024)S(1)} %copy-done.17), kind=kCustom, calls=%fused_computation.3.clone | custom fusion | bytes 12288 | tf_op jit(solution)/shard_map/jit(_take)/gather | solution.py:101
  993.0 37.2 %all-reduce = (f32[]{:T(128)}, f32[1024]{0:T(1024)S(1)}) all-reduce(f32[]{:T(128)} %get-tuple-element.78, f32[1024]{0:T(1024)S(1)} %fusion.20), channel_id=1, replica_groups=mesh['row'=4,'col'=8] {'row','col'}, use_global_device_ids=true, to_apply=%region_7.0 | all-reduce | flops 1025 | bytes 8200 | tf_op jit(solution)/shard_map/psum | solution.py:76
  1031.6 0.6 div.11
  (56 shorter events, 0.2 us)
Async XLA Ops:
  7.2 1.6 copy-start
  7.2 145.6 %all-reduce.5.cloned.1.call-start = ((), (), s32[]{:S(2)}) async-start(), calls=%async_computation | async-start | bytes 16777216 | tf_op jit(solution)/shard_map/psum | solution.py:60
  23.3 376.1 %all-reduce.7.cloned.1.call-start = ((), (), s32[]{:S(2)}) async-start(), calls=%async_computation.1 | async-start | bytes 8388608 | tf_op jit(solution)/shard_map/psum | solution.py:65
  152.7 32.0 %copy-start.4 = (bf16[512,4096]{1,0:T(8,128)(2,1)S(1)}, bf16[512,4096]{1,0:T(8,128)(2,1)}, u32[]{:S(2)}) copy-start(bf16[512,4096]{1,0:T(8,128)(2,1)} %param.12) | copy-start | bytes 12582916
  184.7 59.3 %copy-start.5 = (s32[1024,2]{0,1:T(2,128)S(1)}, s32[1024,2]{0,1:T(2,128)}, u32[]{:S(2)}) copy-start(s32[1024,2]{0,1:T(2,128)} %param.14) | copy-start | bytes 24580
  184.7 59.4 %copy-start.6 = (s32[1024,2]{0,1:T(2,128)S(1)}, s32[1024,2]{0,1:T(2,128)}, u32[]{:S(2)}) copy-start(s32[1024,2]{0,1:T(2,128)} %param.15) | copy-start | bytes 24580
  244.8 203.0 %copy-start.7 = (s32[1024,1]{0,1:T(1,128)}, s32[1024,1]{0,1:T(1,128)S(1)}, u32[]{:S(2)}) copy-start(s32[1024,1]{0,1:T(1,128)S(1)} %get-tuple-element.81) | copy-start | bytes 12292
  244.8 203.0 %copy-start.9 = (s32[1024,1]{0,1:T(1,128)}, s32[1024,1]{0,1:T(1,128)S(1)}, u32[]{:S(2)}) copy-start(s32[1024,1]{0,1:T(1,128)S(1)} %get-tuple-element.82) | copy-start | bytes 12292
  244.9 203.0 %copy-start.11 = (s32[1024,1]{0,1:T(1,128)}, s32[1024,1]{0,1:T(1,128)S(1)}, u32[]{:S(2)}) copy-start(s32[1024,1]{0,1:T(1,128)S(1)} %get-tuple-element.83) | copy-start | bytes 12292
  244.9 203.0 %copy-start.13 = (s32[1024,1]{0,1:T(1,128)}, s32[1024,1]{0,1:T(1,128)S(1)}, u32[]{:S(2)}) copy-start(s32[1024,1]{0,1:T(1,128)S(1)} %get-tuple-element.84) | copy-start | bytes 12292
  586.1 11.1 %copy-start.2 = (f32[4096,16,128]{0,2,1:T(8,128)}, f32[4096,16,128]{0,2,1:T(8,128)S(1)}, u32[]{:S(2)}) copy-start(f32[4096,16,128]{0,2,1:T(8,128)S(1)} %broadcast_add_fusion.1) | copy-start | bytes 100663296
  720.8 11.1 %copy-start.3 = (f32[32,128,2048]{2,1,0:T(8,128)}, f32[32,128,2048]{2,1,0:T(8,128)S(1)}, u32[]{:S(2)}) copy-start(f32[32,128,2048]{2,1,0:T(8,128)S(1)} %broadcast_add_fusion) | copy-start | bytes 100663296
  745.1 44.0 %slice-start = ((s8[33554432]{0:T(1024)(128)(4,1)}), s8[4194304]{0:T(1024)(128)(4,1)S(1)}, s32[]{:S(2)}) async-start(s8[33554432]{0:T(1024)(128)(4,1)} %bitcast.69), calls=%async_computation.2 | async-start | bytes 8388608
  745.1 44.0 %slice-start.1 = ((s8[33554432]{0:T(1024)(128)(4,1)}), s8[4194304]{0:T(1024)(128)(4,1)S(1)}, s32[]{:S(2)}) async-start(s8[33554432]{0:T(1024)(128)(4,1)} %bitcast.69), calls=%async_computation.3 | async-start | bytes 8388608
  745.1 44.0 %slice-start.2 = ((s8[33554432]{0:T(1024)(128)(4,1)}), s8[4194304]{0:T(1024)(128)(4,1)S(1)}, s32[]{:S(2)}) async-start(s8[33554432]{0:T(1024)(128)(4,1)} %bitcast.69), calls=%async_computation.4 | async-start | bytes 8388608
  759.6 29.5 %slice-start.3 = ((s8[33554432]{0:T(1024)(128)(4,1)}), s8[4194304]{0:T(1024)(128)(4,1)S(1)}, s32[]{:S(2)}) async-start(s8[33554432]{0:T(1024)(128)(4,1)} %bitcast.69), calls=%async_computation.5 | async-start | bytes 8388608
  759.6 29.5 %slice-start.4 = ((s8[33554432]{0:T(1024)(128)(4,1)}), s8[4194304]{0:T(1024)(128)(4,1)S(1)}, s32[]{:S(2)}) async-start(s8[33554432]{0:T(1024)(128)(4,1)} %bitcast.69), calls=%async_computation.6 | async-start | bytes 8388608
  759.6 29.5 %slice-start.5 = ((s8[33554432]{0:T(1024)(128)(4,1)}), s8[4194304]{0:T(1024)(128)(4,1)S(1)}, s32[]{:S(2)}) async-start(s8[33554432]{0:T(1024)(128)(4,1)} %bitcast.69), calls=%async_computation.7 | async-start | bytes 8388608
  759.6 29.5 %slice-start.6 = ((s8[33554432]{0:T(1024)(128)(4,1)}), s8[4194304]{0:T(1024)(128)(4,1)S(1)}, s32[]{:S(2)}) async-start(s8[33554432]{0:T(1024)(128)(4,1)} %bitcast.69), calls=%async_computation.8 | async-start | bytes 8388608
  759.6 29.5 %slice-start.7 = ((s8[33554432]{0:T(1024)(128)(4,1)}), s8[4194304]{0:T(1024)(128)(4,1)S(1)}, s32[]{:S(2)}) async-start(s8[33554432]{0:T(1024)(128)(4,1)} %bitcast.69), calls=%async_computation.9 | async-start | bytes 8388608
  802.9 33.6 %copy-start.19 = (s32[1024]{0:T(1024)S(1)}, s32[1024]{0:T(1024)}, u32[]{:S(2)}) copy-start(s32[1024]{0:T(1024)} %fusion.23) | copy-start | bytes 12292
  802.9 77.3 %copy-start.18 = (s32[1024]{0:T(1024)S(1)}, s32[1024]{0:T(1024)}, u32[]{:S(2)}) copy-start(s32[1024]{0:T(1024)} %fusion.24) | copy-start | bytes 12292
  802.9 113.6 %copy-start.16 = (s32[1024]{0:T(1024)S(1)}, s32[1024]{0:T(1024)}, u32[]{:S(2)}) copy-start(s32[1024]{0:T(1024)} %fusion.25) | copy-start | bytes 12292
  802.9 155.3 %copy-start.17 = (s32[1024]{0:T(1024)S(1)}, s32[1024]{0:T(1024)}, u32[]{:S(2)}) copy-start(s32[1024]{0:T(1024)} %fusion.26) | copy-start | bytes 12292
  802.9 190.0 %copy-start.8 = (s32[1024,1]{0,1:T(1,128)S(1)}, s32[1024,1]{0,1:T(1,128)}, u32[]{:S(2)}) copy-start(s32[1024,1]{0,1:T(1,128)} %copy-done.7) | copy-start | bytes 12292
  802.9 190.0 %copy-start.10 = (s32[1024,1]{0,1:T(1,128)S(1)}, s32[1024,1]{0,1:T(1,128)}, u32[]{:S(2)}) copy-start(s32[1024,1]{0,1:T(1,128)} %copy-done.9) | copy-start | bytes 12292
  802.9 190.0 %copy-start.12 = (s32[1024,1]{0,1:T(1,128)S(1)}, s32[1024,1]{0,1:T(1,128)}, u32[]{:S(2)}) copy-start(s32[1024,1]{0,1:T(1,128)} %copy-done.11) | copy-start | bytes 12292
  803.0 190.0 %copy-start.14 = (s32[1024,1]{0,1:T(1,128)S(1)}, s32[1024,1]{0,1:T(1,128)}, u32[]{:S(2)}) copy-start(s32[1024,1]{0,1:T(1,128)} %copy-done.13) | copy-start | bytes 12292
  803.0 190.0 %copy-start.20 = (pred[1024]{0:T(1024)(128)(4,1)S(1)}, pred[1024]{0:T(1024)(128)(4,1)}, u32[]{:S(2)}) copy-start(pred[1024]{0:T(1024)(128)(4,1)} %get-tuple-element.54) | copy-start | bytes 3076
  803.0 190.0 %copy-start.21 = (pred[1024]{0:T(1024)(128)(4,1)S(1)}, pred[1024]{0:T(1024)(128)(4,1)}, u32[]{:S(2)}) copy-start(pred[1024]{0:T(1024)(128)(4,1)} %get-tuple-element.55) | copy-start | bytes 3076
  803.0 190.0 %copy-start.22 = (pred[1024]{0:T(1024)(128)(4,1)S(1)}, pred[1024]{0:T(1024)(128)(4,1)}, u32[]{:S(2)}) copy-start(pred[1024]{0:T(1024)(128)(4,1)} %get-tuple-element.56) | copy-start | bytes 3076
  803.0 190.0 %copy-start.23 = (pred[1024]{0:T(1024)(128)(4,1)S(1)}, pred[1024]{0:T(1024)(128)(4,1)}, u32[]{:S(2)}) copy-start(pred[1024]{0:T(1024)(128)(4,1)} %get-tuple-element.57) | copy-start | bytes 3076
  803.0 228.6 %copy-start.15 = (f32[1024,1]{0,1:T(1,128)S(1)}, f32[1024,1]{0,1:T(1,128)}, u32[]{:S(2)}) copy-start(f32[1024,1]{0,1:T(1,128)} %multiply_rsqrt_fusion) | copy-start | bytes 12292
  803.0 229.2 %copy-start.1 = (bf16[512,2048]{1,0:T(8,128)(2,1)S(1)}, bf16[512,2048]{1,0:T(8,128)(2,1)}, u32[]{:S(2)}) copy-start(bf16[512,2048]{1,0:T(8,128)(2,1)} %param.13) | copy-start | bytes 6291460
Sparse Core Ops, SparseCore 0:
  23.4 129.2 all-reduce.4
  244.2 155.1 all-reduce.6
where the time goes:
time: 1050 us; the launch traced here: 1040 us
  local copies, waits for them, and re-layouts  304 us (29%)
  waiting for transfers between devices  281 us (27%)
  matrix products  217 us (21%)
  other arithmetic  119 us (11%)
  blocking collectives  100 us (10%)
  between operations  18.7 us (2%)
    gather x4, local copies, waits for them, and re-layouts, corner_value(): return jnp.where(inside, jnp.take(flat_prefix, position_flat), 0.0)  156 us
    psum x1, waiting for transfers between devices, shards(): summed_left = lax.psum(partial_left, 'row')  152 us
    psum x1, waiting for transfers between devices, shards(): summed_right = lax.psum(partial_right, 'col')  129 us
    unnamed x72, local copies, waits for them, and re-layouts  109 us
    dot_general x1, matrix products, shards(): jnp.dot(left_wide, middle, precision=highest, preferred_element_type=jnp....  59.3 us
    reduce_sum x1, other arithmetic, shards(): fresh = lax.psum(jnp.sum(residual * residual), ('row', 'col'))  48.9 us
    dot_general x1, matrix products, shards(): lax.dot_general(left_wide, summed_left, (((0,), (0,)), ((), ())), precisi...  48.5 us
    psum x1, blocking collectives, shards(): start_norm = lax.psum(jnp.sum(start_field * start_field), ('row', 'col'))  40 us
  transfers between devices with their start and end apart: 2, of which 2 were waited for; matrix products, arithmetic and copies ran while one was open for 0% of the time, Pallas kernels for 0%

commit v1 on v0

v1 whole, which is shorter than its diff:
```python
import functools

import jax
import jax.numpy as jnp
from jax import lax
from jax.experimental import pallas as pl
from jax.experimental.pallas import tpu as pltpu
from jax.sharding import PartitionSpec as P

F32 = jnp.float32
BF16 = jnp.bfloat16
VMEM_BYTES = 48 * 1024 * 1024


def params(sem_count):
    return pltpu.CompilerParams(
        dimension_semantics=("arbitrary",) * sem_count, vmem_limit_bytes=VMEM_BYTES
    )


def after(value, *earlier):
    return lax.optimization_barrier((value,) + earlier)[0]


def in_hbm(value):
    return pltpu.with_memory_space_constraint(value, pltpu.HBM)


def halves(value):
    high = value.astype(BF16)
    return high, (value - high.astype(F32)).astype(BF16)


def dot(a, b, dims=((1,), (0,))):
    return lax.dot_general(a, b, (dims, ((), ())), preferred_element_type=F32)


def rights_kernel(steps, x_ref, r_ref, l_ref, out_ref, core_ref):
    step = pl.program_id(0)
    summed = dot(x_ref[...], r_ref[...], ((1,), (1,)))
    out_ref[...] = summed.reshape(out_ref.shape)
    high, low = halves(summed)
    left = l_ref[...]
    part = dot(left, high) + dot(left, low)

    @pl.when(step == 0)
    def _():
        core_ref[...] = part

    @pl.when(step > 0)
    def _():
        core_ref[...] += part


def rights(x, r, l, groups, block):
    rows, cols = x.shape
    p = r.shape[0]
    each = rows // groups
    per_step = block // each
    return pl.pallas_call(
        functools.partial(rights_kernel, rows // block),
        out_shape=[
            jax.ShapeDtypeStruct((groups, each + p // groups, p), F32),
            jax.ShapeDtypeStruct((p, p), F32),
        ],
        grid=(rows // block,),
        in_specs=[
            pl.BlockSpec((block, cols), lambda i: (i, 0)),
            pl.BlockSpec((p, cols), lambda i: (0, 0)),
            pl.BlockSpec((p, block), lambda i: (0, i)),
        ],
        out_specs=[
            pl.BlockSpec((per_step, each, p), lambda i: (i, 0, 0)),
            pl.BlockSpec((p, p), lambda i: (0, 0)),
        ],
        compiler_params=params(1),
        cost_estimate=pl.CostEstimate(
            flops=4 * rows * cols * p, bytes_accessed=2 * rows * cols, transcendentals=0
        ),
        name="right_products",
    )(in_hbm(x), in_hbm(r), in_hbm(l))


def append_kernel(core_ref, old_ref, out_ref):
    out_ref[...] = core_ref[...]


def append_core(segments, core, each):
    groups, _, p = segments.shape
    share = p // groups
    return pl.pallas_call(
        append_kernel,
        out_shape=jax.ShapeDtypeStruct(segments.shape, F32),
        grid=(1,),
        in_specs=[
            pl.BlockSpec((groups, share, p), lambda i: (0, 0, 0)),
            pl.BlockSpec(memory_space=pl.ANY),
        ],
        out_specs=pl.BlockSpec((groups, share, p), lambda i: (0, each // share, 0)),
        input_output_aliases={1: 0},
        compiler_params=params(1),
        name="append_core",
    )(core.reshape(groups, share, p), segments)


def lefts_kernel(counts, l_ref, *refs):
    units = sum(counts)
    x_refs, out_refs = refs[:units], refs[units:]

    @pl.when(pl.program_id(0) == 0)
    def _():
        for out in out_refs:
            out[...] = jnp.zeros_like(out)

    left = l_ref[...]
    at = 0
    for count, out in zip(counts, out_refs):
        for k in range(count):
            width = x_refs[at].shape[1]
            out[:, k * width : (k + 1) * width] += dot(left, x_refs[at][...])
            at += 1


def lefts(l, x, start, counts, unit, block):
    p, rows = l.shape
    total = sum(counts)
    return pl.pallas_call(
        functools.partial(lefts_kernel, counts),
        out_shape=[jax.ShapeDtypeStruct((p, n * unit), F32) for n in counts],
        grid=(rows // block,),
        in_specs=[pl.BlockSpec((p, block), lambda i: (0, i))]
        + [
            pl.BlockSpec((block, unit), lambda i, u=start + u: (i, u)) for u in range(total)
        ],
        out_specs=[pl.BlockSpec((p, n * unit), lambda i: (0, 0)) for n in counts],
        compiler_params=params(1),
        cost_estimate=pl.CostEstimate(
            flops=2 * p * rows * total * unit,
            bytes_accessed=2 * rows * total * unit,
            transcendentals=0,
        ),
        name="left_products",
    )(in_hbm(l), *[in_hbm(x)] * total)


def mask_kernel(steps, col_start, rows_ref, cols_ref, x_ref, sums_ref, square_ref, acc):
    step = pl.program_id(0)
    block, width = x_ref.shape
    queries = acc.shape[0]

    @pl.when(step == 0)
    def _():
        acc[...] = jnp.zeros_like(acc)
        square_ref[...] = jnp.zeros_like(square_ref)

    values = x_ref[...]
    at = lax.broadcasted_iota(jnp.int32, (queries, block), 1) + step * block
    inside = (at >= rows_ref[:, 0:1]) & (at < rows_ref[:, 1:2])
    acc[...] += dot(inside.astype(F32).astype(BF16), values)
    wide = values.astype(F32)
    square_ref[...] += jnp.sum(wide * wide, axis=0, keepdims=True)

    @pl.when(step == steps - 1)
    def _():
        place = lax.broadcasted_iota(jnp.int32, (queries, width), 1) + col_start
        keep = (place >= cols_ref[:, 0:1]) & (place < cols_ref[:, 1:2])
        sums_ref[...] = jnp.sum(jnp.where(keep, acc[...], 0.0), axis=1, keepdims=True)


def mask_sums(x, row_bounds, col_bounds, start, width, block):
    rows = x.shape[0]
    queries = row_bounds.shape[0]
    steps = rows // block
    return pl.pallas_call(
        functools.partial(mask_kernel, steps, start),
        out_shape=[
            jax.ShapeDtypeStruct((queries, 1), F32),
            jax.ShapeDtypeStruct((1, width), F32),
        ],
        grid=(steps,),
        in_specs=[
            pl.BlockSpec((queries, 2), lambda i: (0, 0)),
            pl.BlockSpec((queries, 2), lambda i: (0, 0)),
            pl.BlockSpec((block, width), lambda i: (i, start // width)),
        ],
        out_specs=[
            pl.BlockSpec((queries, 1), lambda i: (0, 0)),
            pl.BlockSpec((1, width), lambda i: (0, 0)),
        ],
        scratch_shapes=[pltpu.VMEM((queries, width), F32)],
        compiler_params=params(1),
        cost_estimate=pl.CostEstimate(
            flops=2 * queries * rows * width, bytes_accessed=2 * rows * width, transcendentals=0
        ),
        name="interval_sums",
    )(row_bounds, col_bounds, in_hbm(x))


def finish_kernel(count, scale_ref, x_ref, s_ref, lt_ref, core_ref, r_ref, *refs):
    t_refs = refs[:count]
    out_ref, sum_ref, both, twice, both_low, twice_low = refs[count:]
    p, cols = r_ref.shape

    @pl.when(pl.program_id(0) == 0)
    def _():
        core_high, core_low = halves(core_ref[...])
        at = 0
        for t_ref in t_refs:
            span = slice(at, at + t_ref.shape[1])
            right = r_ref[:, span]
            high, low = halves(t_ref[...] + (dot(core_high, right) + dot(core_low, right)))
            twice[:p, span] = right
            twice[p:, span] = high
            twice_low[:p, span] = right
            twice_low[p:, span] = low
            at += t_ref.shape[1]
        sum_ref[...] = jnp.zeros_like(sum_ref)

    left = lt_ref[...]
    high, low = halves(s_ref[...])
    both[:, :p] = high
    both[:, p:] = left
    both_low[:, :p] = low
    both_low[:, p:] = left
    width = min(512, cols)
    for at in range(0, cols, width):
        span = slice(at, at + width)
        change = dot(both[...], twice[:, span]) + dot(both_low[...], twice_low[:, span])
        left_over = scale_ref[0] * x_ref[:, span].astype(F32) - scale_ref[1] * change
        out_ref[:, span] = left_over
        sum_ref[:, span] += jnp.sum(left_over * left_over, axis=0, keepdims=True)


def finish(scales, x, s, lt, core, r, parts, block):
    rows, cols = x.shape
    p = r.shape[0]
    whole = pl.BlockSpec(memory_space=pltpu.VMEM)
    return pl.pallas_call(
        functools.partial(finish_kernel, len(parts)),
        out_shape=[
            jax.ShapeDtypeStruct((rows, cols), F32),
            jax.ShapeDtypeStruct((1, cols), F32),
        ],
        grid=(rows // block,),
        in_specs=[
            pl.BlockSpec(memory_space=pltpu.SMEM),
            pl.BlockSpec((block, cols), lambda i: (i, 0)),
            pl.BlockSpec((block, p), lambda i: (i, 0)),
            pl.BlockSpec((block, p), lambda i: (i, 0)),
            whole,
            whole,
        ]
        + [whole] * len(parts),
        out_specs=[
            pl.BlockSpec((block, cols), lambda i: (i, 0)),
            pl.BlockSpec((1, cols), lambda i: (0, 0)),
        ],
        scratch_shapes=[
            pltpu.VMEM((block, 2 * p), BF16),
            pltpu.VMEM((2 * p, cols), BF16),
            pltpu.VMEM((block, 2 * p), BF16),
            pltpu.VMEM((2 * p, cols), BF16),
        ],
        compiler_params=params(1),
        cost_estimate=pl.CostEstimate(
            flops=8 * p * rows * cols, bytes_accessed=6 * rows * cols, transcendentals=0
        ),
        name="finish_residual",
    )(scales, in_hbm(x), in_hbm(s), in_hbm(lt), core, r, *parts)


def swap(value, axis, mask, size):
    return lax.ppermute(value, axis, [(i, i ^ mask) for i in range(size)])


def powers(size):
    masks = []
    mask = 1
    while mask < size:
        masks.append(mask)
        mask *= 2
    return masks


def fold(value, axis, size):
    for mask in powers(size):
        value = value + swap(value, axis, mask, size)
    return value


def gather(value, axis, size, place):
    for mask in powers(size):
        got = swap(value, axis, mask, size)
        upper = (place // mask) % 2 == 1
        value = jnp.where(
            upper, jnp.concatenate([got, value]), jnp.concatenate([value, got])
        )
    return value


def shards(n_row, n_col, x, theta_left, theta_right, query_rows, query_cols):
    rows, cols = x.shape
    p = theta_left.shape[0]
    queries = query_rows.shape[0]
    z = lax.axis_index("row")
    j = lax.axis_index("col")
    tall = min(1024, rows)
    each = rows // n_col
    share = p // n_col
    unit = max(128, cols // 8)
    if cols == 8 * unit:
        spans = [1, 2, 2, 2, 1]
        left_groups = [[0], [1], [2, 3, 4]]
    else:
        spans = [1] * (cols // unit)
        left_groups = [[c] for c in range(len(spans))]
    count = len(spans)

    row_bounds = jnp.clip(query_rows - z * rows, 0, rows)
    col_bounds = query_cols - j * cols

    segments, core_part = rights(x, theta_right, theta_left, n_col, tall)
    segments = append_core(segments, core_part, each)
    own = lax.psum_scatter(segments, "col", scatter_dimension=0, tiled=True)

    left_parts = []
    for group in left_groups:
        left_parts += lefts(
            after(theta_left, left_parts[-1] if left_parts else segments),
            x,
            sum(spans[: group[0]]),
            [spans[c] for c in group],
            unit,
            tall,
        )

    half = n_row // 2
    inward = [[(h, h + 1), (n_row - 1 - h, n_row - 2 - h)] for h in range(half - 1)]
    across = [(half - 1, half), (half, half - 1)]
    outward = [[(b, a) for a, b in pairs] for pairs in reversed(inward)]

    def hop(value, pairs):
        return lax.ppermute(value, "row", pairs)

    def send_in(value):
        for pairs in inward:
            value = value + hop(value, pairs)
        return value

    def settle(pending):
        total, got, targets = pending
        chosen = functools.reduce(jnp.logical_or, [z == t for t in targets])
        return jnp.where(chosen, got, total)

    def send_out(total):
        pending = None
        for pairs in outward:
            if pending is not None:
                total = settle(pending)
            pending = (total, hop(total, pairs), [b for _, b in pairs])
        return pending

    flight_in = {}
    for c in range(min(2, count)):
        flight_in[c] = send_in(left_parts[c])
    token = left_parts[-1]

    interval = jnp.zeros((queries, 1), F32)
    squares = jnp.zeros((), F32)
    mask_width = cols // 4
    mask_starts = list(range(0, cols, mask_width))
    last_width = left_parts[-1].shape[1]
    core_rows = share * p // last_width

    current, flight_mid, flight_out = {}, {}, {}
    lt = None
    for step in range(count + 1):
        if step < count:
            current[step] = after(flight_in[step], token)
            token = current[step]
            flight_mid[step] = hop(current[step], across)
            if step == count - 2:
                own = after(own, token)
                own_rows = own[0, :each]
                summed_right = lax.all_gather(own_rows, "col", axis=0, tiled=True)
                flight_in[count - 1] = send_in(
                    jnp.concatenate(
                        [left_parts[count - 1], own[0, each:].reshape(core_rows, last_width)]
                    )
                )
            elif step + 2 < count:
                flight_in[step + 2] = send_in(after(left_parts[step + 2], token))
        if step >= 1:
            c = step - 1
            total = after(current[c], token) + flight_mid[c]
            token = total
            flight_out[c] = send_out(total)
        if mask_starts:
            sums, square = mask_sums(
                x, after(row_bounds, token), col_bounds, mask_starts.pop(0), mask_width, tall
            )
            interval = interval + sums
            squares = squares + jnp.sum(square)
            token = sums
        elif lt is None:
            lt = after(theta_left, token).T
            token = lt
    totals = [settle(flight_out[c]) for c in range(count)]
    own_core = totals[-1][p:].reshape(share, p)
    totals[-1] = totals[-1][:p]
    core = gather(own_core, "col", n_col, j)
    t_square = sum(jnp.sum(total * total) for total in totals)

    lines = queries // 128
    scalars = jnp.stack(
        [
            squares,
            jnp.sum(own_rows * own_rows) + (t_square + jnp.sum(own_core * own_core)) / n_row,
        ]
    )
    packed = jnp.concatenate(
        [interval.reshape(lines, 128), jnp.repeat(scalars, 4)[:, None] + jnp.zeros((1, 128), F32)]
    )
    packed = fold(fold(packed, "row", n_row), "col", n_col)
    start_norm = packed[lines, 0]
    extra = packed[lines + 4, 0]
    curvature = start_norm + extra
    alpha = start_norm / curvature
    low_row, high_row = query_rows[:, 0], query_rows[:, 1]
    low_col, high_col = query_cols[:, 0], query_cols[:, 1]
    area = (high_row - low_row).astype(F32) * (high_col - low_col).astype(F32)
    answers = alpha * packed[:lines].reshape(queries) / jnp.sqrt(area)

    residual, square = finish(
        jnp.stack([extra / curvature, alpha]),
        x,
        summed_right,
        lt,
        core,
        theta_right,
        totals,
        min(256, rows),
    )
    fresh = fold(fold(jnp.full((8, 128), jnp.sum(square)), "row", n_row), "col", n_col)
    step_ratio = (fresh[0, 0] / start_norm).reshape(1)
    return (residual, step_ratio, answers)


def solution(mesh):
    return jax.shard_map(
        functools.partial(shards, mesh.shape["row"], mesh.shape["col"]),
        mesh=mesh,
        in_specs=(P("row", "col"), P(None, "row"), P(None, "col"), P(), P()),
        out_specs=(P("row", "col"), P(), P()),
        check_vma=False,
    )
```

time: 1050 us -> 349 us (0.33)
  local copies, waits for them, and re-layouts: 304 us -> 14.7 us
  matrix products: 217 us -> 0 us
  waiting for transfers between devices: 281 us -> 101 us
  Pallas kernels: 0 us -> 116 us
  blocking collectives: 100 us -> 0 us
  other arithmetic: 119 us -> 39.6 us
  starting transfers between devices: 0.08 us -> 49.1 us
    psum x2 -> x0, waiting for transfers between devices: 281 us -> none  [the longest x1 152 us: shards(): summed_left = lax.psum(partial_left, 'row')]
    dot_general x6 -> x0, matrix products: 217 us -> none  [the longest x1 59.3 us: shards(): jnp.dot(left_wide, middle, precision=highest, preferred_element_type=jnp....]
    gather x4 -> x0, local copies, waits for them, and re-layouts: 156 us -> none  [corner_value(): return jnp.where(inside, jnp.take(flat_prefix, position_flat), 0.0)]
    pallas_call x0 -> x10, Pallas kernels: none -> 116 us  [the longest x1 45 us: finish(): pl.pallas_call(functools.partial(finish_kernel, len(parts)), out_shape=[j...]
    unnamed x72 -> x18, local copies, waits for them, and re-layouts: 109 us -> 4.38 us
    ppermute x0 -> x28, waiting for transfers between devices: none -> 101 us  [the longest x15 71.6 us: hop(): return lax.ppermute(value, 'row', pairs)]
    psum x2 -> x0, blocking collectives: 77.1 us -> none  [the longest x1 40 us: shards(): start_norm = lax.psum(jnp.sum(start_field * start_field), ('row', 'col'))]
    ppermute x0 -> x28, starting transfers between devices: none -> 49 us  [the longest x15 41 us: hop(): return lax.ppermute(value, 'row', pairs)]
  transfers between devices with their start and end apart: 2 -> 30, of which waited for: 2 -> 17; matrix products, arithmetic and copies ran while one was open for 0% -> 13% of each run, Pallas kernels for 0% -> 15%
where the time goes in v1:
time: 349 us; the launch traced here: 347 us
  Pallas kernels  116 us (33%)
  waiting for transfers between devices  101 us (29%)
  starting transfers between devices  49.1 us (14%)
  other arithmetic  39.6 us (11%)
  between operations  26.8 us (8%)
  local copies, waits for them, and re-layouts  14.7 us (4%)
    ppermute x15, waiting for transfers between devices, hop(): return lax.ppermute(value, 'row', pairs)  71.6 us
    pallas_call x1, Pallas kernels, finish(): pl.pallas_call(functools.partial(finish_kernel, len(parts)), out_shape=[j...  45 us
    ppermute x15, starting transfers between devices, hop(): return lax.ppermute(value, 'row', pairs)  41 us
    pallas_call x4, Pallas kernels, mask_sums(): pl.pallas_call(functools.partial(mask_kernel, steps, start), out_shape=[j...  31 us
    ppermute x13, waiting for transfers between devices, swap(): return lax.ppermute(value, axis, [(i, i ^ mask) for i in range(size)])  29.1 us
    pallas_call x3, Pallas kernels, lefts(): pl.pallas_call(functools.partial(lefts_kernel, counts), out_shape=[jax.Sh...  20.3 us
    pallas_call x1, Pallas kernels, rights(): pl.pallas_call(functools.partial(rights_kernel, rows // block), out_shape...  18.9 us
    reduce_sum x4, other arithmetic, shards(): t_square = sum((jnp.sum(total * total) for total in totals))  10 us
  transfers between devices with their start and end apart: 30, of which 17 were waited for; matrix products, arithmetic and copies ran while one was open for 13% of the time, Pallas kernels for 15%

profile of v1, /device:TPU:0, one launch (start us, length us, event | category | flops | bytes accessed | tf_op | source)
XLA Modules:
  0.0 347.3 jit_solution(10600485981470106670)
XLA Ops:
  7.2 18.9 %right_products.1 = (f32[8,576,512]{2,1,0:T(8,128)}, f32[512,512]{1,0:T(8,128)S(1)}) custom-call(bf16[4096,2048]{1,0:T(8,128)(2,1)} %x_ref.11, bf16[512,2048]{1,0:T(8,128)(2,1)} %r_ref.3, bf16[512,4096]{1,0:T(8,128)(2,1)} %l_ref.4), custom_call_target="tpu_custom_call" | custom-call | flops 17179869184 | bytes 16777216 | tf_op jit(solution)/shard_map/right_products/pallas_call | solution.py:60
  26.1 1.0 append_core.1
  27.2 4.3 %left_products.3 = f32[512,256]{1,0:T(8,128)S(1)} custom-call(bf16[512,4096]{1,0:T(8,128)(2,1)} %l_ref.4, bf16[4096,2048]{1,0:T(8,128)(2,1)} %x_ref.11), custom_call_target="tpu_custom_call" | custom-call | flops 1073741824 | bytes 2097152 | tf_op jit(solution)/shard_map/left_products/pallas_call | solution.py:127
  31.5 5.8 %collective-permute-start = (f32[512,256]{1,0:T(8,128)S(1)}, f32[512,256]{1,0:T(8,128)}, u32[]{:S(2)}, u32[]{:S(2)}) collective-permute-start(f32[512,256]{1,0:T(8,128)S(1)} %left_products.3), channel_id=1, source_target_pairs={{0,8},{24,16},{1,9},{25,17},{2,10},{26,18},{3,11},{27,19},{4,12},{... | collective-permute-start | bytes 1572872 | tf_op jit(solution)/shard_map/ppermute | solution.py:343
  37.2 6.9 %left_products.4 = f32[512,512]{1,0:T(8,128)S(1)} custom-call(bf16[512,4096]{1,0:T(8,128)(2,1)} %l_ref.4, bf16[4096,2048]{1,0:T(8,128)(2,1)} %x_ref.11, bf16[4096,2048]{1,0:T(8,128)(2,1)} %x_ref.11), custom_call_target="tpu_custom_call" | custom-call | flops 2147483648 | bytes 4194304 | tf_op jit(solution)/shard_map/left_products/pallas_call | solution.py:127
  44.2 2.3 collective-permute-start.1
  47.1 9.1 %left_products.5 = (f32[512,512]{1,0:T(8,128)S(1)}, f32[512,512]{1,0:T(8,128)S(1)}, f32[512,256]{1,0:T(8,128)S(1)}) custom-call(bf16[512,4096]{1,0:T(8,128)(2,1)} %l_ref.4, bf16[4096,2048]{1,0:T(8,128)(2,1)} %x_ref.11, bf16[4096,2048]{1,0:T(8,128)(2,1)} %x_ref.11, bf16[4096,2048]{1,0:T(8,128)(2,1)} %x_ref.11, bf16[4096,2048]{1,0:T(8,128)(2,1)} %x_ref.11, ...), custom_call_target="tpu_custom_call" | custom-call | flops 5368709120 | bytes 10485760 | tf_op jit(solution)/shard_map/left_products/pallas_call | solution.py:127
  56.2 1.1 add.121
  57.4 1.4 collective-permute-start.3
  58.7 7.8 %interval_sums.4 = (f32[1024,1]{1,0:T(8,128)S(1)}, f32[1,512]{1,0:T(1,128)S(1)}) custom-call(s32[1024,2]{1,0:T(8,128)S(1)} %broadcast_clamp_fusion.rows_ref, s32[1024,2]{1,0:T(8,128)S(1)} %broadcast_subtract_fusion.cols_ref, bf16[4096,2048]{1,0:T(8,128)(2,1)} %x_ref.11), custom_call_target="tpu_custom_call" | custom-call | flops 4294967296 | bytes 4194304 | tf_op jit(solution)/shard_map/interval_sums/pallas_call | solution.py:174
  66.6 4.7 %collective-permute-done.1 = f32[512,512]{1,0:T(8,128)} collective-permute-done((f32[512,512]{1,0:T(8,128)S(1)}, f32[512,512]{1,0:T(8,128)}, u32[]{:S(2)}, u32[]{:S(2)}) %collective-permute-start.1) | collective-permute-done | bytes 1048608 | tf_op jit(solution)/shard_map/ppermute | solution.py:343
  71.2 1.4 add.122
  73.4 7.3 %collective-permute-start.5 = (f32[512,512]{1,0:T(8,128)S(1)}, f32[512,512]{1,0:T(8,128)S(1)}, u32[]{:S(2)}, u32[]{:S(2)}) collective-permute-start(f32[512,512]{1,0:T(8,128)S(1)} %get-tuple-element.59), channel_id=1, source_target_pairs={{0,8},{24,16},{1,9},{25,17},{2,10},{26,18},{3,11},{27,19},{4,12},{... | collective-permute-start | bytes 3145736 | tf_op jit(solution)/shard_map/ppermute | solution.py:343
  82.5 7.7 %interval_sums.5 = (f32[1024,1]{1,0:T(8,128)S(1)}, f32[1,512]{1,0:T(1,128)S(1)}) custom-call(s32[1024,2]{1,0:T(8,128)S(1)} %broadcast_clamp_fusion.rows_ref, s32[1024,2]{1,0:T(8,128)S(1)} %broadcast_subtract_fusion.cols_ref, bf16[4096,2048]{1,0:T(8,128)(2,1)} %x_ref.11), custom_call_target="tpu_custom_call" | custom-call | flops 4294967296 | bytes 4194304 | tf_op jit(solution)/shard_map/interval_sums/pallas_call | solution.py:174
  90.2 3.5 collective-permute-done.3
  93.7 1.2 add.125
  94.9 1.3 add.126
  96.1 18.9 %collective-permute-done.5 = f32[512,512]{1,0:T(8,128)S(1)} collective-permute-done((f32[512,512]{1,0:T(8,128)S(1)}, f32[512,512]{1,0:T(8,128)S(1)}, u32[]{:S(2)}, u32[]{:S(2)}) %collective-permute-start.5) | collective-permute-done | bytes 1048608 | tf_op jit(solution)/shard_map/ppermute | solution.py:343
  115.0 1.2 add.128
  116.2 7.7 %interval_sums.6 = (f32[1024,1]{1,0:T(8,128)S(1)}, f32[1,512]{1,0:T(1,128)S(1)}) custom-call(s32[1024,2]{1,0:T(8,128)S(1)} %broadcast_clamp_fusion.rows_ref, s32[1024,2]{1,0:T(8,128)S(1)} %broadcast_subtract_fusion.cols_ref, bf16[4096,2048]{1,0:T(8,128)(2,1)} %x_ref.11), custom_call_target="tpu_custom_call" | custom-call | flops 4294967296 | bytes 4194304 | tf_op jit(solution)/shard_map/interval_sums/pallas_call | solution.py:174
  123.9 3.0 fusion.3
  127.0 1.7 collective-permute-start.6
  131.1 11.1 %collective-permute-start.10 = (f32[640,256]{1,0:T(8,128)}, f32[640,256]{1,0:T(8,128)S(1)}, u32[]{:S(2)}, u32[]{:S(2)}) collective-permute-start(f32[640,256]{1,0:T(8,128)} %constant_dynamic-update-slice_fusion), channel_id=1, source_target_pairs={{0,8},{24,16},{1,9},{25,17},{2,10},{26,18},{3,11},{27,19},{4,12},{... | collective-permute-start | bytes 1966088 | tf_op jit(solution)/shard_map/ppermute | solution.py:343
  142.2 1.3 collective-permute-start.7
  143.5 1.7 collective-permute-start.11
  145.2 1.3 collective-permute-start.8
  146.5 2.7 add.129
  149.2 7.8 %interval_sums.7 = (f32[1024,1]{1,0:T(8,128)S(1)}, f32[1,512]{1,0:T(1,128)S(1)}) custom-call(s32[1024,2]{1,0:T(8,128)S(1)} %broadcast_clamp_fusion.rows_ref, s32[1024,2]{1,0:T(8,128)S(1)} %broadcast_subtract_fusion.cols_ref, bf16[4096,2048]{1,0:T(8,128)(2,1)} %x_ref.11), custom_call_target="tpu_custom_call" | custom-call | flops 4294967296 | bytes 4194304 | tf_op jit(solution)/shard_map/interval_sums/pallas_call | solution.py:174
  157.9 1.5 collective-permute-start.13
  159.5 1.3 collective-permute-start.9
  163.4 2.6 multiply_reduce_fusion.5
  167.3 2.7 add.137
  170.1 6.5 %copy.19 = bf16[512,4096]{0,1:T(8,128)(2,1)} copy(bf16[512,4096]{1,0:T(8,128)(2,1)} %l_ref.4) | data formatting | bytes 8388608 | tf_op jit(solution)/shard_map/optimization_barrier | solution.py:22
  176.6 2.2 add.139
  178.8 1.3 collective-permute-start.14
  181.5 1.5 collective-permute-start.12
  183.1 2.2 multiply_reduce_fusion.3
  186.6 16.7 %collective-permute-done.9 = f32[512,512]{1,0:T(8,128)} collective-permute-done((f32[512,512]{1,0:T(8,128)}, f32[512,512]{1,0:T(8,128)}, u32[]{:S(2)}, u32[]{:S(2)}) %collective-permute-start.9) | collective-permute-done | bytes 1048608 | tf_op jit(solution)/shard_map/ppermute | solution.py:343
  203.3 2.2 multiply_reduce_fusion.2
  206.1 11.2 %collective-permute-done.14 = f32[640,256]{1,0:T(8,128)} collective-permute-done((f32[640,256]{1,0:T(8,128)}, f32[640,256]{1,0:T(8,128)}, u32[]{:S(2)}, u32[]{:S(2)}) %collective-permute-start.14) | collective-permute-done | bytes 655392 | tf_op jit(solution)/shard_map/ppermute | solution.py:343
  217.4 1.2 broadcast_select_fusion.3
  219.3 16.6 %collective-permute-done.12 = f32[512,512]{1,0:T(8,128)} collective-permute-done((f32[512,512]{1,0:T(8,128)}, f32[512,512]{1,0:T(8,128)}, u32[]{:S(2)}, u32[]{:S(2)}) %collective-permute-start.12) | collective-permute-done | bytes 1048608 | tf_op jit(solution)/shard_map/ppermute | solution.py:343
  236.0 3.1 multiply_reduce_fusion.1
  239.7 1.6 collective-permute-start.21
  241.3 1.5 fusion.4
  245.0 1.1 collective-permute-done.21
  246.2 1.6 collective-permute-start.22
  247.9 3.6 %collective-permute-done.15 = f32[16,128]{1,0:T(8,128)S(1)} collective-permute-done((f32[16,128]{1,0:T(8,128)S(1)}, f32[16,128]{1,0:T(8,128)S(1)}, u32[]{:S(2)}, u32[]{:S(2)}) %collective-permute-start.15) | collective-permute-done | bytes 8224 | tf_op jit(solution)/shard_map/ppermute | solution.py:273
  251.6 4.5 %collective-permute-done.16 = f32[16,128]{1,0:T(8,128)S(1)} collective-permute-done((f32[16,128]{1,0:T(8,128)S(1)}, f32[16,128]{1,0:T(8,128)S(1)}, u32[]{:S(2)}, u32[]{:S(2)}) %collective-permute-start.16) | collective-permute-done | bytes 8224 | tf_op jit(solution)/shard_map/ppermute | solution.py:273
  256.2 1.2 collective-permute-done.17
  257.3 1.8 collective-permute-start.18
  259.1 1.9 collective-permute-done.18
  261.5 3.2 collective-permute-done.19
  268.0 1.8 maximum_select_fusion.core_ref
  269.8 1.2 copy-done
  271.1 1.0 copy-done.1
  272.1 1.0 copy-done.2
  273.1 45.0 %finish_residual.1 = (f32[4096,2048]{1,0:T(8,128)}, f32[1,2048]{1,0:T(1,128)S(1)}) custom-call(f32[2]{0:T(128)S(1)} %pad_maximum_fusion.2.scale_ref, bf16[4096,2048]{1,0:T(8,128)(2,1)} %x_ref.11, f32[4096,512]{1,0:T(8,128)} %bitcast.22, bf16[4096,512]{1,0:T(8,128)(2,1)} %bitcast.18, f32[512,512]{1,0:T(8,128)S(1)} %maximum_select_fusion.core_ref, ...), custom_call_target="tpu_custom_call" | custom-call | flops 34359738368 | bytes 50331648 | tf_op jit(solution)/shard_map/finish_residual/pallas_call | solution.py:238
  319.5 3.6 %collective-permute-done.23 = f32[8,128]{1,0:T(8,128)S(1)} collective-permute-done((f32[8,128]{1,0:T(8,128)S(1)}, f32[8,128]{1,0:T(8,128)S(1)}, u32[]{:S(2)}, u32[]{:S(2)}) %collective-permute-start.23) | collective-permute-done | bytes 4128 | tf_op jit(solution)/shard_map/ppermute | solution.py:273
  323.8 4.5 %collective-permute-done.24 = f32[8,128]{1,0:T(8,128)S(1)} collective-permute-done((f32[8,128]{1,0:T(8,128)S(1)}, f32[8,128]{1,0:T(8,128)S(1)}, u32[]{:S(2)}, u32[]{:S(2)}) %collective-permute-start.24) | collective-permute-done | bytes 4128 | tf_op jit(solution)/shard_map/ppermute | solution.py:273
  329.1 1.2 collective-permute-done.25
  330.2 1.8 collective-permute-start.26
  332.0 1.8 collective-permute-done.26
  334.9 2.5 collective-permute-done.27
  (83 shorter events, 16.2 us)
Async XLA Ops:
  7.2 116.8 %reduce-scatter.2.cloned.1.call-start = ((), (), s32[]{:S(2)}) async-start(), calls=%async_computation.1 | async-start | bytes 10616832 | tf_op jit(solution)/shard_map/reduce_scatter | solution.py:324
  27.1 242.7 %all-gather.3.cloned.1.call-start = ((), (), s32[]{:S(2)}) async-start(), calls=%async_computation.2 | async-start | bytes 9437184 | tf_op jit(solution)/shard_map/all_gather | solution.py:385
  31.5 15.0 %copy-start.7 = (s32[1024,2]{0,1:T(2,128)S(1)}, s32[1024,2]{0,1:T(2,128)}, u32[]{:S(2)}) copy-start(s32[1024,2]{0,1:T(2,128)} %param.8) | copy-start | bytes 24580
  31.5 15.2 %copy-start.6 = (s32[1024,2]{0,1:T(2,128)S(1)}, s32[1024,2]{0,1:T(2,128)}, u32[]{:S(2)}) copy-start(s32[1024,2]{0,1:T(2,128)} %param.9) | copy-start | bytes 24580
  31.5 24.7 %collective-permute-start = (f32[512,256]{1,0:T(8,128)S(1)}, f32[512,256]{1,0:T(8,128)}, u32[]{:S(2)}, u32[]{:S(2)}) collective-permute-start(f32[512,256]{1,0:T(8,128)S(1)} %left_products.3), channel_id=1, source_target_pairs={{0,8},{24,16},{1,9},{25,17},{2,10},{26,18},{3,11},{27,19},{4,12},{... | collective-permute-start | bytes 1572872 | tf_op jit(solution)/shard_map/ppermute | solution.py:343
  44.2 27.0 %collective-permute-start.1 = (f32[512,512]{1,0:T(8,128)S(1)}, f32[512,512]{1,0:T(8,128)}, u32[]{:S(2)}, u32[]{:S(2)}) collective-permute-start(f32[512,512]{1,0:T(8,128)S(1)} %left_products.4), channel_id=1, source_target_pairs={{0,8},{24,16},{1,9},{25,17},{2,10},{26,18},{3,11},{27,19},{4,12},{... | collective-permute-start | bytes 3145736 | tf_op jit(solution)/shard_map/ppermute | solution.py:343
  57.4 36.3 %collective-permute-start.3 = (f32[512,512]{1,0:T(8,128)S(1)}, f32[512,512]{1,0:T(8,128)S(1)}, u32[]{:S(2)}, u32[]{:S(2)}) collective-permute-start(f32[512,512]{1,0:T(8,128)S(1)} %get-tuple-element.53), channel_id=1, source_target_pairs={{0,8},{24,16},{1,9},{25,17},{2,10},{26,18},{3,11},{27,19},{4,12},{... | collective-permute-start | bytes 3145736 | tf_op jit(solution)/shard_map/ppermute | solution.py:343
  72.7 22.2 %collective-permute-start.4 = (f32[512,512]{1,0:T(8,128)S(1)}, f32[512,512]{1,0:T(8,128)S(1)}, u32[]{:S(2)}, u32[]{:S(2)}) collective-permute-start(f32[512,512]{1,0:T(8,128)S(1)} %add.122), channel_id=1, source_target_pairs={{8,16},{16,8},{9,17},{17,9},{10,18},{18,10},{11,19},{19,11},{12,20... | collective-permute-start | bytes 3145736 | tf_op jit(solution)/shard_map/ppermute | solution.py:343
  73.4 41.6 %collective-permute-start.5 = (f32[512,512]{1,0:T(8,128)S(1)}, f32[512,512]{1,0:T(8,128)S(1)}, u32[]{:S(2)}, u32[]{:S(2)}) collective-permute-start(f32[512,512]{1,0:T(8,128)S(1)} %get-tuple-element.59), channel_id=1, source_target_pairs={{0,8},{24,16},{1,9},{25,17},{2,10},{26,18},{3,11},{27,19},{4,12},{... | collective-permute-start | bytes 3145736 | tf_op jit(solution)/shard_map/ppermute | solution.py:343
  80.7 0.9 collective-permute-start.2
  127.0 19.5 %collective-permute-start.6 = (f32[512,512]{1,0:T(8,128)}, f32[512,512]{1,0:T(8,128)}, u32[]{:S(2)}, u32[]{:S(2)}) collective-permute-start(f32[512,512]{1,0:T(8,128)} %add.125), channel_id=1, source_target_pairs={{8,16},{16,8},{9,17},{17,9},{10,18},{18,10},{11,19},{19,11},{12,20... | collective-permute-start | bytes 3145736 | tf_op jit(solution)/shard_map/ppermute | solution.py:343
  131.1 25.9 %collective-permute-start.10 = (f32[640,256]{1,0:T(8,128)}, f32[640,256]{1,0:T(8,128)S(1)}, u32[]{:S(2)}, u32[]{:S(2)}) collective-permute-start(f32[640,256]{1,0:T(8,128)} %constant_dynamic-update-slice_fusion), channel_id=1, source_target_pairs={{0,8},{24,16},{1,9},{25,17},{2,10},{26,18},{3,11},{27,19},{4,12},{... | collective-permute-start | bytes 1966088 | tf_op jit(solution)/shard_map/ppermute | solution.py:343
  142.2 21.3 %collective-permute-start.7 = (f32[512,256]{1,0:T(8,128)}, f32[512,256]{1,0:T(8,128)}, u32[]{:S(2)}, u32[]{:S(2)}) collective-permute-start(f32[512,256]{1,0:T(8,128)} %add.123), channel_id=1, source_target_pairs={{8,0},{16,24},{9,1},{17,25},{10,2},{18,26},{11,3},{19,27},{12,4},{... | collective-permute-start | bytes 1572872 | tf_op jit(solution)/shard_map/ppermute | solution.py:343
  143.5 23.9 %collective-permute-start.11 = (f32[512,512]{1,0:T(8,128)}, f32[512,512]{1,0:T(8,128)}, u32[]{:S(2)}, u32[]{:S(2)}) collective-permute-start(f32[512,512]{1,0:T(8,128)} %add.128), channel_id=1, source_target_pairs={{8,16},{16,8},{9,17},{17,9},{10,18},{18,10},{11,19},{19,11},{12,20... | collective-permute-start | bytes 3145736 | tf_op jit(solution)/shard_map/ppermute | solution.py:343
  145.2 37.9 %collective-permute-start.8 = (f32[512,512]{1,0:T(8,128)}, f32[512,512]{1,0:T(8,128)}, u32[]{:S(2)}, u32[]{:S(2)}) collective-permute-start(f32[512,512]{1,0:T(8,128)} %add.126), channel_id=1, source_target_pairs={{8,0},{16,24},{9,1},{17,25},{10,2},{18,26},{11,3},{19,27},{12,4},{... | collective-permute-start | bytes 3145736 | tf_op jit(solution)/shard_map/ppermute | solution.py:343
  149.2 7.8 %copy-start.4 = (f32[640,256]{1,0:T(8,128)S(1)}, f32[640,256]{1,0:T(8,128)}, u32[]{:S(2)}) copy-start(f32[640,256]{1,0:T(8,128)} %constant_dynamic-update-slice_fusion) | copy-start | bytes 1966084
  157.9 18.6 %collective-permute-start.13 = (f32[640,256]{1,0:T(8,128)}, f32[640,256]{1,0:T(8,128)}, u32[]{:S(2)}, u32[]{:S(2)}) collective-permute-start(f32[640,256]{1,0:T(8,128)} %add.136), channel_id=1, source_target_pairs={{8,16},{16,8},{9,17},{17,9},{10,18},{18,10},{11,19},{19,11},{12,20... | collective-permute-start | bytes 1966088 | tf_op jit(solution)/shard_map/ppermute | solution.py:343
  159.5 43.9 %collective-permute-start.9 = (f32[512,512]{1,0:T(8,128)}, f32[512,512]{1,0:T(8,128)}, u32[]{:S(2)}, u32[]{:S(2)}) collective-permute-start(f32[512,512]{1,0:T(8,128)} %add.129), channel_id=1, source_target_pairs={{8,0},{16,24},{9,1},{17,25},{10,2},{18,26},{11,3},{19,27},{12,4},{... | collective-permute-start | bytes 3145736 | tf_op jit(solution)/shard_map/ppermute | solution.py:343
  163.4 19.6 %copy-start.3 = (f32[512,512]{1,0:T(8,128)S(1)}, f32[512,512]{1,0:T(8,128)}, u32[]{:S(2)}) copy-start(f32[512,512]{1,0:T(8,128)} %add.126) | copy-start | bytes 3145732
  178.8 38.6 %collective-permute-start.14 = (f32[640,256]{1,0:T(8,128)}, f32[640,256]{1,0:T(8,128)}, u32[]{:S(2)}, u32[]{:S(2)}) collective-permute-start(f32[640,256]{1,0:T(8,128)} %add.139), channel_id=1, source_target_pairs={{8,0},{16,24},{9,1},{17,25},{10,2},{18,26},{11,3},{19,27},{12,4},{... | collective-permute-start | bytes 1966088 | tf_op jit(solution)/shard_map/ppermute | solution.py:343
  181.5 54.4 %collective-permute-start.12 = (f32[512,512]{1,0:T(8,128)}, f32[512,512]{1,0:T(8,128)}, u32[]{:S(2)}, u32[]{:S(2)}) collective-permute-start(f32[512,512]{1,0:T(8,128)} %add.137), channel_id=1, source_target_pairs={{8,0},{16,24},{9,1},{17,25},{10,2},{18,26},{11,3},{19,27},{12,4},{... | collective-permute-start | bytes 3145736 | tf_op jit(solution)/shard_map/ppermute | solution.py:343
  219.3 20.4 %collective-permute-start.20 = (f32[64,512]{1,0:T(8,128)S(1)}, f32[64,512]{1,0:T(8,128)S(1)}, u32[]{:S(2)}, u32[]{:S(2)}) collective-permute-start(f32[64,512]{1,0:T(8,128)S(1)} %reshape.30), channel_id=1, source_target_pairs={{0,1},{1,0},{2,3},{3,2},{4,5},{5,4},{6,7},{7,6},{8,9},{9,8},{10,11... | collective-permute-start | bytes 393224 | tf_op jit(solution)/shard_map/ppermute | solution.py:273
  239.7 6.4 %collective-permute-start.21 = (f32[128,512]{1,0:T(8,128)S(1)}, f32[128,512]{1,0:T(8,128)S(1)}, u32[]{:S(2)}, u32[]{:S(2)}) collective-permute-start(f32[128,512]{1,0:T(8,128)S(1)} %maximum_select_fusion.2), channel_id=1, source_target_pairs={{0,2},{1,3},{2,0},{3,1},{4,6},{5,7},{6,4},{7,5},{8,10},{9,11},{10,... | collective-permute-start | bytes 786440 | tf_op jit(solution)/shard_map/ppermute | solution.py:273
  246.2 21.8 %copy-start.5 = (f32[256,512]{1,0:T(8,128)}, f32[256,512]{1,0:T(8,128)S(1)}, u32[]{:S(2)}) copy-start(f32[256,512]{1,0:T(8,128)S(1)} %maximum_select_fusion.1) | copy-start | bytes 1572868
  246.2 21.8 %collective-permute-start.22 = (f32[256,512]{1,0:T(8,128)S(1)}, f32[256,512]{1,0:T(8,128)}, u32[]{:S(2)}, u32[]{:S(2)}) collective-permute-start(f32[256,512]{1,0:T(8,128)S(1)} %maximum_select_fusion.1), channel_id=1, source_target_pairs={{0,4},{1,5},{2,6},{3,7},{4,0},{5,1},{6,2},{7,3},{8,12},{9,13},{10,... | collective-permute-start | bytes 1572872 | tf_op jit(solution)/shard_map/ppermute | solution.py:273
  247.9 3.7 %collective-permute-start.15 = (f32[16,128]{1,0:T(8,128)S(1)}, f32[16,128]{1,0:T(8,128)S(1)}, u32[]{:S(2)}, u32[]{:S(2)}) collective-permute-start(f32[16,128]{1,0:T(8,128)S(1)} %pad_maximum_fusion), channel_id=1, source_target_pairs={{0,8},{8,0},{16,24},{24,16},{1,9},{9,1},{17,25},{25,17},{2,10},{10... | collective-permute-start | bytes 24584 | tf_op jit(solution)/shard_map/ppermute | solution.py:273
  251.6 4.6 %collective-permute-start.16 = (f32[16,128]{1,0:T(8,128)S(1)}, f32[16,128]{1,0:T(8,128)S(1)}, u32[]{:S(2)}, u32[]{:S(2)}) collective-permute-start(f32[16,128]{1,0:T(8,128)S(1)} %fusion.2), channel_id=1, source_target_pairs={{0,16},{8,24},{16,0},{24,8},{1,17},{9,25},{17,1},{25,9},{2,18},{10... | collective-permute-start | bytes 24584 | tf_op jit(solution)/shard_map/ppermute | solution.py:273
  256.2 1.2 collective-permute-start.17
  257.3 3.7 %collective-permute-start.18 = (f32[16,128]{1,0:T(8,128)S(1)}, f32[16,128]{1,0:T(8,128)S(1)}, u32[]{:S(2)}, u32[]{:S(2)}) collective-permute-start(f32[16,128]{1,0:T(8,128)S(1)} %add.147), channel_id=1, source_target_pairs={{0,2},{1,3},{2,0},{3,1},{4,6},{5,7},{6,4},{7,5},{8,10},{9,11},{10,... | collective-permute-start | bytes 24584 | tf_op jit(solution)/shard_map/ppermute | solution.py:273
  261.0 3.7 %collective-permute-start.19 = (f32[16,128]{1,0:T(8,128)S(1)}, f32[16,128]{1,0:T(8,128)S(1)}, u32[]{:S(2)}, u32[]{:S(2)}) collective-permute-start(f32[16,128]{1,0:T(8,128)S(1)} %add.148), channel_id=1, source_target_pairs={{0,4},{1,5},{2,6},{3,7},{4,0},{5,1},{6,2},{7,3},{8,12},{9,13},{10,... | collective-permute-start | bytes 24584 | tf_op jit(solution)/shard_map/ppermute | solution.py:273
  269.8 1.2 copy-start
  271.1 1.0 copy-start.1
  272.1 1.0 copy-start.2
  319.4 3.7 %collective-permute-start.23 = (f32[8,128]{1,0:T(8,128)S(1)}, f32[8,128]{1,0:T(8,128)S(1)}, u32[]{:S(2)}, u32[]{:S(2)}) collective-permute-start(f32[8,128]{1,0:T(8,128)S(1)} %broadcast_in_dim.7), channel_id=1, source_target_pairs={{0,8},{8,0},{16,24},{24,16},{1,9},{9,1},{17,25},{25,17},{2,10},{10... | collective-permute-start | bytes 12296 | tf_op jit(solution)/shard_map/ppermute | solution.py:273
  323.8 4.6 %collective-permute-start.24 = (f32[8,128]{1,0:T(8,128)S(1)}, f32[8,128]{1,0:T(8,128)S(1)}, u32[]{:S(2)}, u32[]{:S(2)}) collective-permute-start(f32[8,128]{1,0:T(8,128)S(1)} %broadcast_add_fusion), channel_id=1, source_target_pairs={{0,16},{8,24},{16,0},{24,8},{1,17},{9,25},{17,1},{25,9},{2,18},{10... | collective-permute-start | bytes 12296 | tf_op jit(solution)/shard_map/ppermute | solution.py:273
  329.0 1.2 collective-permute-start.25
  330.2 3.6 %collective-permute-start.26 = (f32[8,128]{1,0:T(8,128)S(1)}, f32[8,128]{1,0:T(8,128)S(1)}, u32[]{:S(2)}, u32[]{:S(2)}) collective-permute-start(f32[8,128]{1,0:T(8,128)S(1)} %add.156), channel_id=1, source_target_pairs={{0,2},{1,3},{2,0},{3,1},{4,6},{5,7},{6,4},{7,5},{8,10},{9,11},{10,... | collective-permute-start | bytes 12296 | tf_op jit(solution)/shard_map/ppermute | solution.py:273
  333.8 3.6 %collective-permute-start.27 = (f32[8,128]{1,0:T(8,128)S(1)}, f32[8,128]{1,0:T(8,128)S(1)}, u32[]{:S(2)}, u32[]{:S(2)}) collective-permute-start(f32[8,128]{1,0:T(8,128)S(1)} %add.157), channel_id=1, source_target_pairs={{0,4},{1,5},{2,6},{3,7},{4,0},{5,1},{6,2},{7,3},{8,12},{9,13},{10,... | collective-permute-start | bytes 12296 | tf_op jit(solution)/shard_map/ppermute | solution.py:273
Sparse Core Ops, SparseCore 0:
  27.3 79.1 reduce-scatter.1
  127.1 60.4 all-gather.2

commit v2 on v0

v2 whole, which is shorter than its diff:
```python
import functools

import jax
import jax.numpy as jnp
from jax import lax
from jax.experimental import pallas as pl
from jax.experimental.pallas import tpu as pltpu
from jax.sharding import PartitionSpec as P

F32 = jnp.float32
BF16 = jnp.bfloat16
VMEM_BYTES = 48 * 1024 * 1024
COST_SHARE = 0.3


def cost(macs):
    return pl.CostEstimate(
        flops=int(2 * COST_SHARE * macs), bytes_accessed=1024, transcendentals=0
    )


def params(sem_count, vmem_bytes=VMEM_BYTES):
    return pltpu.CompilerParams(
        dimension_semantics=("arbitrary",) * sem_count, vmem_limit_bytes=vmem_bytes
    )


def after(value, *earlier):
    return lax.optimization_barrier((value,) + earlier)[0]


def in_hbm(value):
    return pltpu.with_memory_space_constraint(value, pltpu.HBM)


def halves(value):
    high = value.astype(BF16)
    return high, (value - high.astype(F32)).astype(BF16)


def dot(a, b, dims=((1,), (0,))):
    return lax.dot_general(a, b, (dims, ((), ())), preferred_element_type=F32)


def rights_kernel(bit_ref, x_ref, r_ref, core_ref, sent_ref, kept_ref, square_ref):
    summed = dot(x_ref[...], r_ref[...], ((1,), (1,)))
    pairs = sent_ref.shape[0]
    share, p = core_ref.shape[1:]
    each = sent_ref.shape[1] - share
    upper = bit_ref[0] == 1
    for source, span in (
        (summed.reshape(pairs, 2, each, p), slice(0, each)),
        (core_ref[...].reshape(pairs, 2, share, p), slice(each, each + share)),
    ):
        kept_ref[:, span] = jnp.where(upper, source[:, 1], source[:, 0])
        sent_ref[:, span] = jnp.where(upper, source[:, 0], source[:, 1])
    wide = x_ref[...].astype(F32)
    square = jnp.sum(wide * wide, axis=0, keepdims=True)

    @pl.when(pl.program_id(0) == 0)
    def _():
        square_ref[...] = square

    @pl.when(pl.program_id(0) > 0)
    def _():
        square_ref[...] += square


def rights(x, r, core, bit, part, parts, groups, block):
    rows, cols = x.shape
    p = r.shape[0]
    each = rows // (parts * groups)
    share = p // (parts * groups)
    block = min(block, rows // parts)
    pairs = block // each // 2
    steps = rows // parts // block
    half = jax.ShapeDtypeStruct((groups // 2, each + share, p), F32)
    out_spec = pl.BlockSpec((pairs, each + share, p), lambda i: (i, 0, 0))
    return pl.pallas_call(
        rights_kernel,
        out_shape=[half, half, jax.ShapeDtypeStruct((1, cols), F32)],
        grid=(steps,),
        in_specs=[
            pl.BlockSpec(memory_space=pltpu.SMEM),
            pl.BlockSpec((block, cols), lambda i: (part * steps + i, 0)),
            pl.BlockSpec((p, cols), lambda i: (0, 0)),
            pl.BlockSpec((2 * pairs, share, p), lambda i: (part * steps + i, 0, 0)),
        ],
        out_specs=[out_spec, out_spec, pl.BlockSpec((1, cols), lambda i: (0, 0))],
        compiler_params=params(1),
        cost_estimate=cost(rows // parts * cols * p),
        name="right_products",
    )(bit, in_hbm(x), in_hbm(r), core.reshape(parts * groups, share, p))


def core_kernel(t_ref, r_ref, out_ref):
    right = r_ref[...]
    high, low = halves(t_ref[...])
    part = dot(high, right, ((1,), (1,))) + dot(low, right, ((1,), (1,)))

    @pl.when(pl.program_id(0) == 0)
    def _():
        out_ref[...] = part

    @pl.when(pl.program_id(0) > 0)
    def _():
        out_ref[...] += part


def core_products(t, r):
    count, cols = t.shape
    p = r.shape[0]
    width = min(1024, cols)
    return pl.pallas_call(
        core_kernel,
        out_shape=jax.ShapeDtypeStruct((count, p), F32),
        grid=(cols // width,),
        in_specs=[
            pl.BlockSpec((count, width), lambda i: (0, i)),
            pl.BlockSpec((p, width), lambda i: (0, i)),
        ],
        out_specs=pl.BlockSpec((count, p), lambda i: (0, 0)),
        compiler_params=params(1),
        cost_estimate=cost(2 * count * p * cols),
        name="core_products",
    )(in_hbm(t), in_hbm(r))


def lefts_kernel(l_ref, x_ref, out_ref):
    out_ref[...] = dot(l_ref[...], x_ref[...])


def lefts(l, x, unit):
    p, rows = l.shape
    cols = x.shape[1]
    return pl.pallas_call(
        lefts_kernel,
        out_shape=jax.ShapeDtypeStruct((p, cols), F32),
        grid=(cols // unit,),
        in_specs=[
            pl.BlockSpec((p, rows), lambda i: (0, 0)),
            pl.BlockSpec((rows, unit), lambda i: (0, i)),
        ],
        out_specs=pl.BlockSpec((p, unit), lambda i: (0, i)),
        compiler_params=params(1),
        cost_estimate=cost(p * rows * cols),
        name="left_products",
    )(in_hbm(l), in_hbm(x))


def mask_kernel(steps, col_start, rows_ref, cols_ref, x_ref, sums_ref, acc):
    step = pl.program_id(0)
    block, width = x_ref.shape
    queries = acc.shape[0]

    @pl.when(step == 0)
    def _():
        acc[...] = jnp.zeros_like(acc)

    values = x_ref[...]
    at = lax.broadcasted_iota(jnp.int32, (queries, block), 1) + step * block
    inside = (at >= rows_ref[:, 0:1]) & (at < rows_ref[:, 1:2])
    acc[...] += dot(inside.astype(F32).astype(BF16), values)

    @pl.when(step == steps - 1)
    def _():
        place = lax.broadcasted_iota(jnp.int32, (queries, width), 1) + col_start
        keep = (place >= cols_ref[:, 0:1]) & (place < cols_ref[:, 1:2])
        sums_ref[...] = jnp.sum(jnp.where(keep, acc[...], 0.0), axis=1, keepdims=True)


def mask_sums(x, row_bounds, col_bounds, start, width, block):
    rows = x.shape[0]
    queries = row_bounds.shape[0]
    steps = rows // block
    return pl.pallas_call(
        functools.partial(mask_kernel, steps, start),
        out_shape=jax.ShapeDtypeStruct((queries, 1), F32),
        grid=(steps,),
        in_specs=[
            pl.BlockSpec((queries, 2), lambda i: (0, 0)),
            pl.BlockSpec((queries, 2), lambda i: (0, 0)),
            pl.BlockSpec((block, width), lambda i: (i, start // width)),
        ],
        out_specs=pl.BlockSpec((queries, 1), lambda i: (0, 0)),
        scratch_shapes=[pltpu.VMEM((queries, width), F32)],
        compiler_params=params(1),
        cost_estimate=cost(queries * rows * width),
        name="interval_sums",
    )(row_bounds, col_bounds, in_hbm(x))


def core_spread_kernel(core_ref, r_ref, out_ref):
    high, low = halves(core_ref[...])
    right = r_ref[...]
    out_ref[...] = dot(high, right) + dot(low, right)


def core_spread(core, r):
    p, cols = r.shape
    width = min(512, cols)
    return pl.pallas_call(
        core_spread_kernel,
        out_shape=jax.ShapeDtypeStruct((p, cols), F32),
        grid=(cols // width,),
        in_specs=[
            pl.BlockSpec((p, p), lambda i: (0, 0)),
            pl.BlockSpec((p, width), lambda i: (0, i)),
        ],
        out_specs=pl.BlockSpec((p, width), lambda i: (0, i)),
        compiler_params=params(1),
        cost_estimate=cost(2 * p * p * cols),
        name="core_spread",
    )(core, in_hbm(r))


def finish_kernel(groups, bit_ref, scale_ref, x_ref, *refs):
    s_refs = refs[:4]
    lt_ref, add_ref, r_ref, t_ref, out_ref, sum_ref, both, twice = refs[4:]
    p, cols = r_ref.shape
    each = s_refs[0].shape[1]
    i = pl.program_id(0)
    width = min(512, cols)

    @pl.when(i == 0)
    def _():
        high, low = halves(t_ref[...] + add_ref[...])
        twice[:p, :] = r_ref[...]
        twice[p : 2 * p, :] = r_ref[...]
        twice[2 * p : 3 * p, :] = high
        twice[3 * p :, :] = low
        sum_ref[...] = jnp.zeros_like(sum_ref)

    upper = bit_ref[0] == 1
    early = i < groups // 2
    mine = jnp.where(early, s_refs[0][0], s_refs[2][0])
    got = jnp.where(early, s_refs[1][0], s_refs[3][0])
    for k, rows in enumerate((jnp.where(upper, got, mine), jnp.where(upper, mine, got))):
        high, low = halves(rows)
        both[k * each : (k + 1) * each, :p] = high
        both[k * each : (k + 1) * each, p : 2 * p] = low
    left = lt_ref[...]
    both[:, 2 * p : 3 * p] = left
    both[:, 3 * p :] = left
    for at in range(0, cols, width):
        span = slice(at, at + width)
        change = dot(both[...], twice[:, span])
        left_over = scale_ref[0] * x_ref[:, span].astype(F32) - scale_ref[1] * change
        out_ref[:, span] = left_over
        sum_ref[:, span] += jnp.sum(left_over * left_over, axis=0, keepdims=True)


def finish(bit, scales, x, s_parts, lt, add, r, t, groups):
    rows, cols = x.shape
    p = r.shape[0]
    each = rows // (2 * groups)
    whole = pl.BlockSpec((p, cols), lambda i: (0, 0), pipeline_mode=pl.Buffered(1))
    first = pl.BlockSpec((1, each, p), lambda i: (jnp.minimum(i, groups // 2 - 1), 0, 0))
    second = pl.BlockSpec((1, each, p), lambda i: (jnp.maximum(i - groups // 2, 0), 0, 0))
    return pl.pallas_call(
        functools.partial(finish_kernel, groups),
        out_shape=[
            jax.ShapeDtypeStruct((rows, cols), F32),
            jax.ShapeDtypeStruct((1, cols), F32),
        ],
        grid=(groups,),
        in_specs=[
            pl.BlockSpec(memory_space=pltpu.SMEM),
            pl.BlockSpec(memory_space=pltpu.SMEM),
            pl.BlockSpec((2 * each, cols), lambda i: (i, 0)),
            first,
            first,
            second,
            second,
            pl.BlockSpec((2 * each, p), lambda i: (i, 0)),
            whole,
            whole,
            whole,
        ],
        out_specs=[
            pl.BlockSpec((2 * each, cols), lambda i: (i, 0)),
            pl.BlockSpec((1, cols), lambda i: (0, 0)),
        ],
        scratch_shapes=[
            pltpu.VMEM((2 * each, 4 * p), BF16),
            pltpu.VMEM((4 * p, cols), BF16),
        ],
        compiler_params=params(1),
        cost_estimate=cost(4 * p * rows * cols),
        name="finish_residual",
    )(bit, scales, in_hbm(x), *s_parts, in_hbm(lt), add, in_hbm(r), t)


def swap(value, axis, mask, size):
    return lax.ppermute(value, axis, [(i, i ^ mask) for i in range(size)])


def powers(size):
    masks = []
    mask = 1
    while mask < size:
        masks.append(mask)
        mask *= 2
    return masks


def fold(value, axis, size):
    for mask in powers(size):
        value = value + swap(value, axis, mask, size)
    return value


def shards(n_row, n_col, x, theta_left, theta_right, query_rows, query_cols):
    rows, cols = x.shape
    p = theta_left.shape[0]
    queries = query_rows.shape[0]
    z = lax.axis_index("row")
    j = lax.axis_index("col")
    tall = min(1024, rows)
    streams = 2
    each = rows // (streams * n_col)
    share = p // (streams * n_col)
    tail = each + share
    masks = powers(n_col)
    orders = [masks, masks[:1] + masks[:0:-1]]
    bits = {mask: (j // mask) % 2 for mask in masks}
    core_bit = bits[masks[0]].astype(jnp.int32).reshape(1)
    row_bounds = jnp.clip(query_rows - z * rows, 0, rows)
    col_bounds = query_cols - j * cols

    token = theta_left

    def run(work, first, *others):
        nonlocal token
        out = work(after(first, token), *others)
        token = jax.tree.leaves(out)[0]
        return out

    def pick(value, axis, at):
        return lax.dynamic_index_in_dim(value, at, axis, False)

    partial_left = run(lambda l: lefts(l, x, min(512, cols)), theta_left)
    own_left = lax.psum_scatter(partial_left, "row", scatter_dimension=0, tiled=True)

    intervals = []
    squares = jnp.zeros((), F32)
    mask_width = cols // 4
    mask_starts = list(range(0, cols, mask_width))

    def mask_piece():
        if mask_starts:
            start = mask_starts.pop(0)
            intervals.append(
                run(lambda v: mask_sums(x, v, col_bounds, start, mask_width, tall), row_bounds)
            )

    terms = [None] * streams
    flight = [None] * streams
    left = [list(reversed(masks[1:])) for _ in range(streams)]

    def scatter_start(s, level):
        mask = orders[s][level]
        axis = left[s].index(mask)
        left[s].remove(mask)
        sent = run(
            lambda v, *rest: sum(
                (pick(term, axis, 1 - bits[mask]) for term in rest),
                pick(v, axis, 1 - bits[mask]),
            ),
            *terms[s],
        )
        terms[s] = [pick(term, axis, bits[mask]) for term in terms[s]]
        flight[s] = swap(sent, "col", mask, n_col)

    def add_start(s, level):
        terms[s].append(flight[s])
        scatter_start(s, level)

    def add_start(s, level):
        terms[s].append(flight[s])
        scatter_start(s, level)

    shape = (2,) * (len(masks) - 1)
    core = run(lambda t: core_products(t, theta_right), partial_left)
    for s in range(streams):
        sent, kept, square = run(
            lambda v: rights(x, v, core, core_bit, s, streams, n_col, tall), theta_right
        )
        squares = squares + jnp.sum(square)
        flight[s] = swap(sent, "col", masks[0], n_col).reshape(*shape, tail, p)
        terms[s] = [kept.reshape(*shape, tail, p)]
    for level in range(1, len(masks)):
        for s in range(streams):
            add_start(s, level)
        if level == 1:
            mask_piece()
            mask_piece()
    parts = []
    for s in range(streams):
        got = flight[s]
        parts.append(run(lambda v, *rest: sum(rest, v) + got, *terms[s]))

    core = jnp.concatenate([part[each:] for part in parts])
    local = [
        lambda v: sum(jnp.sum(part[:each] * part[:each]) for part in (v, parts[1])),
        lambda v: jnp.sum(own_left * own_left) + 0.0 * v[0, 0],
    ]
    total = 0.0
    for mask in powers(n_row):
        got = swap(core, "row", mask, n_row)
        if local:
            total = total + run(local.pop(0), parts[0])
        core = run(lambda v: v + got, core)
    own_left = run(lambda v: v, own_left)
    whole_left = lax.all_gather(own_left, "row", axis=0, tiled=True)
    core_square = jnp.sum(core * core)

    def widen_start(s, level):
        flight[s] = swap(parts[s], "col", orders[s][level], n_col)

    def widen(s, level):
        mask = orders[s][level]
        held = [m for m in masks if m in orders[s][level + 1 :]]
        axis = sum(1 for m in held if m > mask)
        dims = (2,) * len(held)
        other = flight[s].reshape(*dims, tail, p)
        parts[s] = run(
            lambda v: jnp.where(
                bits[mask] == 1,
                jnp.stack([other, v], axis=axis),
                jnp.stack([v, other], axis=axis),
            ),
            parts[s].reshape(*dims, tail, p),
        ).reshape(-1, tail, p)
        widen_start(s, level - 1)

    top = len(masks) - 1
    for s in range(streams):
        rows_of = jnp.concatenate([parts[s][:each], core[s * share : (s + 1) * share]])
        parts[s] = run(lambda v: v, rows_of)
        widen_start(s, top)
    sums = jnp.repeat(jnp.stack([squares, total + core_square / n_row]), 4)[:, None]
    sums = sums + jnp.zeros((1, 128), F32)
    sum_hops = [("row", m, n_row) for m in powers(n_row)] + [("col", m, n_col) for m in masks]
    sum_flight = None

    def sum_start():
        nonlocal sum_flight
        if sum_hops:
            axis, mask, size = sum_hops[0]
            sum_flight = swap(sums, axis, mask, size)

    def sum_step():
        nonlocal sums
        if sum_hops:
            sum_hops.pop(0)
            got = sum_flight
            sums = run(lambda v: v + got, sums)
            sum_start()

    sum_start()
    mask_piece()
    for level in range(top, 0, -1):
        sum_step()
        for s in range(streams):
            widen(s, level)
        mask_piece()
    while mask_starts:
        mask_piece()
    while sum_hops:
        sum_step()
    packed = sums

    pieces = []
    for s in range(streams):
        mine, other = (v.reshape(-1, tail, p)[:, each:] for v in (parts[s], flight[s]))
        pieces.append(
            jnp.where(
                bits[masks[0]] == 1,
                jnp.stack([other, mine], axis=1),
                jnp.stack([mine, other], axis=1),
            )
        )
    core = run(lambda *v: jnp.stack(v).reshape(p, p), *pieces)
    lt = run(lambda v: v.T, theta_left)
    core_add = run(lambda v: core_spread(v, theta_right), core)

    start_norm = packed[0, 0]
    extra = packed[4, 0]
    curvature = start_norm + extra
    alpha = start_norm / curvature

    residual, square = finish(
        core_bit,
        jnp.stack([extra / curvature, alpha]),
        x,
        [v.reshape(-1, tail, p) for s in range(streams) for v in (parts[s], flight[s])],
        lt,
        core_add,
        theta_right,
        whole_left,
        n_col,
    )
    lines = queries // 128
    last = jnp.concatenate(
        [sum(intervals).reshape(lines, 128), jnp.full((8, 128), jnp.sum(square))]
    )
    last = fold(fold(last, "row", n_row), "col", n_col)
    step_ratio = (last[lines, 0] / start_norm).reshape(1)
    low_row, high_row = query_rows[:, 0], query_rows[:, 1]
    low_col, high_col = query_cols[:, 0], query_cols[:, 1]
    area = (high_row - low_row).astype(F32) * (high_col - low_col).astype(F32)
    answers = alpha * last[:lines].reshape(queries) / jnp.sqrt(area)
    return (residual, step_ratio, answers)


def solution(mesh):
    return jax.shard_map(
        functools.partial(shards, mesh.shape["row"], mesh.shape["col"]),
        mesh=mesh,
        in_specs=(P("row", "col"), P(None, "row"), P(None, "col"), P(), P()),
        out_specs=(P("row", "col"), P(), P()),
        check_vma=False,
    )
```

time: 1050 us -> 274 us (0.26)
  local copies, waits for them, and re-layouts: 304 us -> 21.6 us
  waiting for transfers between devices: 281 us -> 51.3 us
  matrix products: 217 us -> 0 us
  Pallas kernels: 0 us -> 118 us
  blocking collectives: 100 us -> 0 us
  other arithmetic: 119 us -> 29.8 us
  starting transfers between devices: 0.08 us -> 28.2 us
    psum x2 -> x0, waiting for transfers between devices: 281 us -> none  [the longest x1 152 us: shards(): summed_left = lax.psum(partial_left, 'row')]
    dot_general x6 -> x0, matrix products: 217 us -> none  [the longest x1 59.3 us: shards(): jnp.dot(left_wide, middle, precision=highest, preferred_element_type=jnp....]
    gather x4 -> x0, local copies, waits for them, and re-layouts: 156 us -> none  [corner_value(): return jnp.where(inside, jnp.take(flat_prefix, position_flat), 0.0)]
    pallas_call x0 -> x10, Pallas kernels: none -> 118 us  [the longest x1 46.6 us: finish(): pl.pallas_call(functools.partial(finish_kernel, groups), out_shape=[jax.S...]
    unnamed x72 -> x33, local copies, waits for them, and re-layouts: 109 us -> 8.98 us
    psum x2 -> x0, blocking collectives: 77.1 us -> none  [the longest x1 40 us: shards(): start_norm = lax.psum(jnp.sum(start_field * start_field), ('row', 'col'))]
    add x5 -> x18, other arithmetic: 60.4 us -> 13.3 us  [the longest x4 8.16 us: scatter_start(): sum((pick(term, axis, 1 - bits[mask]) for term in rest), pick(v, axis, 1...]
    ppermute x0 -> x24, waiting for transfers between devices: none -> 46.8 us  [swap(): return lax.ppermute(value, axis, [(i, i ^ mask) for i in range(size)])]
  transfers between devices with their start and end apart: 2 -> 26, of which waited for: 2 -> 15; matrix products, arithmetic and copies ran while one was open for 0% -> 15% of each run, Pallas kernels for 0% -> 21%
where the time goes in v2:
time: 274 us; the launch traced here: 273 us
  Pallas kernels  118 us (43%)
  waiting for transfers between devices  51.3 us (19%)
  other arithmetic  29.8 us (11%)
  starting transfers between devices  28.2 us (10%)
  between operations  24.2 us (9%)
  local copies, waits for them, and re-layouts  21.6 us (8%)
    ppermute x24, waiting for transfers between devices, swap(): return lax.ppermute(value, axis, [(i, i ^ mask) for i in range(size)])  46.8 us
    pallas_call x1, Pallas kernels, finish(): pl.pallas_call(functools.partial(finish_kernel, groups), out_shape=[jax.S...  46.6 us
    pallas_call x4, Pallas kernels, mask_sums(): pl.pallas_call(functools.partial(mask_kernel, steps, start), out_shape=ja...  31.5 us
    ppermute x24, starting transfers between devices, swap(): return lax.ppermute(value, axis, [(i, i ^ mask) for i in range(size)])  28.2 us
    pallas_call x2, Pallas kernels, rights(): pl.pallas_call(rights_kernel, out_shape=[half, half, jax.ShapeDtypeStruct...  17.8 us
    pallas_call x1, Pallas kernels, lefts(): pl.pallas_call(lefts_kernel, out_shape=jax.ShapeDtypeStruct((p, cols), F3...  13.1 us
    unnamed x33, local copies, waits for them, and re-layouts  8.98 us
    add x4, other arithmetic, scatter_start(): sum((pick(term, axis, 1 - bits[mask]) for term in rest), pick(v, axis, 1...  8.16 us
  transfers between devices with their start and end apart: 26, of which 15 were waited for; matrix products, arithmetic and copies ran while one was open for 15% of the time, Pallas kernels for 21%

profile of v2, /device:TPU:0, one launch (start us, length us, event | category | flops | bytes accessed | tf_op | source)
XLA Modules:
  0.0 273.2 jit_solution(17481595543756707073)
XLA Ops:
  7.2 13.1 %left_products.1.t_ref = f32[512,2048]{1,0:T(8,128)S(1)} custom-call(bf16[512,4096]{1,0:T(8,128)(2,1)} %l_ref, bf16[4096,2048]{1,0:T(8,128)(2,1)} %x_ref.15), custom_call_target="tpu_custom_call" | custom-call | flops 2576980480 | bytes 1024 | tf_op jit(solution)/shard_map/left_products/pallas_call | solution.py:136
  20.3 2.0 copy-done
  22.4 4.6 %core_products.1 = f32[512,512]{1,0:T(8,128)S(1)} custom-call(f32[512,2048]{1,0:T(8,128)} %copy-done, bf16[512,2048]{1,0:T(8,128)(2,1)} %refs_6_.1), custom_call_target="tpu_custom_call" | custom-call | flops 644245120 | bytes 1024 | tf_op jit(solution)/shard_map/core_products/pallas_call | solution.py:114
  27.0 8.9 %right_products.2 = (f32[4,288,512]{2,1,0:T(8,128)}, f32[4,288,512]{2,1,0:T(8,128)S(1)}, f32[1,2048]{1,0:T(1,128)S(1)}) custom-call(s32[1]{0:T(128)} %bitcast.bit_ref, bf16[4096,2048]{1,0:T(8,128)(2,1)} %x_ref.15, bf16[512,2048]{1,0:T(8,128)(2,1)} %refs_6_.1, f32[16,32,512]{2,1,0:T(8,128)S(1)} %bitcast.89), custom_call_target="tpu_custom_call" | custom-call | flops 1288490240 | bytes 1024 | tf_op jit(solution)/shard_map/right_products/pallas_call | solution.py:79
  36.3 8.9 %right_products.3 = (f32[4,288,512]{2,1,0:T(8,128)}, f32[4,288,512]{2,1,0:T(8,128)S(1)}, f32[1,2048]{1,0:T(1,128)S(1)}) custom-call(s32[1]{0:T(128)} %bitcast.bit_ref, bf16[4096,2048]{1,0:T(8,128)(2,1)} %x_ref.15, bf16[512,2048]{1,0:T(8,128)(2,1)} %refs_6_.1, f32[16,32,512]{2,1,0:T(8,128)S(1)} %bitcast.90), custom_call_target="tpu_custom_call" | custom-call | flops 1288490240 | bytes 1024 | tf_op jit(solution)/shard_map/right_products/pallas_call | solution.py:79
  45.3 1.4 copy-done.2
  46.7 2.7 add_bitcast_fusion.1
  49.4 3.0 %collective-permute-start.2 = (f32[2,288,512]{2,1,0:T(8,128)}, f32[2,288,512]{2,1,0:T(8,128)}, u32[]{:S(2)}, u32[]{:S(2)}) collective-permute-start(f32[2,288,512]{2,1,0:T(8,128)} %add_bitcast_fusion.1), channel_id=1, source_target_pairs={{0,2},{1,3},{2,0},{3,1},{4,6},{5,7},{6,4},{7,5},{8,10},{9,11},{10,... | collective-permute-start | bytes 3538952 | tf_op jit(solution)/shard_map/ppermute | solution.py:295
  52.4 2.6 add_bitcast_fusion
  55.1 1.8 collective-permute-start.3
  57.2 1.0 copy.18
  58.4 0.9 copy-done.12
  59.3 7.8 %interval_sums.4 = f32[1024,1]{1,0:T(8,128)S(1)} custom-call(s32[1024,2]{1,0:T(8,128)S(1)} %broadcast_clamp_fusion.rows_ref, s32[1024,2]{1,0:T(8,128)S(1)} %broadcast_subtract_fusion.cols_ref, bf16[4096,2048]{1,0:T(8,128)(2,1)} %x_ref.15), custom_call_target="tpu_custom_call" | custom-call | flops 1288490240 | bytes 1024 | tf_op jit(solution)/shard_map/interval_sums/pallas_call | solution.py:176
  67.1 8.1 %interval_sums.5 = f32[1024,1]{1,0:T(8,128)S(1)} custom-call(s32[1024,2]{1,0:T(8,128)S(1)} %broadcast_clamp_fusion.rows_ref, s32[1024,2]{1,0:T(8,128)S(1)} %broadcast_subtract_fusion.cols_ref, bf16[4096,2048]{1,0:T(8,128)(2,1)} %x_ref.15), custom_call_target="tpu_custom_call" | custom-call | flops 1288490240 | bytes 1024 | tf_op jit(solution)/shard_map/interval_sums/pallas_call | solution.py:176
  75.3 3.6 %collective-permute-done.2 = f32[2,288,512]{2,1,0:T(8,128)} collective-permute-done((f32[2,288,512]{2,1,0:T(8,128)}, f32[2,288,512]{2,1,0:T(8,128)}, u32[]{:S(2)}, u32[]{:S(2)}) %collective-permute-start.2) | collective-permute-done | bytes 1179680 | tf_op jit(solution)/shard_map/ppermute | solution.py:295
  78.9 1.4 bitcast_add_fusion.6
  80.3 1.8 collective-permute-start.4
  82.2 1.9 collective-permute-done.3
  84.2 1.4 bitcast_add_fusion.4
  85.6 1.9 collective-permute-start.5
  87.6 8.6 %collective-permute-done.4 = f32[288,512]{1,0:T(8,128)S(1)} collective-permute-done((f32[288,512]{1,0:T(8,128)S(1)}, f32[288,512]{1,0:T(8,128)S(1)}, u32[]{:S(2)}, u32[]{:S(2)}) %collective-permute-start.4) | collective-permute-done | bytes 589856 | tf_op jit(solution)/shard_map/ppermute | solution.py:295
  96.3 1.5 fusion.1
  97.8 2.3 collective-permute-done.5
  100.1 1.5 fusion
  101.6 1.8 collective-permute-start.6
  103.4 1.5 fusion.4
  104.9 0.7 multiply_reduce_fusion.2
  107.0 2.9 %collective-permute-start.7 = (f32[64,512]{1,0:T(8,128)S(1)}, f32[64,512]{1,0:T(8,128)S(1)}, u32[]{:S(2)}, u32[]{:S(2)}) collective-permute-start(f32[64,512]{1,0:T(8,128)S(1)} %add.209), channel_id=1, source_target_pairs={{0,16},{8,24},{16,0},{24,8},{1,17},{9,25},{17,1},{25,9},{2,18},{10... | collective-permute-start | bytes 393224 | tf_op jit(solution)/shard_map/ppermute | solution.py:295
  111.1 2.1 multiply_reduce_fusion
  115.0 1.1 pad_maximum_fusion.1
  116.1 1.6 collective-permute-start.10
  120.3 1.6 collective-permute-start.9
  122.8 0.9 collective-permute-start.8
  123.7 7.9 %interval_sums.6 = f32[1024,1]{1,0:T(8,128)S(1)} custom-call(s32[1024,2]{1,0:T(8,128)S(1)} %broadcast_clamp_fusion.rows_ref, s32[1024,2]{1,0:T(8,128)S(1)} %broadcast_subtract_fusion.cols_ref, bf16[4096,2048]{1,0:T(8,128)(2,1)} %x_ref.15), custom_call_target="tpu_custom_call" | custom-call | flops 1288490240 | bytes 1024 | tf_op jit(solution)/shard_map/interval_sums/pallas_call | solution.py:176
  131.6 0.8 copy-done.9
  132.4 0.8 copy-done.13
  133.2 1.4 maximum_select_fusion.2
  135.2 1.4 maximum_select_fusion.3
  137.0 3.4 %collective-permute-start.11 = (f32[8,128]{1,0:T(8,128)S(1)}, f32[8,128]{1,0:T(8,128)S(1)}, u32[]{:S(2)}, u32[]{:S(2)}) collective-permute-start(f32[8,128]{1,0:T(8,128)S(1)} %add.216), channel_id=1, source_target_pairs={{0,16},{8,24},{16,0},{24,8},{1,17},{9,25},{17,1},{25,9},{2,18},{10... | collective-permute-start | bytes 12296 | tf_op jit(solution)/shard_map/ppermute | solution.py:295
  140.4 7.7 %interval_sums.7 = f32[1024,1]{1,0:T(8,128)S(1)} custom-call(s32[1024,2]{1,0:T(8,128)S(1)} %broadcast_clamp_fusion.rows_ref, s32[1024,2]{1,0:T(8,128)S(1)} %broadcast_subtract_fusion.cols_ref, bf16[4096,2048]{1,0:T(8,128)(2,1)} %x_ref.15), custom_call_target="tpu_custom_call" | custom-call | flops 1288490240 | bytes 1024 | tf_op jit(solution)/shard_map/interval_sums/pallas_call | solution.py:176
  148.2 10.2 %collective-permute-done.15 = f32[2,288,512]{2,1,0:T(8,128)} collective-permute-done((f32[2,288,512]{2,1,0:T(8,128)S(1)}, f32[2,288,512]{2,1,0:T(8,128)}, u32[]{:S(2)}, u32[]{:S(2)}) %collective-permute-start.15) | collective-permute-done | bytes 1179680 | tf_op jit(solution)/shard_map/ppermute | solution.py:295
  158.4 3.0 %maximum_select_fusion = f32[2,2,288,512]{3,2,1,0:T(8,128)S(1)} fusion(f32[2,1,288,512]{3,2,1,0:T(8,128)} %bitcast.99, f32[2,1,288,512]{3,2,1,0:T(8,128)} %bitcast.33, pred[]{:T(512)S(6)} %eq.16), kind=kLoop, calls=%fused_computation | loop fusion | flops 1769472 | bytes 4718593 | tf_op jit(solution)/shard_map/jit(_where)/select_n | solution.py:428
  161.5 1.7 maximum_select_fusion.1
  163.7 2.3 collective-permute-done.12
  166.0 0.8 collective-permute-start.13
  166.9 2.8 %collective-permute-done.13 = f32[8,128]{1,0:T(8,128)S(1)} collective-permute-done((f32[8,128]{1,0:T(8,128)S(1)}, f32[8,128]{1,0:T(8,128)S(1)}, u32[]{:S(2)}, u32[]{:S(2)}) %collective-permute-start.13) | collective-permute-done | bytes 4128 | tf_op jit(solution)/shard_map/ppermute | solution.py:295
  170.1 1.4 add_reduce_fusion
  171.6 1.7 collective-permute-done.14
  176.7 1.0 slice_bitcast_fusion
  177.6 1.0 slice_bitcast_fusion.3
  178.7 1.0 slice_bitcast_fusion.1
  179.9 6.5 %copy.20 = bf16[512,4096]{0,1:T(8,128)(2,1)} copy(bf16[512,4096]{1,0:T(8,128)(2,1)} %l_ref) | data formatting | bytes 8388608 | tf_op jit(solution)/shard_map/optimization_barrier | solution.py:29
  186.4 4.5 %core_spread.1.refs_5_ = f32[512,2048]{1,0:T(8,128)S(1)} custom-call(f32[512,512]{1,0:T(8,128)S(1)} %bitcast.91, bf16[512,2048]{1,0:T(8,128)(2,1)} %refs_6_.1), custom_call_target="tpu_custom_call" | custom-call | flops 644245120 | bytes 1024 | tf_op jit(solution)/shard_map/core_spread/pallas_call | solution.py:202
  190.9 2.0 copy-done.1
  192.9 4.5 %all-gather.2.cloned.1.call-done.refs_7_ = f32[512,2048]{1,0:T(8,128)} async-done(((f32[128,2048]{1,0:T(8,128)}), f32[512,2048]{1,0:T(8,128)}) %all-gather.2.cloned.1.call-update) | async-done | bytes 4194320 | tf_op jit(solution)/shard_map/all_gather | solution.py:415
  197.4 46.6 %finish_residual.1 = (f32[4096,2048]{1,0:T(8,128)}, f32[1,2048]{1,0:T(1,128)S(1)}) custom-call(s32[1]{0:T(128)} %bitcast.bit_ref, f32[2]{0:T(128)S(1)} %pad_maximum_fusion.5.scale_ref, bf16[4096,2048]{1,0:T(8,128)(2,1)} %x_ref.15, f32[4,288,512]{2,1,0:T(8,128)S(1)} %bitcast.88, f32[4,288,512]{2,1,0:T(8,128)} %collective-permute-done.16.refs_1_, ...), custom_call_target="tpu_custom_call" | custom-call | flops 10307921920 | bytes 1024 | tf_op jit(solution)/shard_map/finish_residual/pallas_call | solution.py:260
  245.4 3.6 %collective-permute-done.19 = f32[16,128]{1,0:T(8,128)S(1)} collective-permute-done((f32[16,128]{1,0:T(8,128)S(1)}, f32[16,128]{1,0:T(8,128)S(1)}, u32[]{:S(2)}, u32[]{:S(2)}) %collective-permute-start.19) | collective-permute-done | bytes 8224 | tf_op jit(solution)/shard_map/ppermute | solution.py:295
  249.7 0.9 collective-permute-start.20
  250.6 3.7 %collective-permute-done.20 = f32[16,128]{1,0:T(8,128)S(1)} collective-permute-done((f32[16,128]{1,0:T(8,128)S(1)}, f32[16,128]{1,0:T(8,128)S(1)}, u32[]{:S(2)}, u32[]{:S(2)}) %collective-permute-start.20) | collective-permute-done | bytes 8224 | tf_op jit(solution)/shard_map/ppermute | solution.py:295
  254.3 1.2 collective-permute-done.21
  255.5 1.5 collective-permute-start.22
  257.0 2.1 collective-permute-done.22
  259.1 1.5 collective-permute-start.23
  260.6 2.1 collective-permute-done.23
  (96 shorter events, 10.7 us)
Async XLA Ops:
  7.2 103.9 %reduce-scatter.2.cloned.1.call-start = ((), (), s32[]{:S(2)}) async-start(), calls=%async_computation.1 | async-start | bytes 5242880 | tf_op jit(solution)/shard_map/reduce_scatter | solution.py:343
  20.3 2.0 copy-start
  22.3 175.0 %all-gather.2.cloned.1.call-start = ((), (), s32[]{:S(2)}) async-start(), calls=%async_computation.2 | async-start | bytes 5242880 | tf_op jit(solution)/shard_map/all_gather | solution.py:415
  35.9 10.9 %collective-permute-start = (f32[4,288,512]{2,1,0:T(8,128)}, f32[4,288,512]{2,1,0:T(8,128)}, u32[]{:S(2)}, u32[]{:S(2)}) collective-permute-start(f32[4,288,512]{2,1,0:T(8,128)} %get-tuple-element.46), channel_id=1, source_target_pairs={{0,1},{1,0},{2,3},{3,2},{4,5},{5,4},{6,7},{7,6},{8,9},{9,8},{10,11... | collective-permute-start | bytes 7077896 | tf_op jit(solution)/shard_map/ppermute | solution.py:295
  45.3 1.4 copy-start.2
  46.7 5.8 %collective-permute-start.1 = (f32[4,288,512]{2,1,0:T(8,128)}, f32[4,288,512]{2,1,0:T(8,128)}, u32[]{:S(2)}, u32[]{:S(2)}) collective-permute-start(f32[4,288,512]{2,1,0:T(8,128)} %get-tuple-element.51), channel_id=1, source_target_pairs={{0,1},{1,0},{2,3},{3,2},{4,5},{5,4},{6,7},{7,6},{8,9},{9,8},{10,11... | collective-permute-start | bytes 7077896 | tf_op jit(solution)/shard_map/ppermute | solution.py:295
  46.7 5.7 %copy-start.3 = (f32[4,288,512]{2,1,0:T(8,128)S(1)}, f32[4,288,512]{2,1,0:T(8,128)}, u32[]{:S(2)}) copy-start(f32[4,288,512]{2,1,0:T(8,128)} %copy-done.2) | copy-start | bytes 7077892
  49.4 7.5 %copy-start.15 = (s32[1024,2]{0,1:T(2,128)S(1)}, s32[1024,2]{0,1:T(2,128)}, u32[]{:S(2)}) copy-start(s32[1024,2]{0,1:T(2,128)} %param.8) | copy-start | bytes 24580
  49.4 7.7 %copy-start.14 = (s32[1024,2]{0,1:T(2,128)S(1)}, s32[1024,2]{0,1:T(2,128)}, u32[]{:S(2)}) copy-start(s32[1024,2]{0,1:T(2,128)} %param.9) | copy-start | bytes 24580
  49.4 29.5 %collective-permute-start.2 = (f32[2,288,512]{2,1,0:T(8,128)}, f32[2,288,512]{2,1,0:T(8,128)}, u32[]{:S(2)}, u32[]{:S(2)}) collective-permute-start(f32[2,288,512]{2,1,0:T(8,128)} %add_bitcast_fusion.1), channel_id=1, source_target_pairs={{0,2},{1,3},{2,0},{3,1},{4,6},{5,7},{6,4},{7,5},{8,10},{9,11},{10,... | collective-permute-start | bytes 3538952 | tf_op jit(solution)/shard_map/ppermute | solution.py:295
  55.1 29.1 %collective-permute-start.3 = (f32[2,288,512]{2,1,0:T(8,128)}, f32[2,288,512]{2,1,0:T(8,128)}, u32[]{:S(2)}, u32[]{:S(2)}) collective-permute-start(f32[2,288,512]{2,1,0:T(8,128)} %add_bitcast_fusion), channel_id=1, source_target_pairs={{0,4},{1,5},{2,6},{3,7},{4,0},{5,1},{6,2},{7,3},{8,12},{9,13},{10,... | collective-permute-start | bytes 3538952 | tf_op jit(solution)/shard_map/ppermute | solution.py:295
  58.2 1.0 copy-start.12
  67.1 8.1 %copy-start.5 = (f32[1024,1]{1,0:T(8,128)}, f32[1024,1]{1,0:T(8,128)S(1)}, u32[]{:S(2)}) copy-start(f32[1024,1]{1,0:T(8,128)S(1)} %interval_sums.4) | copy-start | bytes 12292
  75.3 7.0 %copy-start.7 = (f32[1024,1]{1,0:T(8,128)}, f32[1024,1]{1,0:T(8,128)S(1)}, u32[]{:S(2)}) copy-start(f32[1024,1]{1,0:T(8,128)S(1)} %interval_sums.5) | copy-start | bytes 12292
  75.3 6.9 %copy-start.4 = (f32[4,288,512]{2,1,0:T(8,128)S(1)}, f32[4,288,512]{2,1,0:T(8,128)}, u32[]{:S(2)}) copy-start(f32[4,288,512]{2,1,0:T(8,128)} %copy-done.2) | copy-start | bytes 7077892
  80.3 15.9 %collective-permute-start.4 = (f32[288,512]{1,0:T(8,128)S(1)}, f32[288,512]{1,0:T(8,128)S(1)}, u32[]{:S(2)}, u32[]{:S(2)}) collective-permute-start(f32[288,512]{1,0:T(8,128)S(1)} %bitcast_add_fusion.6), channel_id=1, source_target_pairs={{0,4},{1,5},{2,6},{3,7},{4,0},{5,1},{6,2},{7,3},{8,12},{9,13},{10,... | collective-permute-start | bytes 1769480 | tf_op jit(solution)/shard_map/ppermute | solution.py:295
  85.6 14.5 %collective-permute-start.5 = (f32[288,512]{1,0:T(8,128)S(1)}, f32[288,512]{1,0:T(8,128)S(1)}, u32[]{:S(2)}, u32[]{:S(2)}) collective-permute-start(f32[288,512]{1,0:T(8,128)S(1)} %bitcast_add_fusion.4), channel_id=1, source_target_pairs={{0,2},{1,3},{2,0},{3,1},{4,6},{5,7},{6,4},{7,5},{8,10},{9,11},{10,... | collective-permute-start | bytes 1769480 | tf_op jit(solution)/shard_map/ppermute | solution.py:295
  101.6 5.3 %collective-permute-start.6 = (f32[64,512]{1,0:T(8,128)S(1)}, f32[64,512]{1,0:T(8,128)S(1)}, u32[]{:S(2)}, u32[]{:S(2)}) collective-permute-start(f32[64,512]{1,0:T(8,128)S(1)} %pad_maximum_fusion.3), channel_id=1, source_target_pairs={{0,8},{8,0},{16,24},{24,16},{1,9},{9,1},{17,25},{25,17},{2,10},{10... | collective-permute-start | bytes 393224 | tf_op jit(solution)/shard_map/ppermute | solution.py:295
  107.0 7.3 %collective-permute-start.7 = (f32[64,512]{1,0:T(8,128)S(1)}, f32[64,512]{1,0:T(8,128)S(1)}, u32[]{:S(2)}, u32[]{:S(2)}) collective-permute-start(f32[64,512]{1,0:T(8,128)S(1)} %add.209), channel_id=1, source_target_pairs={{0,16},{8,24},{16,0},{24,8},{1,17},{9,25},{17,1},{25,9},{2,18},{10... | collective-permute-start | bytes 393224 | tf_op jit(solution)/shard_map/ppermute | solution.py:295
  116.1 16.2 %collective-permute-start.10 = (f32[288,512]{1,0:T(8,128)S(1)}, f32[288,512]{1,0:T(8,128)S(1)}, u32[]{:S(2)}, u32[]{:S(2)}) collective-permute-start(f32[288,512]{1,0:T(8,128)S(1)} %get-tuple-element.69), channel_id=1, source_target_pairs={{0,4},{1,5},{2,6},{3,7},{4,0},{5,1},{6,2},{7,3},{8,12},{9,13},{10,... | collective-permute-start | bytes 1769480 | tf_op jit(solution)/shard_map/ppermute | solution.py:295
  120.3 14.9 %collective-permute-start.9 = (f32[288,512]{1,0:T(8,128)S(1)}, f32[288,512]{1,0:T(8,128)}, u32[]{:S(2)}, u32[]{:S(2)}) collective-permute-start(f32[288,512]{1,0:T(8,128)S(1)} %get-tuple-element.70), channel_id=1, source_target_pairs={{0,2},{1,3},{2,0},{3,1},{4,6},{5,7},{6,4},{7,5},{8,10},{9,11},{10,... | collective-permute-start | bytes 1769480 | tf_op jit(solution)/shard_map/ppermute | solution.py:295
  122.8 9.6 %collective-permute-start.8 = (f32[8,128]{1,0:T(8,128)S(1)}, f32[8,128]{1,0:T(8,128)S(1)}, u32[]{:S(2)}, u32[]{:S(2)}) collective-permute-start(f32[8,128]{1,0:T(8,128)S(1)} %add.215), channel_id=1, source_target_pairs={{0,8},{8,0},{16,24},{24,16},{1,9},{9,1},{17,25},{25,17},{2,10},{10... | collective-permute-start | bytes 12296 | tf_op jit(solution)/shard_map/ppermute | solution.py:295
  131.6 0.8 copy-start.9
  132.4 0.8 copy-start.13
  134.6 13.6 %copy-start.11 = (f32[2,288,512]{2,1,0:T(8,128)}, f32[2,288,512]{2,1,0:T(8,128)S(1)}, u32[]{:S(2)}) copy-start(f32[2,288,512]{2,1,0:T(8,128)S(1)} %maximum_select_fusion.2) | copy-start | bytes 3538948
  134.6 23.8 %collective-permute-start.15 = (f32[2,288,512]{2,1,0:T(8,128)S(1)}, f32[2,288,512]{2,1,0:T(8,128)}, u32[]{:S(2)}, u32[]{:S(2)}) collective-permute-start(f32[2,288,512]{2,1,0:T(8,128)S(1)} %maximum_select_fusion.2), channel_id=1, source_target_pairs={{0,2},{1,3},{2,0},{3,1},{4,6},{5,7},{6,4},{7,5},{8,10},{9,11},{10,... | collective-permute-start | bytes 3538952 | tf_op jit(solution)/shard_map/ppermute | solution.py:295
  136.6 24.9 %collective-permute-start.17 = (f32[2,288,512]{2,1,0:T(8,128)S(1)}, f32[2,288,512]{2,1,0:T(8,128)S(1)}, u32[]{:S(2)}, u32[]{:S(2)}) collective-permute-start(f32[2,288,512]{2,1,0:T(8,128)S(1)} %maximum_select_fusion.3), channel_id=1, source_target_pairs={{0,4},{1,5},{2,6},{3,7},{4,0},{5,1},{6,2},{7,3},{8,12},{9,13},{10,... | collective-permute-start | bytes 3538952 | tf_op jit(solution)/shard_map/ppermute | solution.py:295
  137.0 11.2 %collective-permute-start.11 = (f32[8,128]{1,0:T(8,128)S(1)}, f32[8,128]{1,0:T(8,128)S(1)}, u32[]{:S(2)}, u32[]{:S(2)}) collective-permute-start(f32[8,128]{1,0:T(8,128)S(1)} %add.216), channel_id=1, source_target_pairs={{0,16},{8,24},{16,0},{24,8},{1,17},{9,25},{17,1},{25,9},{2,18},{10... | collective-permute-start | bytes 12296 | tf_op jit(solution)/shard_map/ppermute | solution.py:295
  148.2 13.2 %copy-start.10 = (f32[1024,1]{1,0:T(8,128)}, f32[1024,1]{1,0:T(8,128)S(1)}, u32[]{:S(2)}) copy-start(f32[1024,1]{1,0:T(8,128)S(1)} %interval_sums.7) | copy-start | bytes 12292
  161.4 16.2 %collective-permute-start.16 = (f32[4,288,512]{2,1,0:T(8,128)S(1)}, f32[4,288,512]{2,1,0:T(8,128)}, u32[]{:S(2)}, u32[]{:S(2)}) collective-permute-start(f32[4,288,512]{2,1,0:T(8,128)S(1)} %bitcast.86), channel_id=1, source_target_pairs={{0,1},{1,0},{2,3},{3,2},{4,5},{5,4},{6,7},{7,6},{8,9},{9,8},{10,11... | collective-permute-start | bytes 7077896 | tf_op jit(solution)/shard_map/ppermute | solution.py:295
  161.5 8.6 %copy-start.6 = (f32[1024,1]{1,0:T(8,128)S(1)}, f32[1024,1]{1,0:T(8,128)}, u32[]{:S(2)}) copy-start(f32[1024,1]{1,0:T(8,128)} %copy-done.5) | copy-start | bytes 12292
  161.5 8.6 %copy-start.8 = (f32[1024,1]{1,0:T(8,128)S(1)}, f32[1024,1]{1,0:T(8,128)}, u32[]{:S(2)}) copy-start(f32[1024,1]{1,0:T(8,128)} %copy-done.7) | copy-start | bytes 12292
  163.2 15.5 %collective-permute-start.18 = (f32[4,288,512]{2,1,0:T(8,128)}, f32[4,288,512]{2,1,0:T(8,128)}, u32[]{:S(2)}, u32[]{:S(2)}) collective-permute-start(f32[4,288,512]{2,1,0:T(8,128)} %bitcast.38.refs_2_), channel_id=1, source_target_pairs={{0,1},{1,0},{2,3},{3,2},{4,5},{5,4},{6,7},{7,6},{8,9},{9,8},{10,11... | collective-permute-start | bytes 7077896 | tf_op jit(solution)/shard_map/ppermute | solution.py:295
  163.7 2.4 collective-permute-start.12
  166.0 3.6 %collective-permute-start.13 = (f32[8,128]{1,0:T(8,128)S(1)}, f32[8,128]{1,0:T(8,128)S(1)}, u32[]{:S(2)}, u32[]{:S(2)}) collective-permute-start(f32[8,128]{1,0:T(8,128)S(1)} %add.218), channel_id=1, source_target_pairs={{0,2},{1,3},{2,0},{3,1},{4,6},{5,7},{6,4},{7,5},{8,10},{9,11},{10,... | collective-permute-start | bytes 12296 | tf_op jit(solution)/shard_map/ppermute | solution.py:295
  169.7 3.6 %collective-permute-start.14 = (f32[8,128]{1,0:T(8,128)S(1)}, f32[8,128]{1,0:T(8,128)S(1)}, u32[]{:S(2)}, u32[]{:S(2)}) collective-permute-start(f32[8,128]{1,0:T(8,128)S(1)} %add.219), channel_id=1, source_target_pairs={{0,4},{1,5},{2,6},{3,7},{4,0},{5,1},{6,2},{7,3},{8,12},{9,13},{10,... | collective-permute-start | bytes 12296 | tf_op jit(solution)/shard_map/ppermute | solution.py:295
  190.9 2.0 copy-start.1
  245.3 3.7 %collective-permute-start.19 = (f32[16,128]{1,0:T(8,128)S(1)}, f32[16,128]{1,0:T(8,128)S(1)}, u32[]{:S(2)}, u32[]{:S(2)}) collective-permute-start(f32[16,128]{1,0:T(8,128)S(1)} %concatenate.29), channel_id=1, source_target_pairs={{0,8},{8,0},{16,24},{24,16},{1,9},{9,1},{17,25},{25,17},{2,10},{10... | collective-permute-start | bytes 24584 | tf_op jit(solution)/shard_map/ppermute | solution.py:295
  249.7 4.6 %collective-permute-start.20 = (f32[16,128]{1,0:T(8,128)S(1)}, f32[16,128]{1,0:T(8,128)S(1)}, u32[]{:S(2)}, u32[]{:S(2)}) collective-permute-start(f32[16,128]{1,0:T(8,128)S(1)} %pad_add_fusion), channel_id=1, source_target_pairs={{0,16},{8,24},{16,0},{24,8},{1,17},{9,25},{17,1},{25,9},{2,18},{10... | collective-permute-start | bytes 24584 | tf_op jit(solution)/shard_map/ppermute | solution.py:295
  254.3 1.2 collective-permute-start.21
  255.5 3.7 %collective-permute-start.22 = (f32[16,128]{1,0:T(8,128)S(1)}, f32[16,128]{1,0:T(8,128)S(1)}, u32[]{:S(2)}, u32[]{:S(2)}) collective-permute-start(f32[16,128]{1,0:T(8,128)S(1)} %add.227), channel_id=1, source_target_pairs={{0,2},{1,3},{2,0},{3,1},{4,6},{5,7},{6,4},{7,5},{8,10},{9,11},{10,... | collective-permute-start | bytes 24584 | tf_op jit(solution)/shard_map/ppermute | solution.py:295
  259.1 3.7 %collective-permute-start.23 = (f32[16,128]{1,0:T(8,128)S(1)}, f32[16,128]{1,0:T(8,128)S(1)}, u32[]{:S(2)}, u32[]{:S(2)}) collective-permute-start(f32[16,128]{1,0:T(8,128)S(1)} %add.228), channel_id=1, source_target_pairs={{0,4},{1,5},{2,6},{3,7},{4,0},{5,1},{6,2},{7,3},{8,12},{9,13},{10,... | collective-permute-start | bytes 24584 | tf_op jit(solution)/shard_map/ppermute | solution.py:295
Sparse Core Ops, SparseCore 0:
  22.5 79.4 reduce-scatter.1
  115.1 82.2 all-gather.1

commit v3 on v2

--- a/solution.py
+++ b/solution.py
@@ -9,6 +9,8 @@
 
 F32 = jnp.float32
 BF16 = jnp.bfloat16
+F8 = jnp.float8_e4m3fn
+F8_TOP = 128.0
 VMEM_BYTES = 48 * 1024 * 1024
 COST_SHARE = 0.3
 
@@ -93,8 +95,9 @@
     )(bit, in_hbm(x), in_hbm(r), core.reshape(parts * groups, share, p))
 
 
-def core_kernel(t_ref, r_ref, out_ref):
+def core_kernel(t_ref, r_ref, out_ref, most_ref):
     right = r_ref[...]
+    most_ref[...] = most(right)
     high, low = halves(t_ref[...])
     part = dot(high, right, ((1,), (1,))) + dot(low, right, ((1,), (1,)))
 
@@ -113,21 +116,35 @@
     width = min(1024, cols)
     return pl.pallas_call(
         core_kernel,
-        out_shape=jax.ShapeDtypeStruct((count, p), F32),
+        out_shape=[
+            jax.ShapeDtypeStruct((count, p), F32),
+            jax.ShapeDtypeStruct((1, cols), F32),
+        ],
         grid=(cols // width,),
         in_specs=[
             pl.BlockSpec((count, width), lambda i: (0, i)),
             pl.BlockSpec((p, width), lambda i: (0, i)),
         ],
-        out_specs=pl.BlockSpec((count, p), lambda i: (0, 0)),
+        out_specs=[
+            pl.BlockSpec((count, p), lambda i: (0, 0)),
+            pl.BlockSpec((1, width), lambda i: (0, i)),
+        ],
         compiler_params=params(1),
         cost_estimate=cost(2 * count * p * cols),
         name="core_products",
     )(in_hbm(t), in_hbm(r))
 
 
-def lefts_kernel(l_ref, x_ref, out_ref):
+def most(value):
+    return jnp.max(jnp.abs(value.astype(F32)), axis=0, keepdims=True)
+
+
+def lefts_kernel(l_ref, x_ref, out_ref, most_ref):
     out_ref[...] = dot(l_ref[...], x_ref[...])
+
+    @pl.when(pl.program_id(0) == 0)
+    def _():
+        most_ref[...] = most(l_ref[...])
 
 
 def lefts(l, x, unit):
@@ -135,13 +152,19 @@
     cols = x.shape[1]
     return pl.pallas_call(
         lefts_kernel,
-        out_shape=jax.ShapeDtypeStruct((p, cols), F32),
+        out_shape=[
+            jax.ShapeDtypeStruct((p, cols), F32),
+            jax.ShapeDtypeStruct((1, rows), F32),
+        ],
         grid=(cols // unit,),
         in_specs=[
             pl.BlockSpec((p, rows), lambda i: (0, 0)),
             pl.BlockSpec((rows, unit), lambda i: (0, i)),
         ],
-        out_specs=pl.BlockSpec((p, unit), lambda i: (0, i)),
+        out_specs=[
+            pl.BlockSpec((p, unit), lambda i: (0, i)),
+            pl.BlockSpec((1, rows), lambda i: (0, 0)),
+        ],
         compiler_params=params(1),
         cost_estimate=cost(p * rows * cols),
         name="left_products",
@@ -190,62 +213,94 @@
     )(row_bounds, col_bounds, in_hbm(x))
 
 
-def core_spread_kernel(core_ref, r_ref, out_ref):
-    high, low = halves(core_ref[...])
+def core_spread_kernel(bit_ref, *refs):
+    parts, r_ref, out_ref, high_ref, low_ref = refs[:4], *refs[4:]
+    half, share, p = parts[0].shape
+
+    @pl.when(pl.program_id(0) == 0)
+    def _():
+        upper = bit_ref[0] == 1
+        for s in range(2):
+            mine, got = parts[2 * s][...], parts[2 * s + 1][...]
+            pairs = jnp.stack(
+                [jnp.where(upper, got, mine), jnp.where(upper, mine, got)], axis=1
+            )
+            span = slice(s * 2 * half * share, (s + 1) * 2 * half * share)
+            high, low = halves(pairs.reshape(2 * half * share, p))
+            high_ref[span, :] = high
+            low_ref[span, :] = low
+
     right = r_ref[...]
-    out_ref[...] = dot(high, right) + dot(low, right)
-
-
-def core_spread(core, r):
+    out_ref[...] = dot(high_ref[...], right) + dot(low_ref[...], right)
+
+
+def core_spread(bit, parts, r, each):
     p, cols = r.shape
-    width = min(512, cols)
+    width = min(1024, cols)
+    half, tail, _ = parts[0].shape
+    share = tail - each
     return pl.pallas_call(
         core_spread_kernel,
         out_shape=jax.ShapeDtypeStruct((p, cols), F32),
         grid=(cols // width,),
-        in_specs=[
-            pl.BlockSpec((p, p), lambda i: (0, 0)),
-            pl.BlockSpec((p, width), lambda i: (0, i)),
-        ],
+        in_specs=[pl.BlockSpec(memory_space=pltpu.SMEM)]
+        + [pl.BlockSpec((half, share, p), lambda i: (0, each // share, 0))] * 4
+        + [pl.BlockSpec((p, width), lambda i: (0, i))],
         out_specs=pl.BlockSpec((p, width), lambda i: (0, i)),
+        scratch_shapes=[pltpu.VMEM((p, p), BF16)] * 2,
         compiler_params=params(1),
         cost_estimate=cost(2 * p * p * cols),
         name="core_spread",
-    )(core, in_hbm(r))
+    )(bit, *parts, in_hbm(r))
+
+
+def top_scale(largest):
+    return F8_TOP / jnp.maximum(largest, 1e-25)
 
 
 def finish_kernel(groups, bit_ref, scale_ref, x_ref, *refs):
     s_refs = refs[:4]
-    lt_ref, add_ref, r_ref, t_ref, out_ref, sum_ref, both, twice = refs[4:]
+    lt_ref, add_ref, r_ref, t_ref = refs[4:8]
+    out_ref, sum_ref, both, twice, low_both, low_twice, factors = refs[8:]
     p, cols = r_ref.shape
-    each = s_refs[0].shape[1]
     i = pl.program_id(0)
     width = min(512, cols)
 
     @pl.when(i == 0)
     def _():
-        high, low = halves(t_ref[...] + add_ref[...])
+        whole = t_ref[...] + add_ref[...]
+        high = whole.astype(BF16)
+        rest = whole - high.astype(F32)
+        s_most, r_scale, l_scale = scale_ref[2], scale_ref[3], scale_ref[4]
+        scale = jnp.minimum(
+            top_scale(s_most / 256.0) * r_scale, top_scale(jnp.max(jnp.abs(rest))) * l_scale
+        )
+        factors[0] = scale / r_scale
+        factors[1] = scale_ref[1] / scale
         twice[:p, :] = r_ref[...]
-        twice[p : 2 * p, :] = r_ref[...]
-        twice[2 * p : 3 * p, :] = high
-        twice[3 * p :, :] = low
+        twice[p:, :] = high
+        low_twice[:p, :] = (r_ref[...].astype(F32) * r_scale).astype(F8)
+        low_twice[p:, :] = (rest * (scale / l_scale)).astype(F8)
         sum_ref[...] = jnp.zeros_like(sum_ref)
 
     upper = bit_ref[0] == 1
     early = i < groups // 2
     mine = jnp.where(early, s_refs[0][0], s_refs[2][0])
     got = jnp.where(early, s_refs[1][0], s_refs[3][0])
-    for k, rows in enumerate((jnp.where(upper, got, mine), jnp.where(upper, mine, got))):
-        high, low = halves(rows)
-        both[k * each : (k + 1) * each, :p] = high
-        both[k * each : (k + 1) * each, p : 2 * p] = low
+    summed = jnp.concatenate([jnp.where(upper, got, mine), jnp.where(upper, mine, got)])
+    high = summed.astype(BF16)
+    both[:, :p] = high
     left = lt_ref[...]
-    both[:, 2 * p : 3 * p] = left
-    both[:, 3 * p :] = left
+    both[:, p:] = left
+    low_both[:, :p] = ((summed - high.astype(F32)) * factors[0]).astype(F8)
+    low_both[:, p:] = (left.astype(F32) * scale_ref[4]).astype(F8)
     for at in range(0, cols, width):
         span = slice(at, at + width)
-        change = dot(both[...], twice[:, span])
-        left_over = scale_ref[0] * x_ref[:, span].astype(F32) - scale_ref[1] * change
+        left_over = (
+            scale_ref[0] * x_ref[:, span].astype(F32)
+            - scale_ref[1] * dot(both[...], twice[:, span])
+            - factors[1] * dot(low_both[...], low_twice[:, span])
+        )
         out_ref[:, span] = left_over
         sum_ref[:, span] += jnp.sum(left_over * left_over, axis=0, keepdims=True)
 
@@ -282,13 +337,16 @@
             pl.BlockSpec((1, cols), lambda i: (0, 0)),
         ],
         scratch_shapes=[
-            pltpu.VMEM((2 * each, 4 * p), BF16),
-            pltpu.VMEM((4 * p, cols), BF16),
+            pltpu.VMEM((2 * each, 2 * p), BF16),
+            pltpu.VMEM((2 * p, cols), BF16),
+            pltpu.VMEM((2 * each, 2 * p), F8),
+            pltpu.VMEM((2 * p, cols), F8),
+            pltpu.SMEM((2,), F32),
         ],
         compiler_params=params(1),
         cost_estimate=cost(4 * p * rows * cols),
         name="finish_residual",
-    )(bit, scales, in_hbm(x), *s_parts, in_hbm(lt), add, in_hbm(r), t)
+    )(bit, scales, in_hbm(x), *s_parts, in_hbm(lt), in_hbm(add), in_hbm(r), in_hbm(t))
 
 
 def swap(value, axis, mask, size):
@@ -339,7 +397,7 @@
     def pick(value, axis, at):
         return lax.dynamic_index_in_dim(value, at, axis, False)
 
-    partial_left = run(lambda l: lefts(l, x, min(512, cols)), theta_left)
+    partial_left, l_most = run(lambda l: lefts(l, x, min(512, cols)), theta_left)
     own_left = lax.psum_scatter(partial_left, "row", scatter_dimension=0, tiled=True)
 
     intervals = []
@@ -381,7 +439,7 @@
         scatter_start(s, level)
 
     shape = (2,) * (len(masks) - 1)
-    core = run(lambda t: core_products(t, theta_right), partial_left)
+    core, r_most = run(lambda t: core_products(t, theta_right), partial_left)
     for s in range(streams):
         sent, kept, square = run(
             lambda v: rights(x, v, core, core_bit, s, streams, n_col, tall), theta_right
@@ -400,20 +458,31 @@
         got = flight[s]
         parts.append(run(lambda v, *rest: sum(rest, v) + got, *terms[s]))
 
+    own_left = run(lambda v: v, own_left)
+    whole_left = lax.all_gather(own_left, "row", axis=0, tiled=True)
+    top = len(masks) - 1
+    for s in range(streams):
+        flight[s] = swap(run(lambda v: v[:each], parts[s]), "col", orders[s][top], n_col)
+
     core = jnp.concatenate([part[each:] for part in parts])
+    total = 0.0
+    s_most = jnp.maximum(*[jnp.max(jnp.abs(part[:each])) for part in parts])
     local = [
         lambda v: sum(jnp.sum(part[:each] * part[:each]) for part in (v, parts[1])),
         lambda v: jnp.sum(own_left * own_left) + 0.0 * v[0, 0],
     ]
-    total = 0.0
     for mask in powers(n_row):
         got = swap(core, "row", mask, n_row)
         if local:
             total = total + run(local.pop(0), parts[0])
+        if not local:
+            mask_piece()
         core = run(lambda v: v + got, core)
-    own_left = run(lambda v: v, own_left)
-    whole_left = lax.all_gather(own_left, "row", axis=0, tiled=True)
     core_square = jnp.sum(core * core)
+    core_parts = jnp.split(core, streams)
+    core_flight = [
+        swap(core_parts[s], "col", orders[s][top], n_col) for s in range(streams)
+    ]
 
     def widen_start(s, level):
         flight[s] = swap(parts[s], "col", orders[s][level], n_col)
@@ -423,6 +492,9 @@
         held = [m for m in masks if m in orders[s][level + 1 :]]
         axis = sum(1 for m in held if m > mask)
         dims = (2,) * len(held)
+        if level == top:
+            flight[s] = jnp.concatenate([flight[s], core_flight[s]])
+            parts[s] = jnp.concatenate([parts[s][:each], core_parts[s]])
         other = flight[s].reshape(*dims, tail, p)
         parts[s] = run(
             lambda v: jnp.where(
@@ -434,13 +506,10 @@
         ).reshape(-1, tail, p)
         widen_start(s, level - 1)
 
-    top = len(masks) - 1
-    for s in range(streams):
-        rows_of = jnp.concatenate([parts[s][:each], core[s * share : (s + 1) * share]])
-        parts[s] = run(lambda v: v, rows_of)
-        widen_start(s, top)
-    sums = jnp.repeat(jnp.stack([squares, total + core_square / n_row]), 4)[:, None]
-    sums = sums + jnp.zeros((1, 128), F32)
+    lane = lax.broadcasted_iota(jnp.int32, (8, 128), 0)
+    sums = jnp.where(
+        lane < 3, squares, jnp.where(lane < 6, total + core_square / n_row, s_most)
+    )
     sum_hops = [("row", m, n_row) for m in powers(n_row)] + [("col", m, n_col) for m in masks]
     sum_flight = None
 
@@ -455,46 +524,40 @@
         if sum_hops:
             sum_hops.pop(0)
             got = sum_flight
-            sums = run(lambda v: v + got, sums)
+            sums = run(lambda v: jnp.where(lane < 6, v + got, jnp.maximum(v, got)), sums)
             sum_start()
 
     sum_start()
-    mask_piece()
+    lt = run(lambda v: v.T, theta_left)
+    l_scale = top_scale(jnp.max(l_most))
+    r_scale = top_scale(jnp.max(r_most))
     for level in range(top, 0, -1):
-        sum_step()
         for s in range(streams):
             widen(s, level)
-        mask_piece()
-    while mask_starts:
-        mask_piece()
+        sum_step()
+        if level == top:
+            while mask_starts:
+                mask_piece()
+            sum_step()
+            sum_step()
+            sum_step()
     while sum_hops:
         sum_step()
     packed = sums
 
-    pieces = []
-    for s in range(streams):
-        mine, other = (v.reshape(-1, tail, p)[:, each:] for v in (parts[s], flight[s]))
-        pieces.append(
-            jnp.where(
-                bits[masks[0]] == 1,
-                jnp.stack([other, mine], axis=1),
-                jnp.stack([mine, other], axis=1),
-            )
-        )
-    core = run(lambda *v: jnp.stack(v).reshape(p, p), *pieces)
-    lt = run(lambda v: v.T, theta_left)
-    core_add = run(lambda v: core_spread(v, theta_right), core)
+    s_parts = [v.reshape(-1, tail, p) for s in range(streams) for v in (parts[s], flight[s])]
+    core_add = run(lambda v: core_spread(core_bit, [v] + s_parts[1:], theta_right, each), s_parts[0])
 
     start_norm = packed[0, 0]
-    extra = packed[4, 0]
+    extra = packed[3, 0]
     curvature = start_norm + extra
     alpha = start_norm / curvature
 
     residual, square = finish(
         core_bit,
-        jnp.stack([extra / curvature, alpha]),
+        jnp.stack([extra / curvature, alpha, packed[6, 0], r_scale, l_scale]),
         x,
-        [v.reshape(-1, tail, p) for s in range(streams) for v in (parts[s], flight[s])],
+        s_parts,
         lt,
         core_add,
         theta_right,

time: 274 us -> 263 us (0.960)
  waiting for transfers between devices: 51.3 us -> 41.9 us
    ppermute x24 -> x26, waiting for transfers between devices: 46.8 us -> 40.5 us  [swap(): return lax.ppermute(value, axis, [(i, i ^ mask) for i in range(size)])]
    select_n x4, other arithmetic: 7.49 us -> 2.18 us  [widen(): jnp.where(bits[mask] == 1, jnp.stack([other, v], axis=axis), jnp.stack([v...]
    pallas_call x1, Pallas kernels: 46.6 us -> 42.7 us  [finish(): pl.pallas_call(functools.partial(finish_kernel, groups), out_shape=[jax.S...]
    squeeze x4, local copies, waits for them, and re-layouts: 0.25 us -> 3.71 us  [pick(): return lax.dynamic_index_in_dim(value, at, axis, False)]
    all_gather x1, waiting for transfers between devices: 4.51 us -> 1.32 us  [shards(): whole_left = lax.all_gather(own_left, 'row', axis=0, tiled=True)]
    unnamed x33 -> x31, local copies, waits for them, and re-layouts: 8.98 us -> 6.15 us
    ppermute x24 -> x26, starting transfers between devices: 28.2 us -> 27.1 us  [swap(): return lax.ppermute(value, axis, [(i, i ^ mask) for i in range(size)])]
  transfers between devices with their start and end apart: 26 -> 28, of which waited for: 15 -> 13; matrix products, arithmetic and copies ran while one was open for 15% -> 16% of each run, Pallas kernels for 21% -> 23%
where the time goes in v3:
time: 263 us; the launch traced here: 262 us
  Pallas kernels  116 us (44%)
  waiting for transfers between devices  41.9 us (16%)
  other arithmetic  29.1 us (11%)
  starting transfers between devices  27.2 us (10%)
  between operations  26.7 us (10%)
  local copies, waits for them, and re-layouts  21.6 us (8%)
    pallas_call x1, Pallas kernels, finish(): pl.pallas_call(functools.partial(finish_kernel, groups), out_shape=[jax.S...  42.7 us
    ppermute x26, waiting for transfers between devices, swap(): return lax.ppermute(value, axis, [(i, i ^ mask) for i in range(size)])  40.5 us
    pallas_call x4, Pallas kernels, mask_sums(): pl.pallas_call(functools.partial(mask_kernel, steps, start), out_shape=ja...  31.3 us
    ppermute x26, starting transfers between devices, swap(): return lax.ppermute(value, axis, [(i, i ^ mask) for i in range(size)])  27.1 us
    pallas_call x2, Pallas kernels, rights(): pl.pallas_call(rights_kernel, out_shape=[half, half, jax.ShapeDtypeStruct...  17.7 us
    pallas_call x1, Pallas kernels, lefts(): pl.pallas_call(lefts_kernel, out_shape=[jax.ShapeDtypeStruct((p, cols), F...  13.6 us
    add x4, other arithmetic, scatter_start(): sum((pick(term, axis, 1 - bits[mask]) for term in rest), pick(v, axis, 1...  8.51 us
    optimization_barrier x1, local copies, waits for them, and re-layouts, after(): return lax.optimization_barrier((value,) + earlier)[0]  6.59 us
  transfers between devices with their start and end apart: 28, of which 13 were waited for; matrix products, arithmetic and copies ran while one was open for 16% of the time, Pallas kernels for 23%

profile of v3, /device:TPU:0, one launch (start us, length us, event | category | flops | bytes accessed | tf_op | source)
XLA Modules:
  0.0 262.1 jit_solution(14146330577376764142)
XLA Ops:
  7.2 13.6 %left_products.1 = (f32[512,2048]{1,0:T(8,128)S(1)}, f32[1,4096]{1,0:T(1,128)S(1)}) custom-call(bf16[512,4096]{1,0:T(8,128)(2,1)} %l_ref, bf16[4096,2048]{1,0:T(8,128)(2,1)} %x_ref.15), custom_call_target="tpu_custom_call" | custom-call | flops 2576980480 | bytes 1024 | tf_op jit(solution)/shard_map/left_products/pallas_call | solution.py:153
  20.8 2.0 copy-done
  22.9 4.6 %core_products.1 = (f32[512,512]{1,0:T(8,128)S(1)}, f32[1,2048]{1,0:T(1,128)S(1)}) custom-call(f32[512,2048]{1,0:T(8,128)} %copy-done, bf16[512,2048]{1,0:T(8,128)(2,1)} %refs_6_.1), custom_call_target="tpu_custom_call" | custom-call | flops 644245120 | bytes 1024 | tf_op jit(solution)/shard_map/core_products/pallas_call | solution.py:117
  27.5 8.9 %right_products.2 = (f32[4,288,512]{2,1,0:T(8,128)}, f32[4,288,512]{2,1,0:T(8,128)S(1)}, f32[1,2048]{1,0:T(1,128)S(1)}) custom-call(s32[1]{0:T(128)} %bitcast.bit_ref, bf16[4096,2048]{1,0:T(8,128)(2,1)} %x_ref.15, bf16[512,2048]{1,0:T(8,128)(2,1)} %refs_6_.1, f32[16,32,512]{2,1,0:T(8,128)S(1)} %bitcast.82), custom_call_target="tpu_custom_call" | custom-call | flops 1288490240 | bytes 1024 | tf_op jit(solution)/shard_map/right_products/pallas_call | solution.py:81
  36.9 8.9 %right_products.3 = (f32[4,288,512]{2,1,0:T(8,128)}, f32[4,288,512]{2,1,0:T(8,128)S(1)}, f32[1,2048]{1,0:T(1,128)S(1)}) custom-call(s32[1]{0:T(128)} %bitcast.bit_ref, bf16[4096,2048]{1,0:T(8,128)(2,1)} %x_ref.15, bf16[512,2048]{1,0:T(8,128)(2,1)} %refs_6_.1, f32[16,32,512]{2,1,0:T(8,128)S(1)} %bitcast.83), custom_call_target="tpu_custom_call" | custom-call | flops 1288490240 | bytes 1024 | tf_op jit(solution)/shard_map/right_products/pallas_call | solution.py:81
  45.7 1.4 copy-done.1
  47.2 2.5 add_bitcast_fusion.1
  49.8 3.0 %collective-permute-start.2 = (f32[2,288,512]{2,1,0:T(8,128)}, f32[2,288,512]{2,1,0:T(8,128)}, u32[]{:S(2)}, u32[]{:S(2)}) collective-permute-start(f32[2,288,512]{2,1,0:T(8,128)} %add_bitcast_fusion.1), channel_id=1, source_target_pairs={{0,2},{1,3},{2,0},{3,1},{4,6},{5,7},{6,4},{7,5},{8,10},{9,11},{10,... | collective-permute-start | bytes 3538952 | tf_op jit(solution)/shard_map/ppermute | solution.py:353
  52.8 3.0 %add_bitcast_fusion = f32[2,288,512]{2,1,0:T(8,128)} fusion(f32[2,2,288,512]{3,2,1,0:T(8,128)} %bitcast.9, s32[]{:T(128)S(6)} %select_n.133, f32[2,2,288,512]{3,2,1,0:T(8,128)} %bitcast.87), kind=kLoop, calls=%fused_computation.4 | loop fusion | flops 294912 | bytes 3538948 | tf_op jit(solution)/shard_map/add | solution.py:424
  55.8 2.0 collective-permute-start.3
  57.8 1.1 dynamic-slice_bitcast_fusion
  59.2 1.1 copy.19
  62.8 1.4 dynamic-slice_bitcast_fusion.1
  64.3 7.8 %interval_sums.4 = f32[1024,1]{1,0:T(8,128)S(1)} custom-call(s32[1024,2]{1,0:T(8,128)S(1)} %broadcast_clamp_fusion.rows_ref, s32[1024,2]{1,0:T(8,128)S(1)} %broadcast_subtract_fusion.cols_ref, bf16[4096,2048]{1,0:T(8,128)(2,1)} %x_ref.15), custom_call_target="tpu_custom_call" | custom-call | flops 1288490240 | bytes 1024 | tf_op jit(solution)/shard_map/interval_sums/pallas_call | solution.py:199
  72.1 0.8 copy-done.2
  72.9 7.8 %interval_sums.5 = f32[1024,1]{1,0:T(8,128)S(1)} custom-call(s32[1024,2]{1,0:T(8,128)S(1)} %broadcast_clamp_fusion.rows_ref, s32[1024,2]{1,0:T(8,128)S(1)} %broadcast_subtract_fusion.cols_ref, bf16[4096,2048]{1,0:T(8,128)(2,1)} %x_ref.15), custom_call_target="tpu_custom_call" | custom-call | flops 1288490240 | bytes 1024 | tf_op jit(solution)/shard_map/interval_sums/pallas_call | solution.py:199
  80.8 1.6 bitcast_add_fusion.6
  82.5 2.1 collective-permute-done.3
  84.6 1.4 bitcast_add_fusion.4
  86.0 1.8 collective-permute-start.5
  87.9 1.1 dynamic-slice_bitcast_fusion.2
  89.0 8.8 %collective-permute-done.4 = f32[288,512]{1,0:T(8,128)S(1)} collective-permute-done((f32[288,512]{1,0:T(8,128)S(1)}, f32[288,512]{1,0:T(8,128)S(1)}, u32[]{:S(2)}, u32[]{:S(2)}) %collective-permute-start.4) | collective-permute-done | bytes 589856 | tf_op jit(solution)/shard_map/ppermute | solution.py:353
  97.8 1.5 fusion.1
  99.3 1.9 collective-permute-done.5
  101.2 1.5 fusion
  102.7 1.6 collective-permute-start.6
  104.4 1.6 multiply_reduce_fusion.1
  105.9 1.4 fusion.4
  108.6 0.9 slice.56
  109.5 0.9 slice.57
  110.4 0.7 multiply_reduce_fusion.2
  112.4 1.6 add.202
  114.1 2.6 collective-permute-start.7
  116.7 0.9 multiply_reduce_fusion
  117.5 1.6 collective-permute-start.8
  119.1 1.5 collective-permute-start.10
  122.4 7.9 %interval_sums.6 = f32[1024,1]{1,0:T(8,128)S(1)} custom-call(s32[1024,2]{1,0:T(8,128)S(1)} %broadcast_clamp_fusion.rows_ref, s32[1024,2]{1,0:T(8,128)S(1)} %broadcast_subtract_fusion.cols_ref, bf16[4096,2048]{1,0:T(8,128)(2,1)} %x_ref.15), custom_call_target="tpu_custom_call" | custom-call | flops 1288490240 | bytes 1024 | tf_op jit(solution)/shard_map/interval_sums/pallas_call | solution.py:199
  130.3 0.8 copy-done.6
  131.1 1.6 multiply_reduce_fusion.3
  132.8 0.9 collective-permute-start.9
  133.6 1.3 collective-permute-start.11
  135.0 6.6 %copy.20 = bf16[512,4096]{0,1:T(8,128)(2,1)} copy(bf16[512,4096]{1,0:T(8,128)(2,1)} %l_ref) | data formatting | bytes 8388608 | tf_op jit(solution)/shard_map/optimization_barrier | solution.py:31
  142.4 1.1 maximum_bitcast_fusion.1
  143.7 0.8 collective-permute-start.17
  144.7 1.6 collective-permute-start.19
  146.3 1.8 collective-permute-done.12
  148.2 7.7 %interval_sums.7 = f32[1024,1]{1,0:T(8,128)S(1)} custom-call(s32[1024,2]{1,0:T(8,128)S(1)} %broadcast_clamp_fusion.rows_ref, s32[1024,2]{1,0:T(8,128)S(1)} %broadcast_subtract_fusion.cols_ref, bf16[4096,2048]{1,0:T(8,128)(2,1)} %x_ref.15), custom_call_target="tpu_custom_call" | custom-call | flops 1288490240 | bytes 1024 | tf_op jit(solution)/shard_map/interval_sums/pallas_call | solution.py:199
  156.1 1.2 collective-permute-done.14
  157.3 1.3 collective-permute-start.15
  158.6 11.6 %collective-permute-done.15 = f32[8,128]{1,0:T(8,128)S(1)} collective-permute-done((f32[8,128]{1,0:T(8,128)S(1)}, f32[8,128]{1,0:T(8,128)S(1)}, u32[]{:S(2)}, u32[]{:S(2)}) %collective-permute-start.15) | collective-permute-done | bytes 4128 | tf_op jit(solution)/shard_map/ppermute | solution.py:353
  170.8 1.7 maximum_select_fusion.1
  176.1 1.4 add_reduce_fusion
  177.5 1.6 collective-permute-done.16
  183.2 5.6 %core_spread.1.refs_5_ = f32[512,2048]{1,0:T(8,128)} custom-call(s32[1]{0:T(128)} %bitcast.bit_ref, f32[4,288,512]{2,1,0:T(8,128)S(1)} %bitcast.80, f32[4,288,512]{2,1,0:T(8,128)} %collective-permute-done.18.refs_1_, f32[4,288,512]{2,1,0:T(8,128)} %bitcast.40.refs_2_, f32[4,288,512]{2,1,0:T(8,128)} %collective-permute-done.20.refs_3_, bf16[512,2048]{1,0:T(8,128)(2,1)} %refs_6_.1), custom_call_target="tpu_custom_call" | custom-call | flops 644245120 | bytes 1024 | tf_op jit(solution)/shard_map/core_spread/pallas_call | solution.py:242
  188.8 1.3 all-gather.2.cloned.1.call-done.refs_7_
  190.2 42.7 %finish_residual.1 = (f32[4096,2048]{1,0:T(8,128)}, f32[1,2048]{1,0:T(1,128)S(1)}) custom-call(s32[1]{0:T(128)} %bitcast.bit_ref, f32[5]{0:T(128)S(1)} %stack.83.scale_ref, bf16[4096,2048]{1,0:T(8,128)(2,1)} %x_ref.15, f32[4,288,512]{2,1,0:T(8,128)S(1)} %bitcast.81, f32[4,288,512]{2,1,0:T(8,128)} %collective-permute-done.18.refs_1_, ...), custom_call_target="tpu_custom_call" | custom-call | flops 10307921920 | bytes 1024 | tf_op jit(solution)/shard_map/finish_residual/pallas_call | solution.py:315
  234.2 3.6 %collective-permute-done.21 = f32[16,128]{1,0:T(8,128)S(1)} collective-permute-done((f32[16,128]{1,0:T(8,128)S(1)}, f32[16,128]{1,0:T(8,128)S(1)}, u32[]{:S(2)}, u32[]{:S(2)}) %collective-permute-start.21) | collective-permute-done | bytes 8224 | tf_op jit(solution)/shard_map/ppermute | solution.py:353
  238.5 2.4 collective-permute-start.22
  240.9 2.2 collective-permute-done.22
  243.2 1.2 collective-permute-done.23
  244.3 1.5 collective-permute-start.24
  245.8 2.2 collective-permute-done.24
  248.0 1.3 collective-permute-start.25
  249.3 2.3 collective-permute-done.25
  (98 shorter events, 11.2 us)
Async XLA Ops:
  7.2 97.2 %reduce-scatter.2.cloned.1.call-start = ((), (), s32[]{:S(2)}) async-start(), calls=%async_computation.1 | async-start | bytes 5242880 | tf_op jit(solution)/shard_map/reduce_scatter | solution.py:401
  20.8 2.0 copy-start
  22.8 167.3 %all-gather.2.cloned.1.call-start = ((), (), s32[]{:S(2)}) async-start(), calls=%async_computation.2 | async-start | bytes 5242880 | tf_op jit(solution)/shard_map/all_gather | solution.py:462
  36.4 10.8 %collective-permute-start = (f32[4,288,512]{2,1,0:T(8,128)}, f32[4,288,512]{2,1,0:T(8,128)}, u32[]{:S(2)}, u32[]{:S(2)}) collective-permute-start(f32[4,288,512]{2,1,0:T(8,128)} %get-tuple-element.51), channel_id=1, source_target_pairs={{0,1},{1,0},{2,3},{3,2},{4,5},{5,4},{6,7},{7,6},{8,9},{9,8},{10,11... | collective-permute-start | bytes 7077896 | tf_op jit(solution)/shard_map/ppermute | solution.py:353
  45.7 1.4 copy-start.1
  47.2 5.6 %copy-start.14 = (s32[1024,2]{0,1:T(2,128)S(1)}, s32[1024,2]{0,1:T(2,128)}, u32[]{:S(2)}) copy-start(s32[1024,2]{0,1:T(2,128)} %param.8) | copy-start | bytes 24580
  47.2 5.6 %collective-permute-start.1 = (f32[4,288,512]{2,1,0:T(8,128)}, f32[4,288,512]{2,1,0:T(8,128)}, u32[]{:S(2)}, u32[]{:S(2)}) collective-permute-start(f32[4,288,512]{2,1,0:T(8,128)} %get-tuple-element.56), channel_id=1, source_target_pairs={{0,1},{1,0},{2,3},{3,2},{4,5},{5,4},{6,7},{7,6},{8,9},{9,8},{10,11... | collective-permute-start | bytes 7077896 | tf_op jit(solution)/shard_map/ppermute | solution.py:353
  49.8 31.0 %collective-permute-start.2 = (f32[2,288,512]{2,1,0:T(8,128)}, f32[2,288,512]{2,1,0:T(8,128)}, u32[]{:S(2)}, u32[]{:S(2)}) collective-permute-start(f32[2,288,512]{2,1,0:T(8,128)} %add_bitcast_fusion.1), channel_id=1, source_target_pairs={{0,2},{1,3},{2,0},{3,1},{4,6},{5,7},{6,4},{7,5},{8,10},{9,11},{10,... | collective-permute-start | bytes 3538952 | tf_op jit(solution)/shard_map/ppermute | solution.py:353
  52.8 6.3 %copy-start.13 = (s32[1024,2]{0,1:T(2,128)S(1)}, s32[1024,2]{0,1:T(2,128)}, u32[]{:S(2)}) copy-start(s32[1024,2]{0,1:T(2,128)} %param.9) | copy-start | bytes 24580
  55.8 28.8 %collective-permute-start.3 = (f32[2,288,512]{2,1,0:T(8,128)}, f32[2,288,512]{2,1,0:T(8,128)}, u32[]{:S(2)}, u32[]{:S(2)}) collective-permute-start(f32[2,288,512]{2,1,0:T(8,128)} %add_bitcast_fusion), channel_id=1, source_target_pairs={{0,4},{1,5},{2,6},{3,7},{4,0},{5,1},{6,2},{7,3},{8,12},{9,13},{10,... | collective-permute-start | bytes 3538952 | tf_op jit(solution)/shard_map/ppermute | solution.py:353
  62.8 1.5 copy-start.12
  72.1 0.8 copy-start.2
  72.9 7.8 %copy-start.9 = (f32[2,288,512]{2,1,0:T(8,128)S(1)}, f32[2,288,512]{2,1,0:T(8,128)}, u32[]{:S(2)}) copy-start(f32[2,288,512]{2,1,0:T(8,128)} %dynamic-slice_bitcast_fusion) | copy-start | bytes 3538948
  80.7 5.3 %copy-start.4 = (f32[1024,1]{1,0:T(8,128)}, f32[1024,1]{1,0:T(8,128)S(1)}, u32[]{:S(2)}) copy-start(f32[1024,1]{1,0:T(8,128)S(1)} %interval_sums.5) | copy-start | bytes 12292
  82.4 15.4 %collective-permute-start.4 = (f32[288,512]{1,0:T(8,128)S(1)}, f32[288,512]{1,0:T(8,128)S(1)}, u32[]{:S(2)}, u32[]{:S(2)}) collective-permute-start(f32[288,512]{1,0:T(8,128)S(1)} %bitcast_add_fusion.6), channel_id=1, source_target_pairs={{0,4},{1,5},{2,6},{3,7},{4,0},{5,1},{6,2},{7,3},{8,12},{9,13},{10,... | collective-permute-start | bytes 1769480 | tf_op jit(solution)/shard_map/ppermute | solution.py:353
  86.0 15.2 %collective-permute-start.5 = (f32[288,512]{1,0:T(8,128)S(1)}, f32[288,512]{1,0:T(8,128)S(1)}, u32[]{:S(2)}, u32[]{:S(2)}) collective-permute-start(f32[288,512]{1,0:T(8,128)S(1)} %bitcast_add_fusion.4), channel_id=1, source_target_pairs={{0,2},{1,3},{2,0},{3,1},{4,6},{5,7},{6,4},{7,5},{8,10},{9,11},{10,... | collective-permute-start | bytes 1769480 | tf_op jit(solution)/shard_map/ppermute | solution.py:353
  102.7 9.7 %collective-permute-start.6 = (f32[64,512]{1,0:T(8,128)S(1)}, f32[64,512]{1,0:T(8,128)}, u32[]{:S(2)}, u32[]{:S(2)}) collective-permute-start(f32[64,512]{1,0:T(8,128)S(1)} %pad_maximum_fusion.2), channel_id=1, source_target_pairs={{0,8},{8,0},{16,24},{24,16},{1,9},{9,1},{17,25},{25,17},{2,10},{10... | collective-permute-start | bytes 393224 | tf_op jit(solution)/shard_map/ppermute | solution.py:353
  104.4 12.3 %copy-start.8 = (f32[128,2048]{1,0:T(8,128)S(1)}, f32[128,2048]{1,0:T(8,128)}, u32[]{:S(2)}) copy-start(f32[128,2048]{1,0:T(8,128)} %reduce-scatter.2.cloned.1.call-done) | copy-start | bytes 3145732
  114.1 17.1 %collective-permute-start.7 = (f32[64,512]{1,0:T(8,128)}, f32[64,512]{1,0:T(8,128)}, u32[]{:S(2)}, u32[]{:S(2)}) collective-permute-start(f32[64,512]{1,0:T(8,128)} %add.202), channel_id=1, source_target_pairs={{0,16},{8,24},{16,0},{24,8},{1,17},{9,25},{17,1},{25,9},{2,18},{10... | collective-permute-start | bytes 393224 | tf_op jit(solution)/shard_map/ppermute | solution.py:353
  117.5 26.9 %collective-permute-start.8 = (f32[256,512]{1,0:T(8,128)}, f32[256,512]{1,0:T(8,128)S(1)}, u32[]{:S(2)}, u32[]{:S(2)}) collective-permute-start(f32[256,512]{1,0:T(8,128)} %slice.57), channel_id=1, source_target_pairs={{0,2},{1,3},{2,0},{3,1},{4,6},{5,7},{6,4},{7,5},{8,10},{9,11},{10,... | collective-permute-start | bytes 1572872 | tf_op jit(solution)/shard_map/ppermute | solution.py:353
  119.1 23.3 %collective-permute-start.10 = (f32[256,512]{1,0:T(8,128)}, f32[256,512]{1,0:T(8,128)}, u32[]{:S(2)}, u32[]{:S(2)}) collective-permute-start(f32[256,512]{1,0:T(8,128)} %slice.56), channel_id=1, source_target_pairs={{0,4},{1,5},{2,6},{3,7},{4,0},{5,1},{6,2},{7,3},{8,12},{9,13},{10,... | collective-permute-start | bytes 1572872 | tf_op jit(solution)/shard_map/ppermute | solution.py:353
  122.4 12.5 %copy-start.11 = (f32[256,512]{1,0:T(8,128)S(1)}, f32[256,512]{1,0:T(8,128)}, u32[]{:S(2)}) copy-start(f32[256,512]{1,0:T(8,128)} %get-tuple-element.91) | copy-start | bytes 1572868
  130.3 0.8 copy-start.6
  132.8 11.7 %collective-permute-start.9 = (f32[32,512]{1,0:T(8,128)S(1)}, f32[32,512]{1,0:T(8,128)S(1)}, u32[]{:S(2)}, u32[]{:S(2)}) collective-permute-start(f32[32,512]{1,0:T(8,128)S(1)} %get-tuple-element.95), channel_id=1, source_target_pairs={{0,2},{1,3},{2,0},{3,1},{4,6},{5,7},{6,4},{7,5},{8,10},{9,11},{10,... | collective-permute-start | bytes 196616 | tf_op jit(solution)/shard_map/ppermute | solution.py:353
  133.6 8.7 %collective-permute-start.11 = (f32[32,512]{1,0:T(8,128)S(1)}, f32[32,512]{1,0:T(8,128)}, u32[]{:S(2)}, u32[]{:S(2)}) collective-permute-start(f32[32,512]{1,0:T(8,128)S(1)} %get-tuple-element.94), channel_id=1, source_target_pairs={{0,4},{1,5},{2,6},{3,7},{4,0},{5,1},{6,2},{7,3},{8,12},{9,13},{10,... | collective-permute-start | bytes 196616 | tf_op jit(solution)/shard_map/ppermute | solution.py:353
  135.0 7.4 %copy-start.10 = (f32[256,512]{1,0:T(8,128)S(1)}, f32[256,512]{1,0:T(8,128)}, u32[]{:S(2)}) copy-start(f32[256,512]{1,0:T(8,128)} %get-tuple-element.93) | copy-start | bytes 1572868
  142.3 5.8 %collective-permute-start.12 = (f32[8,128]{1,0:T(8,128)S(1)}, f32[8,128]{1,0:T(8,128)S(1)}, u32[]{:S(2)}, u32[]{:S(2)}) collective-permute-start(f32[8,128]{1,0:T(8,128)S(1)} %broadcast_select_fusion), channel_id=1, source_target_pairs={{0,8},{8,0},{16,24},{24,16},{1,9},{9,1},{17,25},{25,17},{2,10},{10... | collective-permute-start | bytes 12296 | tf_op jit(solution)/shard_map/ppermute | solution.py:353
  143.7 26.6 %collective-permute-start.17 = (f32[2,288,512]{2,1,0:T(8,128)S(1)}, f32[2,288,512]{2,1,0:T(8,128)S(1)}, u32[]{:S(2)}, u32[]{:S(2)}) collective-permute-start(f32[2,288,512]{2,1,0:T(8,128)S(1)} %maximum_select_fusion.2), channel_id=1, source_target_pairs={{0,2},{1,3},{2,0},{3,1},{4,6},{5,7},{6,4},{7,5},{8,10},{9,11},{10,... | collective-permute-start | bytes 3538952 | tf_op jit(solution)/shard_map/ppermute | solution.py:353
  144.7 26.1 %collective-permute-start.19 = (f32[2,288,512]{2,1,0:T(8,128)S(1)}, f32[2,288,512]{2,1,0:T(8,128)S(1)}, u32[]{:S(2)}, u32[]{:S(2)}) collective-permute-start(f32[2,288,512]{2,1,0:T(8,128)S(1)} %maximum_select_fusion.3), channel_id=1, source_target_pairs={{0,4},{1,5},{2,6},{3,7},{4,0},{5,1},{6,2},{7,3},{8,12},{9,13},{10,... | collective-permute-start | bytes 3538952 | tf_op jit(solution)/shard_map/ppermute | solution.py:353
  148.2 7.8 %collective-permute-start.13 = (f32[8,128]{1,0:T(8,128)S(1)}, f32[8,128]{1,0:T(8,128)S(1)}, u32[]{:S(2)}, u32[]{:S(2)}) collective-permute-start(f32[8,128]{1,0:T(8,128)S(1)} %maximum_select_fusion.8), channel_id=1, source_target_pairs={{0,16},{8,24},{16,0},{24,8},{1,17},{9,25},{17,1},{25,9},{2,18},{10... | collective-permute-start | bytes 12296 | tf_op jit(solution)/shard_map/ppermute | solution.py:353
  155.9 14.6 %copy-start.7 = (f32[1024,1]{1,0:T(8,128)}, f32[1024,1]{1,0:T(8,128)S(1)}, u32[]{:S(2)}) copy-start(f32[1024,1]{1,0:T(8,128)S(1)} %interval_sums.7) | copy-start | bytes 12292
  156.0 1.2 collective-permute-start.14
  157.3 12.9 %collective-permute-start.15 = (f32[8,128]{1,0:T(8,128)S(1)}, f32[8,128]{1,0:T(8,128)S(1)}, u32[]{:S(2)}, u32[]{:S(2)}) collective-permute-start(f32[8,128]{1,0:T(8,128)S(1)} %maximum_select_fusion.6), channel_id=1, source_target_pairs={{0,2},{1,3},{2,0},{3,1},{4,6},{5,7},{6,4},{7,5},{8,10},{9,11},{10,... | collective-permute-start | bytes 12296 | tf_op jit(solution)/shard_map/ppermute | solution.py:353
  170.8 5.3 %copy-start.3 = (f32[1024,1]{1,0:T(8,128)S(1)}, f32[1024,1]{1,0:T(8,128)}, u32[]{:S(2)}) copy-start(f32[1024,1]{1,0:T(8,128)} %copy-done.2) | copy-start | bytes 12292
  170.8 5.3 %copy-start.5 = (f32[1024,1]{1,0:T(8,128)S(1)}, f32[1024,1]{1,0:T(8,128)}, u32[]{:S(2)}) copy-start(f32[1024,1]{1,0:T(8,128)} %copy-done.4) | copy-start | bytes 12292
  172.5 10.7 %collective-permute-start.20 = (f32[4,288,512]{2,1,0:T(8,128)}, f32[4,288,512]{2,1,0:T(8,128)}, u32[]{:S(2)}, u32[]{:S(2)}) collective-permute-start(f32[4,288,512]{2,1,0:T(8,128)} %bitcast.40.refs_2_), channel_id=1, source_target_pairs={{0,1},{1,0},{2,3},{3,2},{4,5},{5,4},{6,7},{7,6},{8,9},{9,8},{10,11... | collective-permute-start | bytes 7077896 | tf_op jit(solution)/shard_map/ppermute | solution.py:353
  172.5 10.7 %collective-permute-start.18 = (f32[4,288,512]{2,1,0:T(8,128)S(1)}, f32[4,288,512]{2,1,0:T(8,128)}, u32[]{:S(2)}, u32[]{:S(2)}) collective-permute-start(f32[4,288,512]{2,1,0:T(8,128)S(1)} %bitcast.79), channel_id=1, source_target_pairs={{0,1},{1,0},{2,3},{3,2},{4,5},{5,4},{6,7},{7,6},{8,9},{9,8},{10,11... | collective-permute-start | bytes 7077896 | tf_op jit(solution)/shard_map/ppermute | solution.py:353
  175.5 3.7 %collective-permute-start.16 = (f32[8,128]{1,0:T(8,128)S(1)}, f32[8,128]{1,0:T(8,128)S(1)}, u32[]{:S(2)}, u32[]{:S(2)}) collective-permute-start(f32[8,128]{1,0:T(8,128)S(1)} %maximum_select_fusion.5), channel_id=1, source_target_pairs={{0,4},{1,5},{2,6},{3,7},{4,0},{5,1},{6,2},{7,3},{8,12},{9,13},{10,... | collective-permute-start | bytes 12296 | tf_op jit(solution)/shard_map/ppermute | solution.py:353
  234.2 3.7 %collective-permute-start.21 = (f32[16,128]{1,0:T(8,128)S(1)}, f32[16,128]{1,0:T(8,128)S(1)}, u32[]{:S(2)}, u32[]{:S(2)}) collective-permute-start(f32[16,128]{1,0:T(8,128)S(1)} %concatenate.23), channel_id=1, source_target_pairs={{0,8},{8,0},{16,24},{24,16},{1,9},{9,1},{17,25},{25,17},{2,10},{10... | collective-permute-start | bytes 24584 | tf_op jit(solution)/shard_map/ppermute | solution.py:353
  238.5 4.6 %collective-permute-start.22 = (f32[16,128]{1,0:T(8,128)S(1)}, f32[16,128]{1,0:T(8,128)S(1)}, u32[]{:S(2)}, u32[]{:S(2)}) collective-permute-start(f32[16,128]{1,0:T(8,128)S(1)} %pad_add_fusion), channel_id=1, source_target_pairs={{0,16},{8,24},{16,0},{24,8},{1,17},{9,25},{17,1},{25,9},{2,18},{10... | collective-permute-start | bytes 24584 | tf_op jit(solution)/shard_map/ppermute | solution.py:353
  243.2 1.2 collective-permute-start.23
  244.3 3.7 %collective-permute-start.24 = (f32[16,128]{1,0:T(8,128)S(1)}, f32[16,128]{1,0:T(8,128)S(1)}, u32[]{:S(2)}, u32[]{:S(2)}) collective-permute-start(f32[16,128]{1,0:T(8,128)S(1)} %add.218), channel_id=1, source_target_pairs={{0,2},{1,3},{2,0},{3,1},{4,6},{5,7},{6,4},{7,5},{8,10},{9,11},{10,... | collective-permute-start | bytes 24584 | tf_op jit(solution)/shard_map/ppermute | solution.py:353
  248.0 3.7 %collective-permute-start.25 = (f32[16,128]{1,0:T(8,128)S(1)}, f32[16,128]{1,0:T(8,128)S(1)}, u32[]{:S(2)}, u32[]{:S(2)}) collective-permute-start(f32[16,128]{1,0:T(8,128)S(1)} %add.219), channel_id=1, source_target_pairs={{0,4},{1,5},{2,6},{3,7},{4,0},{5,1},{6,2},{7,3},{8,12},{9,13},{10,... | collective-permute-start | bytes 24584 | tf_op jit(solution)/shard_map/ppermute | solution.py:353
Sparse Core Ops, SparseCore 0:
  23.0 79.4 reduce-scatter.1
  104.5 85.6 all-gather.1

commit v4 on v3

--- a/solution.py
+++ b/solution.py
@@ -33,6 +33,10 @@
 
 def in_hbm(value):
     return pltpu.with_memory_space_constraint(value, pltpu.HBM)
+
+
+def hbm_shape(shape):
+    return pltpu.HBM(shape, F32)
 
 
 def halves(value):
@@ -152,10 +156,7 @@
     cols = x.shape[1]
     return pl.pallas_call(
         lefts_kernel,
-        out_shape=[
-            jax.ShapeDtypeStruct((p, cols), F32),
-            jax.ShapeDtypeStruct((1, rows), F32),
-        ],
+        out_shape=[hbm_shape((p, cols)), jax.ShapeDtypeStruct((1, rows), F32)],
         grid=(cols // unit,),
         in_specs=[
             pl.BlockSpec((p, rows), lambda i: (0, 0)),
@@ -214,18 +215,20 @@
 
 
 def core_spread_kernel(bit_ref, *refs):
-    parts, r_ref, out_ref, high_ref, low_ref = refs[:4], *refs[4:]
+    parts, r_ref, out_ref, square_ref, high_ref, low_ref = refs[:4], *refs[4:]
     half, share, p = parts[0].shape
 
     @pl.when(pl.program_id(0) == 0)
     def _():
         upper = bit_ref[0] == 1
+        square_ref[...] = jnp.zeros_like(square_ref)
         for s in range(2):
             mine, got = parts[2 * s][...], parts[2 * s + 1][...]
             pairs = jnp.stack(
                 [jnp.where(upper, got, mine), jnp.where(upper, mine, got)], axis=1
             )
             span = slice(s * 2 * half * share, (s + 1) * 2 * half * share)
+            square_ref[...] += jnp.sum(pairs * pairs)
             high, low = halves(pairs.reshape(2 * half * share, p))
             high_ref[span, :] = high
             low_ref[span, :] = low
@@ -241,27 +244,33 @@
     share = tail - each
     return pl.pallas_call(
         core_spread_kernel,
-        out_shape=jax.ShapeDtypeStruct((p, cols), F32),
+        out_shape=[
+            hbm_shape((p, cols)),
+            jax.ShapeDtypeStruct((1, 128), F32),
+        ],
         grid=(cols // width,),
         in_specs=[pl.BlockSpec(memory_space=pltpu.SMEM)]
         + [pl.BlockSpec((half, share, p), lambda i: (0, each // share, 0))] * 4
         + [pl.BlockSpec((p, width), lambda i: (0, i))],
-        out_specs=pl.BlockSpec((p, width), lambda i: (0, i)),
+        out_specs=[
+            pl.BlockSpec((p, width), lambda i: (0, i)),
+            pl.BlockSpec((1, 128), lambda i: (0, 0)),
+        ],
         scratch_shapes=[pltpu.VMEM((p, p), BF16)] * 2,
         compiler_params=params(1),
         cost_estimate=cost(2 * p * p * cols),
         name="core_spread",
-    )(bit, *parts, in_hbm(r))
+    )(bit, *[in_hbm(v) for v in parts], in_hbm(r))
 
 
 def top_scale(largest):
     return F8_TOP / jnp.maximum(largest, 1e-25)
 
 
-def finish_kernel(groups, bit_ref, scale_ref, x_ref, *refs):
+def finish_kernel(groups, bit_ref, packed_ref, square_ref, l_ref, rm_ref, x_ref, *refs):
     s_refs = refs[:4]
     lt_ref, add_ref, r_ref, t_ref = refs[4:8]
-    out_ref, sum_ref, both, twice, low_both, low_twice, factors = refs[8:]
+    out_ref, total_ref, sum_ref, both, twice, low_both, low_twice, factors = refs[8:]
     p, cols = r_ref.shape
     i = pl.program_id(0)
     width = min(512, cols)
@@ -271,12 +280,20 @@
         whole = t_ref[...] + add_ref[...]
         high = whole.astype(BF16)
         rest = whole - high.astype(F32)
-        s_most, r_scale, l_scale = scale_ref[2], scale_ref[3], scale_ref[4]
+        start_norm = jnp.max(packed_ref[0:1, :])
+        extra = jnp.max(packed_ref[3:4, :]) + jnp.max(square_ref[...])
+        alpha = start_norm / (start_norm + extra)
+        s_most = jnp.max(packed_ref[6:7, :])
+        l_scale = top_scale(jnp.max(l_ref[...]))
+        r_scale = top_scale(jnp.max(rm_ref[...]))
         scale = jnp.minimum(
             top_scale(s_most / 256.0) * r_scale, top_scale(jnp.max(jnp.abs(rest))) * l_scale
         )
         factors[0] = scale / r_scale
-        factors[1] = scale_ref[1] / scale
+        factors[1] = alpha / scale
+        factors[2] = alpha
+        factors[3] = extra / (start_norm + extra)
+        factors[4] = l_scale
         twice[:p, :] = r_ref[...]
         twice[p:, :] = high
         low_twice[:p, :] = (r_ref[...].astype(F32) * r_scale).astype(F8)
@@ -293,19 +310,23 @@
     left = lt_ref[...]
     both[:, p:] = left
     low_both[:, :p] = ((summed - high.astype(F32)) * factors[0]).astype(F8)
-    low_both[:, p:] = (left.astype(F32) * scale_ref[4]).astype(F8)
+    low_both[:, p:] = (left.astype(F32) * factors[4]).astype(F8)
     for at in range(0, cols, width):
         span = slice(at, at + width)
         left_over = (
-            scale_ref[0] * x_ref[:, span].astype(F32)
-            - scale_ref[1] * dot(both[...], twice[:, span])
+            factors[3] * x_ref[:, span].astype(F32)
+            - factors[2] * dot(both[...], twice[:, span])
             - factors[1] * dot(low_both[...], low_twice[:, span])
         )
         out_ref[:, span] = left_over
         sum_ref[:, span] += jnp.sum(left_over * left_over, axis=0, keepdims=True)
 
-
-def finish(bit, scales, x, s_parts, lt, add, r, t, groups):
+    @pl.when(i == groups - 1)
+    def _():
+        total_ref[...] = jnp.full(total_ref.shape, jnp.sum(sum_ref[...]))
+
+
+def finish(bit, packed, square, l_most, r_most, x, s_parts, lt, add, r, t, groups):
     rows, cols = x.shape
     p = r.shape[0]
     each = rows // (2 * groups)
@@ -316,12 +337,15 @@
         functools.partial(finish_kernel, groups),
         out_shape=[
             jax.ShapeDtypeStruct((rows, cols), F32),
-            jax.ShapeDtypeStruct((1, cols), F32),
+            jax.ShapeDtypeStruct((8, 128), F32),
         ],
         grid=(groups,),
         in_specs=[
             pl.BlockSpec(memory_space=pltpu.SMEM),
-            pl.BlockSpec(memory_space=pltpu.SMEM),
+            pl.BlockSpec((8, 128), lambda i: (0, 0)),
+            pl.BlockSpec((1, 128), lambda i: (0, 0)),
+            pl.BlockSpec((1, rows), lambda i: (0, 0)),
+            pl.BlockSpec((1, cols), lambda i: (0, 0)),
             pl.BlockSpec((2 * each, cols), lambda i: (i, 0)),
             first,
             first,
@@ -334,19 +358,20 @@
         ],
         out_specs=[
             pl.BlockSpec((2 * each, cols), lambda i: (i, 0)),
-            pl.BlockSpec((1, cols), lambda i: (0, 0)),
+            pl.BlockSpec((8, 128), lambda i: (0, 0)),
         ],
         scratch_shapes=[
+            pltpu.VMEM((1, cols), F32),
             pltpu.VMEM((2 * each, 2 * p), BF16),
             pltpu.VMEM((2 * p, cols), BF16),
             pltpu.VMEM((2 * each, 2 * p), F8),
             pltpu.VMEM((2 * p, cols), F8),
-            pltpu.SMEM((2,), F32),
+            pltpu.SMEM((5,), F32),
         ],
         compiler_params=params(1),
         cost_estimate=cost(4 * p * rows * cols),
         name="finish_residual",
-    )(bit, scales, in_hbm(x), *s_parts, in_hbm(lt), in_hbm(add), in_hbm(r), in_hbm(t))
+    )(bit, packed, square, l_most, r_most, in_hbm(x), *[in_hbm(v) for v in s_parts], in_hbm(lt), in_hbm(add), in_hbm(r), in_hbm(t))
 
 
 def swap(value, axis, mask, size):
@@ -464,21 +489,42 @@
     for s in range(streams):
         flight[s] = swap(run(lambda v: v[:each], parts[s]), "col", orders[s][top], n_col)
 
+    total = run(
+        lambda v: sum(jnp.sum(part[:each] * part[:each]) for part in (v, parts[1])), parts[0]
+    )
+    total = total + run(lambda v: jnp.sum(v * v), own_left)
+    s_most = run(
+        lambda v: jnp.maximum(*[jnp.max(jnp.abs(part[:each])) for part in (v, parts[1])]),
+        parts[0],
+    )
+    lane = lax.broadcasted_iota(jnp.int32, (8, 128), 0)
+    sums = jnp.where(lane < 3, squares, jnp.where(lane < 6, total, s_most))
+    sum_hops = [("row", m, n_row) for m in powers(n_row)] + [("col", m, n_col) for m in masks]
+    sum_flight = None
+
+    def sum_start():
+        nonlocal sum_flight
+        if sum_hops:
+            axis, mask, size = sum_hops[0]
+            sum_flight = swap(sums, axis, mask, size)
+
+    def sum_step():
+        nonlocal sums
+        if sum_hops:
+            sum_hops.pop(0)
+            got = sum_flight
+            sums = run(lambda v: jnp.where(lane < 6, v + got, jnp.maximum(v, got)), sums)
+            sum_start()
+
     core = jnp.concatenate([part[each:] for part in parts])
-    total = 0.0
-    s_most = jnp.maximum(*[jnp.max(jnp.abs(part[:each])) for part in parts])
-    local = [
-        lambda v: sum(jnp.sum(part[:each] * part[:each]) for part in (v, parts[1])),
-        lambda v: jnp.sum(own_left * own_left) + 0.0 * v[0, 0],
-    ]
-    for mask in powers(n_row):
+    for k, mask in enumerate(powers(n_row)):
         got = swap(core, "row", mask, n_row)
-        if local:
-            total = total + run(local.pop(0), parts[0])
-        if not local:
+        if k == 0:
+            sum_start()
+        else:
             mask_piece()
         core = run(lambda v: v + got, core)
-    core_square = jnp.sum(core * core)
+        sum_step()
     core_parts = jnp.split(core, streams)
     core_flight = [
         swap(core_parts[s], "col", orders[s][top], n_col) for s in range(streams)
@@ -506,56 +552,39 @@
         ).reshape(-1, tail, p)
         widen_start(s, level - 1)
 
-    lane = lax.broadcasted_iota(jnp.int32, (8, 128), 0)
-    sums = jnp.where(
-        lane < 3, squares, jnp.where(lane < 6, total + core_square / n_row, s_most)
-    )
-    sum_hops = [("row", m, n_row) for m in powers(n_row)] + [("col", m, n_col) for m in masks]
-    sum_flight = None
-
-    def sum_start():
-        nonlocal sum_flight
-        if sum_hops:
-            axis, mask, size = sum_hops[0]
-            sum_flight = swap(sums, axis, mask, size)
-
-    def sum_step():
-        nonlocal sums
-        if sum_hops:
-            sum_hops.pop(0)
-            got = sum_flight
-            sums = run(lambda v: jnp.where(lane < 6, v + got, jnp.maximum(v, got)), sums)
-            sum_start()
-
-    sum_start()
-    lt = run(lambda v: v.T, theta_left)
-    l_scale = top_scale(jnp.max(l_most))
-    r_scale = top_scale(jnp.max(r_most))
     for level in range(top, 0, -1):
+        if level == top:
+            sum_step()
         for s in range(streams):
             widen(s, level)
-        sum_step()
         if level == top:
             while mask_starts:
                 mask_piece()
-            sum_step()
-            sum_step()
-            sum_step()
-    while sum_hops:
-        sum_step()
+            lt = run(lambda v: v.T, theta_left)
+            while sum_hops:
+                sum_step()
     packed = sums
 
     s_parts = [v.reshape(-1, tail, p) for s in range(streams) for v in (parts[s], flight[s])]
-    core_add = run(lambda v: core_spread(core_bit, [v] + s_parts[1:], theta_right, each), s_parts[0])
+    core_add, core_square = run(
+        lambda v: core_spread(core_bit, [v] + s_parts[1:], theta_right, each), s_parts[0]
+    )
 
     start_norm = packed[0, 0]
-    extra = packed[3, 0]
-    curvature = start_norm + extra
-    alpha = start_norm / curvature
+    alpha = start_norm / (start_norm + packed[3, 0] + core_square[0, 0])
+    low_row, high_row = query_rows[:, 0], query_rows[:, 1]
+    low_col, high_col = query_cols[:, 0], query_cols[:, 1]
+    area = (high_row - low_row).astype(F32) * (high_col - low_col).astype(F32)
+    lines = queries // 128
+    scale = run(lambda v: (alpha / jnp.sqrt(v)).reshape(lines, 128), area)
+    back = run(lambda v: jnp.broadcast_to(1.0 / v, (8, 128)), start_norm)
 
     residual, square = finish(
         core_bit,
-        jnp.stack([extra / curvature, alpha, packed[6, 0], r_scale, l_scale]),
+        after(packed, scale, back),
+        core_square,
+        l_most,
+        r_most,
         x,
         s_parts,
         lt,
@@ -564,17 +593,9 @@
         whole_left,
         n_col,
     )
-    lines = queries // 128
-    last = jnp.concatenate(
-        [sum(intervals).reshape(lines, 128), jnp.full((8, 128), jnp.sum(square))]
-    )
-    last = fold(fold(last, "row", n_row), "col", n_col)
-    step_ratio = (last[lines, 0] / start_norm).reshape(1)
-    low_row, high_row = query_rows[:, 0], query_rows[:, 1]
-    low_col, high_col = query_cols[:, 0], query_cols[:, 1]
-    area = (high_row - low_row).astype(F32) * (high_col - low_col).astype(F32)
-    answers = alpha * last[:lines].reshape(queries) / jnp.sqrt(area)
-    return (residual, step_ratio, answers)
+    last = jnp.concatenate([sum(intervals).reshape(lines, 128), square])
+    last = fold(fold(last, "row", n_row), "col", n_col) * jnp.concatenate([scale, back])
+    return (residual, last[lines, :1], last[:lines].reshape(queries))
 
 
 def solution(mesh):

time: 263 us -> 258 us (0.981)
  local copies, waits for them, and re-layouts: 21.6 us -> 15.3 us
  between operations: 26.7 us -> 21.3 us
  waiting for transfers between devices: 41.9 us -> 47 us
  other arithmetic: 29.1 us -> 25.3 us
  starting transfers between devices: 27.2 us -> 30.8 us
    select_n x4, other arithmetic: 2.18 us -> 7.59 us  [widen(): jnp.where(bits[mask] == 1, jnp.stack([other, v], axis=axis), jnp.stack([v...]
    ppermute x26, waiting for transfers between devices: 40.5 us -> 45.9 us  [swap(): return lax.ppermute(value, axis, [(i, i ^ mask) for i in range(size)])]
    ppermute x26, starting transfers between devices: 27.1 us -> 30.7 us  [swap(): return lax.ppermute(value, axis, [(i, i ^ mask) for i in range(size)])]
    squeeze x4, local copies, waits for them, and re-layouts: 3.71 us -> 0.26 us  [pick(): return lax.dynamic_index_in_dim(value, at, axis, False)]
    unnamed x31 -> x25, local copies, waits for them, and re-layouts: 6.15 us -> 3.38 us
  transfers between devices with their start and end apart: 28 -> 28, of which waited for: 13 -> 17; matrix products, arithmetic and copies ran while one was open for 16% -> 14% of each run, Pallas kernels for 23% -> 23%
where the time goes in v4:
time: 258 us; the launch traced here: 257 us
  Pallas kernels  117 us (45%)
  waiting for transfers between devices  47 us (18%)
  starting transfers between devices  30.8 us (12%)
  other arithmetic  25.3 us (10%)
  between operations  21.3 us (8%)
  local copies, waits for them, and re-layouts  15.3 us (6%)
    ppermute x26, waiting for transfers between devices, swap(): return lax.ppermute(value, axis, [(i, i ^ mask) for i in range(size)])  45.9 us
    pallas_call x1, Pallas kernels, finish(): pl.pallas_call(functools.partial(finish_kernel, groups), out_shape=[jax.S...  43 us
    pallas_call x4, Pallas kernels, mask_sums(): pl.pallas_call(functools.partial(mask_kernel, steps, start), out_shape=ja...  31.2 us
    ppermute x26, starting transfers between devices, swap(): return lax.ppermute(value, axis, [(i, i ^ mask) for i in range(size)])  30.7 us
    pallas_call x2, Pallas kernels, rights(): pl.pallas_call(rights_kernel, out_shape=[half, half, jax.ShapeDtypeStruct...  17.8 us
    pallas_call x1, Pallas kernels, lefts(): pl.pallas_call(lefts_kernel, out_shape=[hbm_shape((p, cols)), jax.ShapeDt...  14.5 us
    add x4, other arithmetic, scatter_start(): sum((pick(term, axis, 1 - bits[mask]) for term in rest), pick(v, axis, 1...  8.16 us
    select_n x4, other arithmetic, widen(): jnp.where(bits[mask] == 1, jnp.stack([other, v], axis=axis), jnp.stack([v...  7.59 us
  transfers between devices with their start and end apart: 28, of which 17 were waited for; matrix products, arithmetic and copies ran while one was open for 14% of the time, Pallas kernels for 23%

profile of v4, /device:TPU:0, one launch (start us, length us, event | category | flops | bytes accessed | tf_op | source)
XLA Modules:
  0.0 256.9 jit_solution(16848365573848249912)
XLA Ops:
  7.2 14.5 %left_products.1 = (f32[512,2048]{1,0:T(8,128)}, f32[1,4096]{1,0:T(1,128)S(1)}) custom-call(bf16[512,4096]{1,0:T(8,128)(2,1)} %l_ref, bf16[4096,2048]{1,0:T(8,128)(2,1)} %x_ref.15), custom_call_target="tpu_custom_call" | custom-call | flops 2576980480 | bytes 1024 | tf_op jit(solution)/shard_map/left_products/pallas_call | solution.py:157
  21.8 4.7 %core_products.1 = (f32[512,512]{1,0:T(8,128)S(1)}, f32[1,2048]{1,0:T(1,128)S(1)}) custom-call(f32[512,2048]{1,0:T(8,128)} %get-tuple-element.53.t_ref, bf16[512,2048]{1,0:T(8,128)(2,1)} %refs_6_.1), custom_call_target="tpu_custom_call" | custom-call | flops 644245120 | bytes 1024 | tf_op jit(solution)/shard_map/core_products/pallas_call | solution.py:121
  26.5 8.9 %right_products.2 = (f32[4,288,512]{2,1,0:T(8,128)}, f32[4,288,512]{2,1,0:T(8,128)S(1)}, f32[1,2048]{1,0:T(1,128)S(1)}) custom-call(s32[1]{0:T(128)} %bitcast.bit_ref, bf16[4096,2048]{1,0:T(8,128)(2,1)} %x_ref.15, bf16[512,2048]{1,0:T(8,128)(2,1)} %refs_6_.1, f32[16,32,512]{2,1,0:T(8,128)S(1)} %bitcast.74), custom_call_target="tpu_custom_call" | custom-call | flops 1288490240 | bytes 1024 | tf_op jit(solution)/shard_map/right_products/pallas_call | solution.py:85
  35.8 8.9 %right_products.3 = (f32[4,288,512]{2,1,0:T(8,128)}, f32[4,288,512]{2,1,0:T(8,128)S(1)}, f32[1,2048]{1,0:T(1,128)S(1)}) custom-call(s32[1]{0:T(128)} %bitcast.bit_ref, bf16[4096,2048]{1,0:T(8,128)(2,1)} %x_ref.15, bf16[512,2048]{1,0:T(8,128)(2,1)} %refs_6_.1, f32[16,32,512]{2,1,0:T(8,128)S(1)} %bitcast.75), custom_call_target="tpu_custom_call" | custom-call | flops 1288490240 | bytes 1024 | tf_op jit(solution)/shard_map/right_products/pallas_call | solution.py:85
  44.7 1.4 copy-done
  46.2 2.7 %add_bitcast_fusion.1 = f32[2,288,512]{2,1,0:T(8,128)} fusion(f32[2,2,288,512]{3,2,1,0:T(8,128)} %bitcast.7, s32[]{:T(128)S(6)} %select_n.132, f32[2,2,288,512]{3,2,1,0:T(8,128)S(1)} %bitcast.76), kind=kLoop, calls=%fused_computation.5 | loop fusion | flops 294912 | bytes 3538948 | tf_op jit(solution)/shard_map/add | solution.py:449
  49.0 3.0 %collective-permute-start.2 = (f32[2,288,512]{2,1,0:T(8,128)}, f32[2,288,512]{2,1,0:T(8,128)}, u32[]{:S(2)}, u32[]{:S(2)}) collective-permute-start(f32[2,288,512]{2,1,0:T(8,128)} %add_bitcast_fusion.1), channel_id=1, source_target_pairs={{0,2},{1,3},{2,0},{3,1},{4,6},{5,7},{6,4},{7,5},{8,10},{9,11},{10,... | collective-permute-start | bytes 3538952 | tf_op jit(solution)/shard_map/ppermute | solution.py:378
  52.0 2.5 add_bitcast_fusion
  54.5 1.8 collective-permute-start.3
  56.6 1.0 copy.19
  57.6 0.6 reduce_sum.45
  58.2 0.6 reduce_sum.46
  60.4 0.9 copy-done.9
  61.3 7.8 %interval_sums.4 = f32[1024,1]{1,0:T(8,128)S(1)} custom-call(s32[1024,2]{1,0:T(8,128)S(1)} %broadcast_clamp_fusion.rows_ref, s32[1024,2]{1,0:T(8,128)S(1)} %broadcast_subtract_fusion.cols_ref, bf16[4096,2048]{1,0:T(8,128)(2,1)} %x_ref.15), custom_call_target="tpu_custom_call" | custom-call | flops 1288490240 | bytes 1024 | tf_op jit(solution)/shard_map/interval_sums/pallas_call | solution.py:200
  69.1 7.9 %interval_sums.5 = f32[1024,1]{1,0:T(8,128)S(1)} custom-call(s32[1024,2]{1,0:T(8,128)S(1)} %broadcast_clamp_fusion.rows_ref, s32[1024,2]{1,0:T(8,128)S(1)} %broadcast_subtract_fusion.cols_ref, bf16[4096,2048]{1,0:T(8,128)(2,1)} %x_ref.15), custom_call_target="tpu_custom_call" | custom-call | flops 1288490240 | bytes 1024 | tf_op jit(solution)/shard_map/interval_sums/pallas_call | solution.py:200
  77.1 1.4 collective-permute-done.2
  78.4 1.4 bitcast_add_fusion.6
  79.9 1.8 collective-permute-start.4
  81.8 1.8 collective-permute-done.3
  83.6 1.5 bitcast_add_fusion.4
  85.1 1.9 collective-permute-start.5
  87.1 8.6 %collective-permute-done.4 = f32[288,512]{1,0:T(8,128)S(1)} collective-permute-done((f32[288,512]{1,0:T(8,128)S(1)}, f32[288,512]{1,0:T(8,128)S(1)}, u32[]{:S(2)}, u32[]{:S(2)}) %collective-permute-start.4) | collective-permute-done | bytes 589856 | tf_op jit(solution)/shard_map/ppermute | solution.py:378
  95.7 1.5 fusion.1
  97.2 2.3 collective-permute-done.5
  99.5 1.5 fusion
  101.1 1.8 collective-permute-start.6
  102.9 0.7 abs_reduce_fusion
  103.6 0.8 slice.55
  104.5 0.8 slice.56
  105.3 0.7 multiply_reduce_fusion.2
  107.3 2.1 multiply_reduce_fusion
  110.0 0.6 abs_reduce_fusion.1
  112.3 2.9 %collective-permute-start.8 = (f32[64,512]{1,0:T(8,128)S(1)}, f32[64,512]{1,0:T(8,128)S(1)}, u32[]{:S(2)}, u32[]{:S(2)}) collective-permute-start(f32[64,512]{1,0:T(8,128)S(1)} %add.200), channel_id=1, source_target_pairs={{0,16},{8,24},{16,0},{24,8},{1,17},{9,25},{17,1},{25,9},{2,18},{10... | collective-permute-start | bytes 393224 | tf_op jit(solution)/shard_map/ppermute | solution.py:378
  115.2 1.5 collective-permute-start.11
  116.7 1.6 collective-permute-start.13
  118.6 7.7 %interval_sums.6 = f32[1024,1]{1,0:T(8,128)S(1)} custom-call(s32[1024,2]{1,0:T(8,128)S(1)} %broadcast_clamp_fusion.rows_ref, s32[1024,2]{1,0:T(8,128)S(1)} %broadcast_subtract_fusion.cols_ref, bf16[4096,2048]{1,0:T(8,128)(2,1)} %x_ref.15), custom_call_target="tpu_custom_call" | custom-call | flops 1288490240 | bytes 1024 | tf_op jit(solution)/shard_map/interval_sums/pallas_call | solution.py:200
  126.3 2.4 collective-permute-done.8
  129.0 1.5 collective-permute-start.14
  130.4 1.5 collective-permute-start.12
  132.1 1.4 collective-permute-done.14
  133.5 1.1 maximum_select_fusion.2
  134.9 1.5 collective-permute-start.19
  136.4 1.5 collective-permute-start.17
  137.8 0.6 collective-permute-start.15
  138.4 7.7 %interval_sums.7 = f32[1024,1]{1,0:T(8,128)S(1)} custom-call(s32[1024,2]{1,0:T(8,128)S(1)} %broadcast_clamp_fusion.rows_ref, s32[1024,2]{1,0:T(8,128)S(1)} %broadcast_subtract_fusion.cols_ref, bf16[4096,2048]{1,0:T(8,128)(2,1)} %x_ref.15), custom_call_target="tpu_custom_call" | custom-call | flops 1288490240 | bytes 1024 | tf_op jit(solution)/shard_map/interval_sums/pallas_call | solution.py:200
  146.1 6.5 %copy.20 = bf16[512,4096]{0,1:T(8,128)(2,1)} copy(bf16[512,4096]{1,0:T(8,128)(2,1)} %l_ref) | data formatting | bytes 8388608 | tf_op jit(solution)/shard_map/optimization_barrier | solution.py:31
  152.6 11.5 %collective-permute-done.15 = f32[8,128]{1,0:T(8,128)S(1)} collective-permute-done((f32[8,128]{1,0:T(8,128)S(1)}, f32[8,128]{1,0:T(8,128)S(1)}, u32[]{:S(2)}, u32[]{:S(2)}) %collective-permute-start.15) | collective-permute-done | bytes 4128 | tf_op jit(solution)/shard_map/ppermute | solution.py:378
  164.8 3.1 %collective-permute-done.16 = f32[8,128]{1,0:T(8,128)S(1)} collective-permute-done((f32[8,128]{1,0:T(8,128)S(1)}, f32[8,128]{1,0:T(8,128)S(1)}, u32[]{:S(2)}, u32[]{:S(2)}) %collective-permute-start.16) | collective-permute-done | bytes 4128 | tf_op jit(solution)/shard_map/ppermute | solution.py:378
  167.9 3.3 %maximum_select_fusion.1 = f32[2,2,288,512]{3,2,1,0:T(8,128)} fusion(f32[1,2,288,512]{3,2,1,0:T(8,128)S(1)} %bitcast.84, f32[1,2,288,512]{3,2,1,0:T(8,128)} %bitcast.32, pred[]{:T(512)S(6)} %eq.13), kind=kLoop, calls=%fused_computation.1 | loop fusion | flops 1769472 | bytes 4718593 | tf_op jit(solution)/shard_map/jit(_where)/select_n | solution.py:546
  171.2 3.0 %maximum_select_fusion = f32[2,2,288,512]{3,2,0,1:T(8,128)S(1)} fusion(f32[2,1,288,512]{3,2,0,1:T(8,128)} %bitcast.30, f32[2,1,288,512]{3,2,0,1:T(8,128)} %bitcast.29, pred[]{:T(512)S(6)} %eq.12), kind=kLoop, calls=%fused_computation | loop fusion | flops 1769472 | bytes 4718593 | tf_op jit(solution)/shard_map/jit(_where)/select_n | solution.py:546
  174.3 1.6 copy.21
  178.5 2.4 collective-permute-done.18.refs_1_
  180.9 5.9 %core_spread.1 = (f32[512,2048]{1,0:T(8,128)}, f32[1,128]{1,0:T(1,128)S(1)}) custom-call(s32[1]{0:T(128)} %bitcast.bit_ref, f32[4,288,512]{2,1,0:T(8,128)} %bitcast.31.refs_0_, f32[4,288,512]{2,1,0:T(8,128)} %collective-permute-done.18.refs_1_, f32[4,288,512]{2,1,0:T(8,128)} %bitcast.34.refs_2_, f32[4,288,512]{2,1,0:T(8,128)} %copy-done.8, ...), custom_call_target="tpu_custom_call" | custom-call | flops 644245120 | bytes 1024 | tf_op jit(solution)/shard_map/core_spread/pallas_call | solution.py:245
  187.5 1.0 all-gather.2.cloned.1.call-done.refs_7_
  188.5 43.0 %finish_residual.1 = (f32[4096,2048]{1,0:T(8,128)}, f32[8,128]{1,0:T(8,128)S(1)}) custom-call(s32[1]{0:T(128)} %bitcast.bit_ref, f32[8,128]{1,0:T(8,128)S(1)} %maximum_select_fusion.4.packed_ref, f32[1,128]{1,0:T(1,128)S(1)} %get-tuple-element.90.square_ref, f32[1,4096]{1,0:T(1,128)S(1)} %get-tuple-element.94.l_ref, f32[1,2048]{1,0:T(1,128)S(1)} %get-tuple-element.95.rm_ref, ...), custom_call_target="tpu_custom_call" | custom-call | flops 10307921920 | bytes 1024 | tf_op jit(solution)/shard_map/finish_residual/pallas_call | solution.py:336
  231.6 3.6 %collective-permute-done.21 = f32[16,128]{1,0:T(8,128)S(1)} collective-permute-done((f32[16,128]{1,0:T(8,128)S(1)}, f32[16,128]{1,0:T(8,128)S(1)}, u32[]{:S(2)}, u32[]{:S(2)}) %collective-permute-start.21) | collective-permute-done | bytes 8224 | tf_op jit(solution)/shard_map/ppermute | solution.py:378
  235.2 3.5 %collective-permute-start.22 = (f32[16,128]{1,0:T(8,128)S(1)}, f32[16,128]{1,0:T(8,128)S(1)}, u32[]{:S(2)}, u32[]{:S(2)}) collective-permute-start(f32[16,128]{1,0:T(8,128)S(1)} %fusion.2), channel_id=1, source_target_pairs={{0,16},{8,24},{16,0},{24,8},{1,17},{9,25},{17,1},{25,9},{2,18},{10... | collective-permute-start | bytes 24584 | tf_op jit(solution)/shard_map/ppermute | solution.py:378
  238.7 1.7 collective-permute-done.22
  240.4 1.2 collective-permute-done.23
  241.6 1.5 collective-permute-start.24
  243.1 2.2 collective-permute-done.24
  245.3 0.8 collective-permute-start.25
  246.7 2.2 collective-permute-done.25
  249.4 0.6 slice_bitcast_fusion
  (90 shorter events, 5.2 us)
Async XLA Ops:
  7.2 96.5 %reduce-scatter.2.cloned.1.call-start = ((), (), s32[]{:S(2)}) async-start(), calls=%async_computation.1 | async-start | bytes 5242880 | tf_op jit(solution)/shard_map/reduce_scatter | solution.py:426
  21.8 166.7 %all-gather.2.cloned.1.call-start = ((), (), s32[]{:S(2)}) async-start(), calls=%async_computation.2 | async-start | bytes 5242880 | tf_op jit(solution)/shard_map/all_gather | solution.py:487
  35.4 10.9 %collective-permute-start = (f32[4,288,512]{2,1,0:T(8,128)}, f32[4,288,512]{2,1,0:T(8,128)}, u32[]{:S(2)}, u32[]{:S(2)}) collective-permute-start(f32[4,288,512]{2,1,0:T(8,128)} %get-tuple-element.57), channel_id=1, source_target_pairs={{0,1},{1,0},{2,3},{3,2},{4,5},{5,4},{6,7},{7,6},{8,9},{9,8},{10,11... | collective-permute-start | bytes 7077896 | tf_op jit(solution)/shard_map/ppermute | solution.py:378
  44.7 1.4 copy-start
  46.2 5.8 %collective-permute-start.1 = (f32[4,288,512]{2,1,0:T(8,128)}, f32[4,288,512]{2,1,0:T(8,128)}, u32[]{:S(2)}, u32[]{:S(2)}) collective-permute-start(f32[4,288,512]{2,1,0:T(8,128)} %get-tuple-element.62), channel_id=1, source_target_pairs={{0,1},{1,0},{2,3},{3,2},{4,5},{5,4},{6,7},{7,6},{8,9},{9,8},{10,11... | collective-permute-start | bytes 7077896 | tf_op jit(solution)/shard_map/ppermute | solution.py:378
  46.2 5.7 %copy-start.1 = (f32[4,288,512]{2,1,0:T(8,128)S(1)}, f32[4,288,512]{2,1,0:T(8,128)}, u32[]{:S(2)}) copy-start(f32[4,288,512]{2,1,0:T(8,128)} %copy-done) | copy-start | bytes 7077892
  49.0 7.4 %copy-start.11 = (s32[1024,2]{0,1:T(2,128)S(1)}, s32[1024,2]{0,1:T(2,128)}, u32[]{:S(2)}) copy-start(s32[1024,2]{0,1:T(2,128)} %param.8) | copy-start | bytes 24580
  49.0 7.6 %copy-start.10 = (s32[1024,2]{0,1:T(2,128)S(1)}, s32[1024,2]{0,1:T(2,128)}, u32[]{:S(2)}) copy-start(s32[1024,2]{0,1:T(2,128)} %param.9) | copy-start | bytes 24580
  49.0 29.5 %collective-permute-start.2 = (f32[2,288,512]{2,1,0:T(8,128)}, f32[2,288,512]{2,1,0:T(8,128)}, u32[]{:S(2)}, u32[]{:S(2)}) collective-permute-start(f32[2,288,512]{2,1,0:T(8,128)} %add_bitcast_fusion.1), channel_id=1, source_target_pairs={{0,2},{1,3},{2,0},{3,1},{4,6},{5,7},{6,4},{7,5},{8,10},{9,11},{10,... | collective-permute-start | bytes 3538952 | tf_op jit(solution)/shard_map/ppermute | solution.py:378
  54.5 29.1 %collective-permute-start.3 = (f32[2,288,512]{2,1,0:T(8,128)}, f32[2,288,512]{2,1,0:T(8,128)}, u32[]{:S(2)}, u32[]{:S(2)}) collective-permute-start(f32[2,288,512]{2,1,0:T(8,128)} %add_bitcast_fusion), channel_id=1, source_target_pairs={{0,4},{1,5},{2,6},{3,7},{4,0},{5,1},{6,2},{7,3},{8,12},{9,13},{10,... | collective-permute-start | bytes 3538952 | tf_op jit(solution)/shard_map/ppermute | solution.py:378
  60.2 1.0 copy-start.9
  69.1 7.9 %copy-start.3 = (f32[1024,1]{1,0:T(8,128)}, f32[1024,1]{1,0:T(8,128)S(1)}, u32[]{:S(2)}) copy-start(f32[1024,1]{1,0:T(8,128)S(1)} %interval_sums.4) | copy-start | bytes 12292
  77.0 4.8 %copy-start.5 = (f32[1024,1]{1,0:T(8,128)}, f32[1024,1]{1,0:T(8,128)S(1)}, u32[]{:S(2)}) copy-start(f32[1024,1]{1,0:T(8,128)S(1)} %interval_sums.5) | copy-start | bytes 12292
  77.0 4.7 %copy-start.2 = (f32[4,288,512]{2,1,0:T(8,128)S(1)}, f32[4,288,512]{2,1,0:T(8,128)}, u32[]{:S(2)}) copy-start(f32[4,288,512]{2,1,0:T(8,128)} %copy-done) | copy-start | bytes 7077892
  79.9 15.8 %collective-permute-start.4 = (f32[288,512]{1,0:T(8,128)S(1)}, f32[288,512]{1,0:T(8,128)S(1)}, u32[]{:S(2)}, u32[]{:S(2)}) collective-permute-start(f32[288,512]{1,0:T(8,128)S(1)} %bitcast_add_fusion.6), channel_id=1, source_target_pairs={{0,4},{1,5},{2,6},{3,7},{4,0},{5,1},{6,2},{7,3},{8,12},{9,13},{10,... | collective-permute-start | bytes 1769480 | tf_op jit(solution)/shard_map/ppermute | solution.py:378
  85.1 14.4 %collective-permute-start.5 = (f32[288,512]{1,0:T(8,128)S(1)}, f32[288,512]{1,0:T(8,128)S(1)}, u32[]{:S(2)}, u32[]{:S(2)}) collective-permute-start(f32[288,512]{1,0:T(8,128)S(1)} %bitcast_add_fusion.4), channel_id=1, source_target_pairs={{0,2},{1,3},{2,0},{3,1},{4,6},{5,7},{6,4},{7,5},{8,10},{9,11},{10,... | collective-permute-start | bytes 1769480 | tf_op jit(solution)/shard_map/ppermute | solution.py:378
  97.2 15.1 %copy-start.7 = (f32[288,512]{1,0:T(8,128)}, f32[288,512]{1,0:T(8,128)S(1)}, u32[]{:S(2)}) copy-start(f32[288,512]{1,0:T(8,128)S(1)} %fusion.1) | copy-start | bytes 1769476
  101.1 11.2 %collective-permute-start.6 = (f32[64,512]{1,0:T(8,128)S(1)}, f32[64,512]{1,0:T(8,128)S(1)}, u32[]{:S(2)}, u32[]{:S(2)}) collective-permute-start(f32[64,512]{1,0:T(8,128)S(1)} %pad_maximum_fusion.2), channel_id=1, source_target_pairs={{0,8},{8,0},{16,24},{24,16},{1,9},{9,1},{17,25},{25,17},{2,10},{10... | collective-permute-start | bytes 393224 | tf_op jit(solution)/shard_map/ppermute | solution.py:378
  112.0 6.3 %collective-permute-start.7 = (f32[8,128]{1,0:T(8,128)S(1)}, f32[8,128]{1,0:T(8,128)S(1)}, u32[]{:S(2)}, u32[]{:S(2)}) collective-permute-start(f32[8,128]{1,0:T(8,128)S(1)} %broadcast_select_fusion), channel_id=1, source_target_pairs={{0,8},{8,0},{16,24},{24,16},{1,9},{9,1},{17,25},{25,17},{2,10},{10... | collective-permute-start | bytes 12296 | tf_op jit(solution)/shard_map/ppermute | solution.py:378
  112.3 16.4 %collective-permute-start.8 = (f32[64,512]{1,0:T(8,128)S(1)}, f32[64,512]{1,0:T(8,128)S(1)}, u32[]{:S(2)}, u32[]{:S(2)}) collective-permute-start(f32[64,512]{1,0:T(8,128)S(1)} %add.200), channel_id=1, source_target_pairs={{0,16},{8,24},{16,0},{24,8},{1,17},{9,25},{17,1},{25,9},{2,18},{10... | collective-permute-start | bytes 393224 | tf_op jit(solution)/shard_map/ppermute | solution.py:378
  115.2 19.5 %collective-permute-start.11 = (f32[256,512]{1,0:T(8,128)}, f32[256,512]{1,0:T(8,128)S(1)}, u32[]{:S(2)}, u32[]{:S(2)}) collective-permute-start(f32[256,512]{1,0:T(8,128)} %slice.56), channel_id=1, source_target_pairs={{0,2},{1,3},{2,0},{3,1},{4,6},{5,7},{6,4},{7,5},{8,10},{9,11},{10,... | collective-permute-start | bytes 1572872 | tf_op jit(solution)/shard_map/ppermute | solution.py:378
  116.7 16.7 %collective-permute-start.13 = (f32[256,512]{1,0:T(8,128)}, f32[256,512]{1,0:T(8,128)S(1)}, u32[]{:S(2)}, u32[]{:S(2)}) collective-permute-start(f32[256,512]{1,0:T(8,128)} %slice.55), channel_id=1, source_target_pairs={{0,4},{1,5},{2,6},{3,7},{4,0},{5,1},{6,2},{7,3},{8,12},{9,13},{10,... | collective-permute-start | bytes 1572872 | tf_op jit(solution)/shard_map/ppermute | solution.py:378
  118.4 13.6 %slice-start = ((f32[288,512]{1,0:T(8,128)}), f32[256,512]{1,0:T(8,128)S(1)}, s32[]{:S(2)}) async-start(f32[288,512]{1,0:T(8,128)} %copy-done.7), calls=%async_computation.3 | async-start | bytes 1048576 | tf_op jit(solution)/shard_map/slice | solution.py:543
  118.4 10.5 %collective-permute-start.9 = (f32[8,128]{1,0:T(8,128)S(1)}, f32[8,128]{1,0:T(8,128)S(1)}, u32[]{:S(2)}, u32[]{:S(2)}) collective-permute-start(f32[8,128]{1,0:T(8,128)S(1)} %maximum_select_fusion.8), channel_id=1, source_target_pairs={{0,16},{8,24},{16,0},{24,8},{1,17},{9,25},{17,1},{25,9},{2,18},{10... | collective-permute-start | bytes 12296 | tf_op jit(solution)/shard_map/ppermute | solution.py:378
  129.0 3.1 %collective-permute-start.10 = (f32[8,128]{1,0:T(8,128)S(1)}, f32[8,128]{1,0:T(8,128)S(1)}, u32[]{:S(2)}, u32[]{:S(2)}) collective-permute-start(f32[8,128]{1,0:T(8,128)S(1)} %maximum_select_fusion.7), channel_id=1, source_target_pairs={{0,1},{1,0},{2,3},{3,2},{4,5},{5,4},{6,7},{7,6},{8,9},{9,8},{10,11... | collective-permute-start | bytes 12296 | tf_op jit(solution)/shard_map/ppermute | solution.py:378
  129.0 4.5 %collective-permute-start.14 = (f32[32,512]{1,0:T(8,128)S(1)}, f32[32,512]{1,0:T(8,128)S(1)}, u32[]{:S(2)}, u32[]{:S(2)}) collective-permute-start(f32[32,512]{1,0:T(8,128)S(1)} %get-tuple-element.102), channel_id=1, source_target_pairs={{0,4},{1,5},{2,6},{3,7},{4,0},{5,1},{6,2},{7,3},{8,12},{9,13},{10,... | collective-permute-start | bytes 196616 | tf_op jit(solution)/shard_map/ppermute | solution.py:378
  130.4 4.3 %collective-permute-start.12 = (f32[32,512]{1,0:T(8,128)S(1)}, f32[32,512]{1,0:T(8,128)S(1)}, u32[]{:S(2)}, u32[]{:S(2)}) collective-permute-start(f32[32,512]{1,0:T(8,128)S(1)} %get-tuple-element.103), channel_id=1, source_target_pairs={{0,2},{1,3},{2,0},{3,1},{4,6},{5,7},{6,4},{7,5},{8,10},{9,11},{10,... | collective-permute-start | bytes 196616 | tf_op jit(solution)/shard_map/ppermute | solution.py:378
  134.9 33.0 %collective-permute-start.19 = (f32[2,288,512]{2,1,0:T(8,128)S(1)}, f32[2,288,512]{2,1,0:T(8,128)}, u32[]{:S(2)}, u32[]{:S(2)}) collective-permute-start(f32[2,288,512]{2,1,0:T(8,128)S(1)} %maximum_select_fusion.3), channel_id=1, source_target_pairs={{0,4},{1,5},{2,6},{3,7},{4,0},{5,1},{6,2},{7,3},{8,12},{9,13},{10,... | collective-permute-start | bytes 3538952 | tf_op jit(solution)/shard_map/ppermute | solution.py:378
  136.4 34.9 %collective-permute-start.17 = (f32[2,288,512]{2,1,0:T(8,128)}, f32[2,288,512]{2,1,0:T(8,128)}, u32[]{:S(2)}, u32[]{:S(2)}) collective-permute-start(f32[2,288,512]{2,1,0:T(8,128)} %maximum_select_fusion.2), channel_id=1, source_target_pairs={{0,2},{1,3},{2,0},{3,1},{4,6},{5,7},{6,4},{7,5},{8,10},{9,11},{10,... | collective-permute-start | bytes 3538952 | tf_op jit(solution)/shard_map/ppermute | solution.py:378
  137.8 26.3 %collective-permute-start.15 = (f32[8,128]{1,0:T(8,128)S(1)}, f32[8,128]{1,0:T(8,128)S(1)}, u32[]{:S(2)}, u32[]{:S(2)}) collective-permute-start(f32[8,128]{1,0:T(8,128)S(1)} %maximum_select_fusion.6), channel_id=1, source_target_pairs={{0,2},{1,3},{2,0},{3,1},{4,6},{5,7},{6,4},{7,5},{8,10},{9,11},{10,... | collective-permute-start | bytes 12296 | tf_op jit(solution)/shard_map/ppermute | solution.py:378
  164.2 3.6 %collective-permute-start.16 = (f32[8,128]{1,0:T(8,128)S(1)}, f32[8,128]{1,0:T(8,128)S(1)}, u32[]{:S(2)}, u32[]{:S(2)}) collective-permute-start(f32[8,128]{1,0:T(8,128)S(1)} %maximum_select_fusion.5), channel_id=1, source_target_pairs={{0,4},{1,5},{2,6},{3,7},{4,0},{5,1},{6,2},{7,3},{8,12},{9,13},{10,... | collective-permute-start | bytes 12296 | tf_op jit(solution)/shard_map/ppermute | solution.py:378
  171.2 7.3 %collective-permute-start.20 = (f32[4,288,512]{2,1,0:T(8,128)}, f32[4,288,512]{2,1,0:T(8,128)S(1)}, u32[]{:S(2)}, u32[]{:S(2)}) collective-permute-start(f32[4,288,512]{2,1,0:T(8,128)} %bitcast.34.refs_2_), channel_id=1, source_target_pairs={{0,1},{1,0},{2,3},{3,2},{4,5},{5,4},{6,7},{7,6},{8,9},{9,8},{10,11... | collective-permute-start | bytes 7077896 | tf_op jit(solution)/shard_map/ppermute | solution.py:378
  174.3 2.2 copy-start.4
  174.3 2.2 copy-start.6
  175.9 5.0 %collective-permute-start.18 = (f32[4,288,512]{2,1,0:T(8,128)}, f32[4,288,512]{2,1,0:T(8,128)}, u32[]{:S(2)}, u32[]{:S(2)}) collective-permute-start(f32[4,288,512]{2,1,0:T(8,128)} %bitcast.31.refs_0_), channel_id=1, source_target_pairs={{0,1},{1,0},{2,3},{3,2},{4,5},{5,4},{6,7},{7,6},{8,9},{9,8},{10,11... | collective-permute-start | bytes 7077896 | tf_op jit(solution)/shard_map/ppermute | solution.py:378
  178.5 2.4 copy-start.8
  231.5 3.7 %collective-permute-start.21 = (f32[16,128]{1,0:T(8,128)S(1)}, f32[16,128]{1,0:T(8,128)S(1)}, u32[]{:S(2)}, u32[]{:S(2)}) collective-permute-start(f32[16,128]{1,0:T(8,128)S(1)} %pad_maximum_fusion.3), channel_id=1, source_target_pairs={{0,8},{8,0},{16,24},{24,16},{1,9},{9,1},{17,25},{25,17},{2,10},{10... | collective-permute-start | bytes 24584 | tf_op jit(solution)/shard_map/ppermute | solution.py:378
  235.2 5.2 %collective-permute-start.22 = (f32[16,128]{1,0:T(8,128)S(1)}, f32[16,128]{1,0:T(8,128)S(1)}, u32[]{:S(2)}, u32[]{:S(2)}) collective-permute-start(f32[16,128]{1,0:T(8,128)S(1)} %fusion.2), channel_id=1, source_target_pairs={{0,16},{8,24},{16,0},{24,8},{1,17},{9,25},{17,1},{25,9},{2,18},{10... | collective-permute-start | bytes 24584 | tf_op jit(solution)/shard_map/ppermute | solution.py:378
  240.4 1.2 collective-permute-start.23
  241.6 3.7 %collective-permute-start.24 = (f32[16,128]{1,0:T(8,128)S(1)}, f32[16,128]{1,0:T(8,128)S(1)}, u32[]{:S(2)}, u32[]{:S(2)}) collective-permute-start(f32[16,128]{1,0:T(8,128)S(1)} %add.214), channel_id=1, source_target_pairs={{0,2},{1,3},{2,0},{3,1},{4,6},{5,7},{6,4},{7,5},{8,10},{9,11},{10,... | collective-permute-start | bytes 24584 | tf_op jit(solution)/shard_map/ppermute | solution.py:378
  245.3 3.7 %collective-permute-start.25 = (f32[16,128]{1,0:T(8,128)S(1)}, f32[16,128]{1,0:T(8,128)S(1)}, u32[]{:S(2)}, u32[]{:S(2)}) collective-permute-start(f32[16,128]{1,0:T(8,128)S(1)} %add.215), channel_id=1, source_target_pairs={{0,4},{1,5},{2,6},{3,7},{4,0},{5,1},{6,2},{7,3},{8,12},{9,13},{10,... | collective-permute-start | bytes 24584 | tf_op jit(solution)/shard_map/ppermute | solution.py:378
Sparse Core Ops, SparseCore 0:
  21.9 79.4 reduce-scatter.1
  103.8 84.6 all-gather.1
